TPU v7x, 512 devices: a whole 4x4x16 slice. The times are simulated.
512 devices in a mesh: tm: 16 (over z_lo, core), patch: 32 (over x, y, z_hi).
Axes of the slice: x: 4, y: 4, z: 16 (z_hi: 2, z_lo: 8; z = z_hi * 8 + z_lo), core: 2. Of those that a mesh axis runs over, the one named last changes fastest.
Arguments:
- stream: bfloat16 [16, 1792, 1152], P('tm', 'patch'), may hold values from -6 to 6
- stale_keys: bfloat16 [16, 1792, 1152], P(None, 'patch', 'tm'), may hold values from -10 to 10
- stale_values: bfloat16 [16, 1792, 1152], P(None, 'patch', 'tm'), may hold values from -6 to 6
- modulation: float32 [2, 3, 1152], replicated, may hold values from -4 to 4
- w_qkv: bfloat16 [2, 3, 1152, 1152], P(None, None, 'tm'), may hold values from -0.1875 to 0.1875
- w_out: bfloat16 [2, 1152, 1152], P(None, 'tm'), may hold values from -0.1875 to 0.1875
- qk_gain: float32 [2, 2, 72], replicated, may hold values from 1.4 to 7
Outputs:
- output: bfloat16 [16, 1792, 1152], P('tm', 'patch')
All inputs are finite; a program needn't handle non-finite values.
Results may differ from a plain program's by a relative error of at most 0.035.
Values may be sent and summed in bfloat16 or wider, within the bound.
No kernel may reach another device: no remote copies, remote signals or barrier semaphores. Data moves between devices by JAX's collectives and lax.ppermute only.
A program may use at most 64 MiB of HBM per device.

v0:
```python
import jax
import jax.numpy as jnp
from jax import lax
from jax.sharding import PartitionSpec as P

HEAD_DIM = 72


EPS = 1e-06


def softmax_rows(scores):
    top = jnp.max(scores, axis=-1, keepdims=True)
    expo = jnp.exp(scores - top)
    return expo / jnp.sum(expo, axis=-1, keepdims=True)


def modulate(stream, shift, scale):
    values = stream.astype(jnp.float32)
    center = jnp.mean(values, axis=-1, keepdims=True)
    spread = jnp.mean(jnp.square(values - center), axis=-1, keepdims=True)
    normed = (values - center) * lax.rsqrt(spread + EPS)
    return (normed * (1.0 + scale) + shift).astype(jnp.bfloat16)


def head_norm(values, gain):
    factor = lax.rsqrt(jnp.mean(values * values, axis=-1, keepdims=True) + EPS)
    return (values * factor * gain).astype(jnp.bfloat16)


def projections(hmod, weights, gains):
    mixed = jnp.einsum("fpd,ced->cfpe", hmod, weights, preferred_element_type=jnp.float32)
    width = mixed.shape[3]
    shaped = mixed.reshape(3, mixed.shape[1], mixed.shape[2], width // HEAD_DIM, HEAD_DIM)
    query = head_norm(shaped[0], gains[0])
    keys = head_norm(shaped[1], gains[1])
    values = shaped[2].astype(jnp.bfloat16)
    return jnp.stack([query, keys, values]).reshape(mixed.shape)


def front_end(modulation, w_qkv, qk_gain, block, piece):
    hmod = modulate(piece, modulation[block, 0], modulation[block, 1])
    return projections(hmod, w_qkv[block], qk_gain[block])


def local(stream, stale_keys, stale_values, modulation, w_qkv, w_out, qk_gain):
    rows = stream.shape[1]
    local_width = w_out.shape[1]
    heads_here = local_width // HEAD_DIM
    factor = HEAD_DIM ** (-0.5)
    packed = front_end(
        modulation, w_qkv, qk_gain, 0, lax.all_gather(stream, "tm", axis=0, tiled=True)
    )
    frames = packed.shape[1]
    old_keys, old_values = (
        lax.all_gather(stale_keys, "patch", axis=1, tiled=True),
        lax.all_gather(stale_values, "patch", axis=1, tiled=True),
    )
    spatial_len = old_keys.shape[1]
    offset = lax.axis_index("patch") * rows
    keys = lax.dynamic_update_slice_in_dim(old_keys, packed[1], offset, 1)
    values = lax.dynamic_update_slice_in_dim(old_values, packed[2], offset, 1)
    query4 = packed[0].reshape(frames, rows, heads_here, HEAD_DIM)
    keys4 = keys.reshape(frames, spatial_len, heads_here, HEAD_DIM)
    values4 = values.reshape(frames, spatial_len, heads_here, HEAD_DIM)
    scores = (
        jnp.einsum("fqhd,fkhd->fhqk", query4, keys4, preferred_element_type=jnp.float32) * factor
    )
    weights = softmax_rows(scores).astype(jnp.bfloat16)
    attn = jnp.einsum("fhqk,fkhd->fqhd", weights, values4, preferred_element_type=jnp.float32)
    attn = attn.astype(jnp.bfloat16).reshape(frames, rows, local_width)
    partial_mid = jnp.einsum("fpe,ed->fpd", attn, w_out[0], preferred_element_type=jnp.float32)
    summed = lax.psum_scatter(
        partial_mid.astype(jnp.bfloat16), "tm", scatter_dimension=0, tiled=True
    ).astype(jnp.float32)
    middle = (stream.astype(jnp.float32) + modulation[0, 2] * summed).astype(jnp.bfloat16)
    packed = front_end(
        modulation, w_qkv, qk_gain, 1, lax.all_gather(middle, "tm", axis=0, tiled=True)
    )
    query4 = packed[0].reshape(frames, rows, heads_here, HEAD_DIM)
    keys4 = packed[1].reshape(frames, rows, heads_here, HEAD_DIM)
    values4 = packed[2].reshape(frames, rows, heads_here, HEAD_DIM)
    scores = (
        jnp.einsum("fphd,gphd->phfg", query4, keys4, preferred_element_type=jnp.float32) * factor
    )
    weights = softmax_rows(scores).astype(jnp.bfloat16)
    attn = jnp.einsum("phfg,gphd->fphd", weights, values4, preferred_element_type=jnp.float32)
    attn = attn.astype(jnp.bfloat16).reshape(frames, rows, local_width)
    partial_out = jnp.einsum("fpe,ed->fpd", attn, w_out[1], preferred_element_type=jnp.float32)
    summed_out = lax.psum_scatter(
        partial_out.astype(jnp.bfloat16), "tm", scatter_dimension=0, tiled=True
    ).astype(jnp.float32)
    return (middle.astype(jnp.float32) + modulation[1, 2] * summed_out).astype(jnp.bfloat16)


def solution(mesh):
    placed = (
        P("tm", "patch", None),
        P(None, "patch", "tm"),
        P(None, "patch", "tm"),
        P(),
        P(None, None, "tm", None),
        P(None, "tm", None),
        P(),
    )
    return jax.shard_map(
        local, mesh=mesh, in_specs=placed, out_specs=P("tm", "patch", None), check_vma=False
    )
```

profile of v0, /device:TPU:1, one launch (start us, length us, event | category | flops | bytes accessed | tf_op | source)
XLA Modules:
  0.0 937.1 jit_solution(6152999744270605610)
XLA Ops:
  6.5 0.0 copy-start.5
  6.5 0.0 all-gather.7.cloned.1.call-start
  6.5 0.7 all-gather.7.cloned.1.call-update
  7.3 0.0 all-gather.9.cloned.1.call-start
  7.3 0.7 all-gather.9.cloned.1.call-update
  8.0 0.0 all-gather.5.cloned.1.call-start
  8.1 0.7 all-gather.5.cloned.1.call-update
  8.7 0.0 reduce-scatter.9.cloned.1.call-start
  8.8 0.9 slice_reduce_fusion.1
  9.7 0.8 slice_bitcast_fusion.1
  10.4 104.8 %all-gather.7.cloned.1.call-done = bf16[16,56,1152]{2,1,0:T(8,128)(2,1)} async-done(((bf16[1,56,1152]{2,1,0:T(8,128)(2,1)}), bf16[16,56,1152]{2,1,0:T(8,128)(2,1)}) %all-gather.7.cloned.1.call-update) | async-done | bytes 2064400 | tf_op jit(solution)/shard_map/all_gather | solution.py:52
  115.2 2.1 convert_reduce_fusion.1
  117.3 2.3 fusion.13
  119.6 0.0 copy-done.5
  119.6 0.0 copy-done
  119.6 2.0 fusion.25
  121.6 0.3 multiply_reduce_fusion.4
  122.0 225.7 %all-gather.9.cloned.1.call-done = bf16[16,1792,72]{2,1,0:T(8,128)(2,1)} async-done(((bf16[16,56,72]{2,1,0:T(8,128)(2,1)}), bf16[16,1792,72]{2,1,0:T(8,128)(2,1)}) %all-gather.9.cloned.1.call-update) | async-done | bytes 4128784 | tf_op jit(solution)/shard_map/all_gather | solution.py:56
  347.6 236.4 %all-gather.5.cloned.1.call-done = bf16[16,1792,72]{2,1,0:T(8,128)(2,1)} async-done(((bf16[16,56,72]{2,1,0:T(8,128)(2,1)}), bf16[16,1792,72]{2,1,0:T(8,128)(2,1)}) %all-gather.5.cloned.1.call-update) | async-done | bytes 4128784 | tf_op jit(solution)/shard_map/all_gather | solution.py:57
  584.1 1.0 fusion.50
  585.1 5.8 fusion.48
  590.9 0.0 copy-start.4
  590.9 4.2 fusion.72
  595.1 0.0 copy-done.4
  595.1 8.2 convolution_convert_fusion.1
  603.3 0.0 reduce-scatter.9.cloned.1.call-update
  603.4 0.0 all-gather.11.cloned.1.call-start
  603.4 107.4 %reduce-scatter.9.cloned.1.call-done = bf16[1,56,1152]{2,1,0:T(8,128)(2,1)} async-done(((bf16[16,56,1152]{2,1,0:T(8,128)(2,1)}), bf16[1,56,1152]{2,1,0:T(8,128)(2,1)}) %reduce-scatter.9.cloned.1.call-update) | async-done | bytes 129040
  710.8 0.0 copy-done.3
  710.8 1.6 add_convert_fusion.1
  712.4 0.0 all-gather.11.cloned.1.call-update
  712.4 0.2 reduce-scatter.11.cloned.1.call-start
  712.7 102.6 %all-gather.11.cloned.1.call-done = bf16[16,56,1152]{2,1,0:T(8,128)(2,1)} async-done(((bf16[1,56,1152]{2,1,0:T(8,128)(2,1)}), bf16[16,56,1152]{2,1,0:T(8,128)(2,1)}) %all-gather.11.cloned.1.call-update) | async-done | bytes 2064400 | tf_op jit(solution)/shard_map/all_gather | solution.py:78
  815.2 2.1 convert_reduce_fusion
  817.3 2.3 fusion.9
  819.6 0.0 copy-done.1
  819.6 2.0 fusion.28
  821.6 0.3 multiply_reduce_fusion.2
  822.0 0.3 fusion.43
  822.3 0.4 fusion.73
  822.7 0.0 copy-start.2
  822.7 0.3 convolution_multiply_fusion
  822.9 0.3 fusion.34
  823.3 2.1 convolution_convert_fusion
  825.4 0.0 reduce-scatter.11.cloned.1.call-update
  825.4 103.2 %reduce-scatter.11.cloned.1.call-done = bf16[1,56,1152]{2,1,0:T(8,128)(2,1)} async-done(((bf16[16,56,1152]{2,1,0:T(8,128)(2,1)}), bf16[1,56,1152]{2,1,0:T(8,128)(2,1)}) %reduce-scatter.11.cloned.1.call-update) | async-done | bytes 129040
  928.6 0.0 copy-done.2
  928.6 1.6 add_convert_fusion
  (11 shorter events, 0.1 us)
Async XLA Ops:
  6.5 113.1 %copy-start.5 = (bf16[2,3,72,1152]{3,2,1,0:T(8,128)(2,1)S(1)}, bf16[2,3,72,1152]{3,2,1,0:T(8,128)(2,1)}, u32[]{:S(2)}) copy-start(bf16[2,3,72,1152]{3,2,1,0:T(8,128)(2,1)} %param.11) | copy-start | bytes 2985988
  6.5 108.7 %all-gather.7.cloned.1.call-start = ((), (), s32[]{:S(2)}) async-start(), calls=%async_computation.3 | async-start | bytes 2193408 | tf_op jit(solution)/shard_map/all_gather | solution.py:52
  7.3 340.4 %all-gather.9.cloned.1.call-start = ((), (), s32[]{:S(2)}) async-start(), calls=%async_computation.4 | async-start | bytes 7569408 | tf_op jit(solution)/shard_map/all_gather | solution.py:56
  8.0 576.1 %all-gather.5.cloned.1.call-start = ((), (), s32[]{:S(2)}) async-start(), calls=%async_computation.2 | async-start | bytes 7569408 | tf_op jit(solution)/shard_map/all_gather | solution.py:57
  8.7 702.1 %reduce-scatter.9.cloned.1.call-start = ((), (), s32[]{:S(2)}) async-start(), calls=%async_computation.6 | async-start | bytes 2193408
  115.2 4.4 copy-start
  590.9 4.3 copy-start.4
  595.1 115.7 %copy-start.3 = (bf16[1,56,1152]{2,1,0:T(8,128)(2,1)S(1)}, bf16[1,56,1152]{2,1,0:T(8,128)(2,1)}, u32[]{:S(2)}) copy-start(bf16[1,56,1152]{2,1,0:T(8,128)(2,1)} %param.7) | copy-start | bytes 387076
  603.4 211.9 %all-gather.11.cloned.1.call-start = ((), (), s32[]{:S(2)}) async-start(), calls=%async_computation.5 | async-start | bytes 2193408 | tf_op jit(solution)/shard_map/all_gather | solution.py:78
  712.4 216.2 %reduce-scatter.11.cloned.1.call-start = ((), (), s32[]{:S(2)}) async-start(), calls=%async_computation.7 | async-start | bytes 2193408
  815.2 4.4 copy-start.1
  822.7 105.9 %copy-start.2 = (bf16[1,56,1152]{2,1,0:T(8,128)(2,1)S(1)}, bf16[1,56,1152]{2,1,0:T(8,128)(2,1)}, u32[]{:S(2)}) copy-start(bf16[1,56,1152]{2,1,0:T(8,128)(2,1)} %add_convert_fusion.1) | copy-start | bytes 387076
Sparse Core Ops, SparseCore 0:
  9.4 105.7 all-gather.6
  119.6 227.9 all-gather.8
  352.1 231.9 all-gather.4
  603.5 107.2 reduce-scatter.8
  712.9 102.2 all-gather.10
  825.5 103.0 reduce-scatter.10
where the time goes:
time: 944 us; the launch traced here: 937 us
  waiting for transfers between devices  882 us (93%)
  matrix products  21 us (2%)
  other arithmetic  19 us (2%)
  between operations  13.6 us (1%)
    all_gather x1, waiting for transfers between devices, local(): lax.all_gather(stale_values, 'patch', axis=1, tiled=True)  236 us
    all_gather x1, waiting for transfers between devices, local(): lax.all_gather(stale_keys, 'patch', axis=1, tiled=True)  226 us
    unnamed x8, waiting for transfers between devices  213 us
    all_gather x1, waiting for transfers between devices, local(): lax.all_gather(stream, 'tm', axis=0, tiled=True)  105 us
    all_gather x1, waiting for transfers between devices, local(): lax.all_gather(middle, 'tm', axis=0, tiled=True)  103 us
  transfers between devices with their start and end apart: 6, of which 6 were waited for; matrix products, arithmetic and copies ran while one was open for 1% of the time, Pallas kernels for 0%

commit v1 on v0

v1 whole, which is shorter than its diff:
```python
import functools

import jax
import jax.numpy as jnp
from jax import lax
from jax.experimental import pallas as pl
from jax.experimental.pallas import tpu as pltpu
from jax.sharding import Mesh
from jax.sharding import PartitionSpec as P

HEAD_DIM = 72
EPS = 1e-06
AXES = ("z", "c", "x", "y", "h")
SIZES = (8, 2, 4, 4, 2)
ROWS = 56
PLANE = 16
QBLOCK = 4 * ROWS
NEG = -1e30
VMEM_LIMIT = 48 * 1024 * 1024
NT = (((1,), (1,)), ((), ()))


def modulate(stream, shift, scale):
    values = stream.astype(jnp.float32)
    center = jnp.mean(values, axis=-1, keepdims=True)
    spread = jnp.mean(jnp.square(values - center), axis=-1, keepdims=True)
    normed = (values - center) * lax.rsqrt(spread + EPS)
    return (normed * (1.0 + scale) + shift).astype(jnp.bfloat16)


def head_norm(values, gain):
    factor = lax.rsqrt(jnp.mean(values * values, axis=-1, keepdims=True) + EPS)
    return (values * factor * gain).astype(jnp.bfloat16)


def dot(a, b, dims=(((1,), (0,)), ((), ()))):
    return lax.dot_general(a, b, dims, preferred_element_type=jnp.float32)


def spatial_kernel(tok, w, gain, keys, vals, wout, rowp, colp, out, q_s, k_s, v_s):
    step = pl.program_id(0)
    factor = HEAD_DIM ** (-0.5)

    @pl.when(step == 0)
    def _():
        raw = dot(tok[...], w[...], NT)
        q_s[...] = head_norm(raw[:, :HEAD_DIM], gain[0:1])
        k_s[...] = head_norm(raw[:, HEAD_DIM : 2 * HEAD_DIM], gain[1:2])
        v_s[...] = raw[:, 2 * HEAD_DIM :].astype(jnp.bfloat16)

    at = pl.ds(pl.multiple_of(step * QBLOCK, QBLOCK), QBLOCK)
    q = q_s[at]
    rows = rowp[at]
    old = dot(q, keys[...], NT)
    old = jnp.where(rows == colp[...], NEG, old)
    new = dot(q, k_s[at], NT)
    r_id = lax.broadcasted_iota(jnp.int32, (QBLOCK, QBLOCK), 0) // ROWS
    c_id = lax.broadcasted_iota(jnp.int32, (QBLOCK, QBLOCK), 1) // ROWS
    new = jnp.where(r_id == c_id, new, NEG)
    top = jnp.maximum(jnp.max(old, axis=1, keepdims=True), jnp.max(new, axis=1, keepdims=True))
    e_old = jnp.exp((old - top) * factor)
    e_new = jnp.exp((new - top) * factor)
    total = jnp.sum(e_old, axis=1, keepdims=True) + jnp.sum(e_new, axis=1, keepdims=True)
    mixed = dot(e_old.astype(jnp.bfloat16), vals[...]) + dot(e_new.astype(jnp.bfloat16), v_s[at])
    attn = (mixed / total).astype(jnp.bfloat16)
    out[...] = dot(attn, wout[...]).astype(jnp.bfloat16)


def spatial(tok, w, gain, keys, vals, wout, rowp, colp):
    rows, width = tok.shape
    whole = lambda a: pl.BlockSpec(a.shape, lambda i: (0,) * a.ndim)
    args = (tok, w, gain, keys, vals, wout, rowp, colp)
    return pl.pallas_call(
        spatial_kernel,
        grid=(rows // QBLOCK,),
        in_specs=[whole(a) for a in args],
        out_specs=pl.BlockSpec((QBLOCK, width), lambda i: (i, 0)),
        out_shape=jax.ShapeDtypeStruct((rows, width), jnp.bfloat16),
        scratch_shapes=[pltpu.VMEM((rows, HEAD_DIM), jnp.bfloat16)] * 3,
        compiler_params=pltpu.CompilerParams(vmem_limit_bytes=VMEM_LIMIT),
        cost_estimate=pl.CostEstimate(
            flops=1200_000_000, bytes_accessed=6_000_000, transcendentals=1_800_000
        ),
        name="spatial",
    )(*args)


def qkv_kernel(tok, w_own, w_sib, gain, own, sib):
    for w, out in ((w_own, own), (w_sib, sib)):
        raw = dot(tok[...], w[...], NT)
        out[0] = head_norm(raw[:, :HEAD_DIM], gain[0:1])
        out[1] = head_norm(raw[:, HEAD_DIM : 2 * HEAD_DIM], gain[1:2])
        out[2] = raw[:, 2 * HEAD_DIM :].astype(jnp.bfloat16)


def qkv_pair(tok, w_own, w_sib, gain):
    shape = jax.ShapeDtypeStruct((3, tok.shape[0], HEAD_DIM), jnp.bfloat16)
    return pl.pallas_call(
        qkv_kernel,
        out_shape=(shape, shape),
        compiler_params=pltpu.CompilerParams(vmem_limit_bytes=VMEM_LIMIT),
        cost_estimate=pl.CostEstimate(flops=450_000_000, bytes_accessed=3_000_000, transcendentals=0),
        name="qkv",
    )(tok, w_own, w_sib, gain)


def temporal_kernel(own, other, out):
    factor = HEAD_DIM ** (-0.5)
    half = own.shape[1]
    size = 2 * half * 8
    r_id = lax.broadcasted_iota(jnp.int32, (size, size), 0) % 8
    c_id = lax.broadcasted_iota(jnp.int32, (size, size), 1) % 8
    same = r_id == c_id

    for g in range(ROWS // 8):
        at = slice(8 * g, 8 * g + 8)

        def pick(i):
            return jnp.concatenate(
                [r[i, f, at].astype(jnp.float32) for r in (own, other) for f in range(half)], axis=0
            ).astype(jnp.bfloat16)

        scores = jnp.where(same, dot(pick(0), pick(1), NT), NEG)
        top = jnp.max(scores, axis=1, keepdims=True)
        expo = jnp.exp((scores - top) * factor)
        weights = (expo / jnp.sum(expo, axis=1, keepdims=True)).astype(jnp.bfloat16)
        mixed = dot(weights, pick(2)).astype(jnp.bfloat16)
        for f in range(2 * half):
            out[f // half, f % half, at] = mixed[8 * f : 8 * f + 8]


def temporal(own, other):
    shape = jax.ShapeDtypeStruct((2,) + own.shape[1:], jnp.bfloat16)
    return pl.pallas_call(
        temporal_kernel,
        out_shape=shape,
        compiler_params=pltpu.CompilerParams(vmem_limit_bytes=VMEM_LIMIT),
        cost_estimate=pl.CostEstimate(flops=50_000_000, bytes_accessed=1_000_000, transcendentals=120_000),
        name="temporal",
    )(own, other)


def flat(z, c, x, y, h):
    index = 0
    for value, size in zip((z, c, x, y, h), SIZES):
        index = index * size + value
    return index


def spread(offset):
    pairs = []
    for x in range(4):
        for y in range(4):
            q = 4 * x + y
            for h in range(2):
                start = 8 * h + q // 2
                end = (start + offset) % 16
                pairs.append(
                    (flat(start % 8, q % 2, x, y, start // 8), flat(end % 8, q % 2, x, y, end // 8))
                )
    return pairs


SWAP = [(0, 1), (1, 0)]


def column_weights(w):
    q = 4 * lax.axis_index("x") + lax.axis_index("y")
    here = 2 * lax.axis_index("z") + lax.axis_index("c")
    mine = jnp.where(q == here, w, jnp.zeros_like(w))
    for offset in (4, -3, 3, -2, 2, -1, 1):
        mine = mine + lax.ppermute(w, AXES, spread(offset))
    return mine + lax.ppermute(mine, "c", SWAP)


def local(stream, stale_keys, stale_values, modulation, w_qkv, w_out, qk_gain):
    width = stream.shape[2]
    h = lax.axis_index("h")
    c = lax.axis_index("c")

    packed = jnp.concatenate([w_qkv[0].reshape(3 * HEAD_DIM, width), w_out[0]], axis=0)
    w_col = column_weights(packed)
    w_full = lax.all_gather(w_out[1], ("z", "c"), axis=0)
    w_own = w_qkv[1].reshape(3 * HEAD_DIM, width)
    w_sib = lax.ppermute(w_own, "c", SWAP)

    main = jnp.concatenate([stale_keys, stale_values[:, :, :56]], axis=2)
    tail = stale_values[:, :, 56:].reshape(16, 7, 8, 16).transpose(0, 2, 1, 3).reshape(16, 8, 112)
    tail = jnp.pad(tail, ((0, 0), (0, 0), (0, 16)))
    chunk = jnp.concatenate([main, tail], axis=1)
    chunk = jnp.broadcast_to(chunk[:, None], (16, 2, 64, 128)).reshape(32, 64, 128)
    old = lax.all_to_all(chunk, ("z", "c", "h"), 0, 0, tiled=True)
    old = lax.all_to_all(old.reshape(16, 2, 64, 128), ("x", "y"), 0, 0, tiled=True)
    keys = old[:, :, :56, :72].reshape(-1, HEAD_DIM)
    rest = old[:, :, 56:, :112].reshape(16, 2, 8, 7, 16).transpose(0, 1, 3, 2, 4).reshape(16, 2, 56, 16)
    values = jnp.concatenate([old[:, :, :56, 72:], rest], axis=3).reshape(-1, HEAD_DIM)

    hmod = modulate(stream[0], modulation[0, 0], modulation[0, 1])
    tok = lax.all_to_all(
        jnp.broadcast_to(hmod[None], (PLANE,) + hmod.shape), ("x", "y"), 0, 0, tiled=True
    ).reshape(PLANE * ROWS, width)
    rowp = (2 * (lax.iota(jnp.int32, PLANE * ROWS) // ROWS) + h)[:, None]
    colp = (lax.iota(jnp.int32, 2 * PLANE * ROWS) // ROWS)[None, :]
    part = spatial(
        tok, w_col[: 3 * HEAD_DIM], qk_gain[0], keys, values, w_col[3 * HEAD_DIM :], rowp, colp
    )
    part = lax.all_to_all(part.reshape(PLANE, ROWS, width), ("x", "y"), 0, 0, tiled=True)
    summed = jnp.sum(part.astype(jnp.float32), axis=0)
    middle = (stream[0].astype(jnp.float32) + modulation[0, 2] * summed).astype(jnp.bfloat16)

    hmod = modulate(middle, modulation[1, 0], modulation[1, 1])
    tok = lax.all_gather(hmod, "z", axis=0).reshape(8 * ROWS, width)
    own, sib = qkv_pair(tok, w_own, w_sib, qk_gain[1])
    other = lax.ppermute(sib, "c", SWAP)
    shape = (3, 8, ROWS, HEAD_DIM)
    attn = temporal(own.reshape(shape), other.reshape(shape))
    attn = jnp.where(c == 0, attn, attn[::-1]).transpose(1, 0, 2, 3).reshape(16, ROWS, HEAD_DIM)
    attn = lax.all_to_all(attn, ("z", "c"), 0, 0, tiled=True)
    attn = attn.transpose(1, 0, 2).reshape(ROWS, width)
    summed = dot(attn, w_full.reshape(width, width))
    out = (middle.astype(jnp.float32) + modulation[1, 2] * summed).astype(jnp.bfloat16)
    return out[None]


def solution(mesh):
    wide = Mesh(mesh.devices.reshape(SIZES), AXES)
    tm, patch = ("z", "c"), ("x", "y", "h")
    placed = (
        P(tm, patch, None),
        P(None, patch, tm),
        P(None, patch, tm),
        P(),
        P(None, None, tm, None),
        P(None, tm, None),
        P(),
    )
    return jax.shard_map(
        local, mesh=wide, in_specs=placed, out_specs=P(tm, patch, None), check_vma=False
    )
```

time: 944 us -> 263 us (0.28)
  waiting for transfers between devices: 882 us -> 74.7 us
  starting transfers between devices: 0.38 us -> 83.4 us
  blocking collectives: 0 us -> 45.5 us
  matrix products: 21 us -> 3.04 us
  Pallas kernels: 0 us -> 15.5 us
  local copies, waits for them, and re-layouts: 0.82 us -> 14.8 us
    all_gather x4 -> x1, waiting for transfers between devices: 669 us -> 0.01 us  [local(): w_full = lax.all_gather(w_out[1], ('z', 'c'), axis=0)]
    unnamed x8 -> x1, waiting for transfers between devices: 213 us -> 0.02 us
    all_to_all x0 -> x5, waiting for transfers between devices: none -> 72.5 us  [the longest x1 26.3 us: local(): lax.all_to_all(part.reshape(PLANE, ROWS, width), ('x', 'y'), 0, 0, tiled=...]
    all_to_all x0 -> x5, starting transfers between devices: none -> 54.6 us  [the longest x1 23.4 us: local(): lax.all_to_all(part.reshape(PLANE, ROWS, width), ('x', 'y'), 0, 0, tiled=...]
    all_gather x0 -> x1, blocking collectives: none -> 45.5 us  [local(): tok = lax.all_gather(hmod, 'z', axis=0).reshape(8 * ROWS, width)]
    ppermute x0 -> x10, starting transfers between devices: none -> 28.8 us  [the longest x1 11.1 us: local(): other = lax.ppermute(sib, 'c', SWAP)]
    dot_general x7 -> x1, matrix products: 20.7 us -> 3.04 us  [dot(): return lax.dot_general(a, b, dims, preferred_element_type=jnp.float32)]
    pallas_call x0 -> x3, Pallas kernels: none -> 15.5 us  [the longest x1 9.57 us: spatial(): pl.pallas_call(spatial_kernel, grid=(rows // QBLOCK,), in_specs=[whole(a)...]
  transfers between devices with their start and end apart: 6 -> 16, of which waited for: 6 -> 7; matrix products, arithmetic and copies ran while one was open for 1% -> 8% of each run, Pallas kernels for 0% -> 6%
where the time goes in v1:
time: 263 us; the launch traced here: 262 us
  starting transfers between devices  83.4 us (32%)
  waiting for transfers between devices  74.7 us (28%)
  blocking collectives  45.5 us (17%)
  Pallas kernels  15.5 us (6%)
  local copies, waits for them, and re-layouts  14.8 us (6%)
  between operations  13.8 us (5%)
  other arithmetic  11.7 us (4%)
  matrix products  3.04 us (1%)
    all_gather x1, blocking collectives, local(): tok = lax.all_gather(hmod, 'z', axis=0).reshape(8 * ROWS, width)  45.5 us
    all_to_all x1, waiting for transfers between devices, local(): lax.all_to_all(part.reshape(PLANE, ROWS, width), ('x', 'y'), 0, 0, tiled=...  26.3 us
    all_to_all x1, starting transfers between devices, local(): lax.all_to_all(part.reshape(PLANE, ROWS, width), ('x', 'y'), 0, 0, tiled=...  23.4 us
    all_to_all x1, waiting for transfers between devices, local(): old = lax.all_to_all(chunk, ('z', 'c', 'h'), 0, 0, tiled=True)  19.7 us
    all_to_all x1, starting transfers between devices, local(): old = lax.all_to_all(chunk, ('z', 'c', 'h'), 0, 0, tiled=True)  16.8 us
    all_to_all x1, waiting for transfers between devices, local(): attn = lax.all_to_all(attn, ('z', 'c'), 0, 0, tiled=True)  15.8 us
    ppermute x1, starting transfers between devices, local(): other = lax.ppermute(sib, 'c', SWAP)  11.1 us
    pallas_call x1, Pallas kernels, spatial(): pl.pallas_call(spatial_kernel, grid=(rows // QBLOCK,), in_specs=[whole(a)...  9.57 us
  transfers between devices with their start and end apart: 16, of which 7 were waited for; matrix products, arithmetic and copies ran while one was open for 8% of the time, Pallas kernels for 6%

profile of v1, /device:TPU:1, one launch (start us, length us, event | category | flops | bytes accessed | tf_op | source)
XLA Modules:
  0.0 262.3 jit_solution(12318187080671236751)
XLA Ops:
  6.5 1.1 slice_bitcast_fusion
  8.1 0.9 broadcast_in_dim.13
  9.0 16.8 %all-to-all-start.1 = ((bf16[32,64,128]{2,1,0:T(8,128)(2,1)}), bf16[32,64,128]{2,1,0:T(8,128)(2,1)}, u32[]{:S(2)}, u32[]{:S(2)}) async-start(bf16[32,64,128]{2,1,0:T(8,128)(2,1)} %bitcast.8), calls=%async_computation.1 | async-start | bytes 1048576 | tf_op jit(solution)/shard_map/all_to_all | solution.py:192
  25.9 0.7 slice_bitcast_fusion.1
  26.6 0.9 pad_maximum_fusion
  27.6 0.7 collective-permute-start
  28.2 0.7 collective-permute-start.1
  29.0 1.5 collective-permute-start.2
  30.5 1.5 collective-permute-start.3
  32.0 1.5 collective-permute-start.4
  33.8 19.7 %all-to-all-done.1 = bf16[32,64,128]{2,1,0:T(8,128)(2,1)} async-done(((bf16[32,64,128]{2,1,0:T(8,128)(2,1)}), bf16[32,64,128]{2,1,0:T(8,128)(2,1)}, u32[]{:S(2)}, u32[]{:S(2)}) %all-to-all-start.1) | async-done | bytes 524320 | tf_op jit(solution)/shard_map/all_to_all | solution.py:192
  53.5 6.8 %all-to-all-start.2 = ((bf16[16,2,64,128]{3,2,1,0:T(8,128)(2,1)}), bf16[16,2,64,128]{3,2,1,0:T(8,128)(2,1)S(1)}, u32[]{:S(2)}, u32[]{:S(2)}) async-start(bf16[16,2,64,128]{3,2,1,0:T(8,128)(2,1)} %bitcast.9), calls=%async_computation.2 | async-start | bytes 1048576 | tf_op jit(solution)/shard_map/all_to_all | solution.py:193
  60.3 0.7 slice_reduce_fusion.1
  61.0 1.5 collective-permute-start.5
  62.5 1.5 collective-permute-start.6
  64.1 5.3 %all-to-all-done.2 = bf16[16,2,64,128]{3,2,1,0:T(8,128)(2,1)S(1)} async-done(((bf16[16,2,64,128]{3,2,1,0:T(8,128)(2,1)}), bf16[16,2,64,128]{3,2,1,0:T(8,128)(2,1)S(1)}, u32[]{:S(2)}, u32[]{:S(2)}) %all-to-all-start.2) | async-done | bytes 524320 | tf_op jit(solution)/shard_map/all_to_all | solution.py:193
  69.5 1.5 broadcast_in_dim.11
  71.0 3.9 %all-to-all-start = ((bf16[16,56,1152]{2,1,0:T(8,128)(2,1)}), bf16[16,56,1152]{2,1,0:T(8,128)(2,1)S(1)}, u32[]{:S(2)}, u32[]{:S(2)}) async-start(bf16[16,56,1152]{2,1,0:T(8,128)(2,1)} %broadcast_in_dim.11), calls=%async_computation | async-start | bytes 4128768 | tf_op jit(solution)/shard_map/all_to_all | solution.py:199
  75.0 3.9 %add_add_fusion = bf16[288,1152]{1,0:T(8,128)(2,1)} fusion(bf16[288,1152]{1,0:T(8,128)(2,1)} %collective-permute-done.6, bf16[288,1152]{1,0:T(8,128)(2,1)} %collective-permute-done.5, bf16[288,1152]{1,0:T(8,128)(2,1)} %collective-permute-done.4, bf16[288,1152]{1,0:T(8,128)(2,1)} %collective-permute-done.3, bf16[288,1152]{1,0:T(8,128)(2,1)} %collective-permute-done.2, ...), kind=kLoop, calls=%fused_computation.11 | loop fusion | flops 6967296 | bytes 5971969 | tf_op jit(solution)/shard_map/add | solution.py:172
  78.9 6.2 %collective-permute-start.7 = (bf16[288,1152]{1,0:T(8,128)(2,1)}, bf16[288,1152]{1,0:T(8,128)(2,1)S(1)}, u32[]{:S(2)}, u32[]{:S(2)}) collective-permute-start(bf16[288,1152]{1,0:T(8,128)(2,1)} %add_add_fusion), channel_id=1, source_target_pairs={{0,32},{32,0},{1,33},{33,1},{2,34},{34,2},{3,35},{35,3},{4,36},{36... | collective-permute-start | bytes 1990664 | tf_op jit(solution)/shard_map/ppermute | solution.py:173
  85.2 0.9 fusion.6.rowp
  86.1 0.9 collective-permute-done.7
  87.1 1.3 add.143
  88.4 0.7 slice.80.wout
  89.1 0.8 slice.79
  89.9 1.1 reshape.250
  91.1 1.1 copy.13
  92.2 1.3 slice.78
  93.4 1.0 pad_maximum_fusion.1.vals
  94.5 5.3 %all-to-all-done = bf16[16,56,1152]{2,1,0:T(8,128)(2,1)S(1)} async-done(((bf16[16,56,1152]{2,1,0:T(8,128)(2,1)}), bf16[16,56,1152]{2,1,0:T(8,128)(2,1)S(1)}, u32[]{:S(2)}, u32[]{:S(2)}) %all-to-all-start) | async-done | bytes 2064416 | tf_op jit(solution)/shard_map/all_to_all | solution.py:199
  99.8 1.0 copy-done.1
  100.8 1.0 copy-done.2
  101.8 0.9 copy-done.3
  102.8 9.6 %spatial.1 = bf16[896,1152]{1,0:T(8,128)(2,1)S(1)} custom-call(bf16[896,1152]{1,0:T(8,128)(2,1)S(1)} %bitcast.67, bf16[216,1152]{1,0:T(8,128)(2,1)S(1)} %slice.76.w, f32[2,72]{1,0:T(2,128)S(1)} %get-tuple-element.22.gain, bf16[1792,72]{1,0:T(8,128)(2,1)S(1)} %bitcast.72, bf16[1792,72]{1,0:T(8,128)(2,1)S(1)} %copy-done.2, bf16[72,1152]{1,0:T(8,128)(2,1)S(1)} %copy-done.3, ...), custom_call_target="tpu_custom_call" | custom-call | flops 1200000000 | bytes 6000000 | tf_op jit(solution)/shard_map/spatial/pallas_call | solution.py:73
  112.3 1.4 copy-done
  113.7 23.4 %all-to-all-start.3 = ((bf16[16,56,1152]{2,1,0:T(8,128)(2,1)}), bf16[16,56,1152]{2,1,0:T(8,128)(2,1)}, u32[]{:S(2)}, u32[]{:S(2)}) async-start(bf16[16,56,1152]{2,1,0:T(8,128)(2,1)} %bitcast.68), calls=%async_computation.3 | async-start | bytes 4128768 | tf_op jit(solution)/shard_map/all_to_all | solution.py:207
  137.2 2.5 collective-permute-start.8
  139.7 26.3 %all-to-all-done.3 = bf16[16,56,1152]{2,1,0:T(8,128)(2,1)} async-done(((bf16[16,56,1152]{2,1,0:T(8,128)(2,1)}), bf16[16,56,1152]{2,1,0:T(8,128)(2,1)}, u32[]{:S(2)}, u32[]{:S(2)}) %all-to-all-start.3) | async-done | bytes 2064416 | tf_op jit(solution)/shard_map/all_to_all | solution.py:207
  166.0 1.9 convert_reduce_fusion
  168.4 45.5 %all_gather.7 = bf16[8,56,1152]{2,1,0:T(8,128)(2,1)S(1)} all-gather(bf16[1,56,1152]{2,1,0:T(8,128)(2,1)S(1)} %add_convert_fusion), channel_id=1, replica_groups=mesh['z'=8,'c'=2,'x'=4,'y'=4,'h'=2] {'z'}, dimensions={0}, use_global_device_ids=true | all-gather | bytes 1161216 | tf_op jit(solution)/shard_map/all_gather | solution.py:212
  213.9 3.5 %qkv.1 = (bf16[3,448,72]{2,1,0:T(8,128)(2,1)S(1)}, bf16[3,448,72]{2,1,0:T(8,128)(2,1)S(1)}) custom-call(bf16[448,1152]{1,0:T(8,128)(2,1)S(1)} %bitcast.69, bf16[216,1152]{1,0:T(8,128)(2,1)S(1)} %bitcast.71, bf16[216,1152]{1,0:T(8,128)(2,1)S(1)} %collective-permute-done.8.w_sib, f32[2,72]{1,0:T(2,128)S(1)} %get-tuple-element.21.gain), custom_call_target="tpu_custom_call" | custom-call | flops 450000000 | bytes 3000000 | tf_op jit(solution)/shard_map/qkv/pallas_call | solution.py:98
  217.4 11.1 %collective-permute-start.9 = (bf16[3,448,72]{2,1,0:T(8,128)(2,1)S(1)}, bf16[3,448,72]{2,1,0:T(8,128)(2,1)S(1)}, u32[]{:S(2)}, u32[]{:S(2)}) collective-permute-start(bf16[3,448,72]{2,1,0:T(8,128)(2,1)S(1)} %get-tuple-element.8), channel_id=1, source_target_pairs={{0,32},{32,0},{1,33},{33,1},{2,34},{34,2},{3,35},{35,3},{4,36},{36... | collective-permute-start | bytes 580616 | tf_op jit(solution)/shard_map/ppermute | solution.py:214
  228.5 1.3 collective-permute-done.9
  229.8 2.4 temporal.1
  232.2 0.7 copy.14
  232.9 3.7 %all-to-all-start.4 = ((bf16[16,56,72]{2,1,0:T(8,128)(2,1)}), bf16[16,56,72]{2,1,0:T(8,128)(2,1)S(1)}, u32[]{:S(2)}, u32[]{:S(2)}) async-start(bf16[16,56,72]{2,1,0:T(8,128)(2,1)} %bitcast.22), calls=%async_computation.4 | async-start | bytes 458752 | tf_op jit(solution)/shard_map/all_to_all | solution.py:218
  236.6 15.8 %all-to-all-done.4 = bf16[16,56,72]{2,1,0:T(8,128)(2,1)S(1)} async-done(((bf16[16,56,72]{2,1,0:T(8,128)(2,1)}), bf16[16,56,72]{2,1,0:T(8,128)(2,1)S(1)}, u32[]{:S(2)}, u32[]{:S(2)}) %all-to-all-start.4) | async-done | bytes 129056 | tf_op jit(solution)/shard_map/all_to_all | solution.py:218
  252.5 3.0 %fusion.3 = bf16[1,56,1152]{2,1,0:T(8,128)(2,1)} fusion(bf16[16,72,1152]{2,1,0:T(8,128)(2,1)} %all-gather.2.cloned.1.call-done, bf16[56,1152]{1,0:T(8,128)(2,1)S(1)} %get-tuple-element.16, bf16[16,56,72]{2,1,0:T(8,128)(2,1)S(1)} %all-to-all-done.4, f32[1152]{0:T(1024)S(1)} %get-tuple-element.9), kind=kOutput, calls=%fused_computation.5 | convolution fusion | flops 148893696 | bytes 3045888 | tf_op jit(solution)/shard_map/dot_general | solution.py:37
  (62 shorter events, 1.7 us)
Async XLA Ops:
  6.5 1.4 copy-start.9
  6.5 1.4 copy-start.13
  7.9 17.9 %copy-start.12 = (bf16[2,72,1152]{2,1,0:T(8,128)(2,1)S(1)}, bf16[2,72,1152]{2,1,0:T(8,128)(2,1)}, u32[]{:S(2)}) copy-start(bf16[2,72,1152]{2,1,0:T(8,128)(2,1)} %param.12) | copy-start | bytes 995332
  8.1 18.5 %copy-start.8 = (bf16[2,3,72,1152]{3,2,1,0:T(8,128)(2,1)S(1)}, bf16[2,3,72,1152]{3,2,1,0:T(8,128)(2,1)}, u32[]{:S(2)}) copy-start(bf16[2,3,72,1152]{3,2,1,0:T(8,128)(2,1)} %param.11) | copy-start | bytes 2985988
  9.0 44.5 %all-to-all-start.1 = ((bf16[32,64,128]{2,1,0:T(8,128)(2,1)}), bf16[32,64,128]{2,1,0:T(8,128)(2,1)}, u32[]{:S(2)}, u32[]{:S(2)}) async-start(bf16[32,64,128]{2,1,0:T(8,128)(2,1)} %bitcast.8), calls=%async_computation.1 | async-start | bytes 1048576 | tf_op jit(solution)/shard_map/all_to_all | solution.py:192
  26.6 7.0 %copy-start.6 = (bf16[1,56,1152]{2,1,0:T(8,128)(2,1)S(1)}, bf16[1,56,1152]{2,1,0:T(8,128)(2,1)}, u32[]{:S(2)}) copy-start(bf16[1,56,1152]{2,1,0:T(8,128)(2,1)} %param.7) | copy-start | bytes 387076
  26.6 33.7 %copy-start.16 = (f32[2,3,1152]{2,0,1:T(2,128)S(1)}, f32[2,3,1152]{2,0,1:T(2,128)}, u32[]{:S(2)}) copy-start(f32[2,3,1152]{2,0,1:T(2,128)} %param.10) | copy-start | bytes 82948
  27.6 33.4 %collective-permute-start = (bf16[288,1152]{1,0:T(8,128)(2,1)}, bf16[288,1152]{1,0:T(8,128)(2,1)S(1)}, u32[]{:S(2)}, u32[]{:S(2)}) collective-permute-start(bf16[288,1152]{1,0:T(8,128)(2,1)} %pad_maximum_fusion), channel_id=1, source_target_pairs={{0,256},{1,257},{34,290},{35,291},{68,324},{69,325},{102,358},{103... | collective-permute-start | bytes 1990664 | tf_op jit(solution)/shard_map/ppermute | solution.py:172
  28.2 34.3 %collective-permute-start.1 = (bf16[288,1152]{1,0:T(8,128)(2,1)}, bf16[288,1152]{1,0:T(8,128)(2,1)S(1)}, u32[]{:S(2)}, u32[]{:S(2)}) collective-permute-start(bf16[288,1152]{1,0:T(8,128)(2,1)} %pad_maximum_fusion), channel_id=1, source_target_pairs={{0,321},{1,320},{34,355},{35,354},{68,389},{69,388},{102,423},{103... | collective-permute-start | bytes 1990664 | tf_op jit(solution)/shard_map/ppermute | solution.py:172
  29.0 46.0 %collective-permute-start.2 = (bf16[288,1152]{1,0:T(8,128)(2,1)}, bf16[288,1152]{1,0:T(8,128)(2,1)}, u32[]{:S(2)}, u32[]{:S(2)}) collective-permute-start(bf16[288,1152]{1,0:T(8,128)(2,1)} %pad_maximum_fusion), channel_id=1, source_target_pairs={{0,192},{1,193},{34,226},{35,227},{68,260},{69,261},{102,294},{103... | collective-permute-start | bytes 1990664 | tf_op jit(solution)/shard_map/ppermute | solution.py:172
  30.5 44.5 %collective-permute-start.3 = (bf16[288,1152]{1,0:T(8,128)(2,1)}, bf16[288,1152]{1,0:T(8,128)(2,1)}, u32[]{:S(2)}, u32[]{:S(2)}) collective-permute-start(bf16[288,1152]{1,0:T(8,128)(2,1)} %pad_maximum_fusion), channel_id=1, source_target_pairs={{0,385},{1,384},{34,419},{35,418},{68,453},{69,452},{102,487},{103... | collective-permute-start | bytes 1990664 | tf_op jit(solution)/shard_map/ppermute | solution.py:172
  32.0 43.0 %collective-permute-start.4 = (bf16[288,1152]{1,0:T(8,128)(2,1)}, bf16[288,1152]{1,0:T(8,128)(2,1)}, u32[]{:S(2)}, u32[]{:S(2)}) collective-permute-start(bf16[288,1152]{1,0:T(8,128)(2,1)} %pad_maximum_fusion), channel_id=1, source_target_pairs={{0,128},{1,129},{34,162},{35,163},{68,196},{69,197},{102,230},{103... | collective-permute-start | bytes 1990664 | tf_op jit(solution)/shard_map/ppermute | solution.py:172
  53.5 15.9 %all-to-all-start.2 = ((bf16[16,2,64,128]{3,2,1,0:T(8,128)(2,1)}), bf16[16,2,64,128]{3,2,1,0:T(8,128)(2,1)S(1)}, u32[]{:S(2)}, u32[]{:S(2)}) async-start(bf16[16,2,64,128]{3,2,1,0:T(8,128)(2,1)} %bitcast.9), calls=%async_computation.2 | async-start | bytes 1048576 | tf_op jit(solution)/shard_map/all_to_all | solution.py:193
  61.0 10.0 %copy-start.10 = (bf16[288,1152]{1,0:T(8,128)(2,1)}, bf16[288,1152]{1,0:T(8,128)(2,1)S(1)}, u32[]{:S(2)}) copy-start(bf16[288,1152]{1,0:T(8,128)(2,1)S(1)} %collective-permute-done) | copy-start | bytes 1990660
  61.0 14.0 %collective-permute-start.5 = (bf16[288,1152]{1,0:T(8,128)(2,1)}, bf16[288,1152]{1,0:T(8,128)(2,1)}, u32[]{:S(2)}, u32[]{:S(2)}) collective-permute-start(bf16[288,1152]{1,0:T(8,128)(2,1)} %pad_maximum_fusion), channel_id=1, source_target_pairs={{0,449},{1,448},{34,483},{35,482},{68,4},{69,5},{102,38},{103,39},... | collective-permute-start | bytes 1990664 | tf_op jit(solution)/shard_map/ppermute | solution.py:172
  62.5 8.5 %copy-start.11 = (bf16[288,1152]{1,0:T(8,128)(2,1)}, bf16[288,1152]{1,0:T(8,128)(2,1)S(1)}, u32[]{:S(2)}) copy-start(bf16[288,1152]{1,0:T(8,128)(2,1)S(1)} %collective-permute-done.1) | copy-start | bytes 1990660
  62.5 12.5 %collective-permute-start.6 = (bf16[288,1152]{1,0:T(8,128)(2,1)}, bf16[288,1152]{1,0:T(8,128)(2,1)}, u32[]{:S(2)}, u32[]{:S(2)}) collective-permute-start(bf16[288,1152]{1,0:T(8,128)(2,1)} %pad_maximum_fusion), channel_id=1, source_target_pairs={{0,64},{1,65},{34,98},{35,99},{68,132},{69,133},{102,166},{103,167... | collective-permute-start | bytes 1990664 | tf_op jit(solution)/shard_map/ppermute | solution.py:172
  69.5 1.5 copy-start.4
  71.0 28.8 %all-to-all-start = ((bf16[16,56,1152]{2,1,0:T(8,128)(2,1)}), bf16[16,56,1152]{2,1,0:T(8,128)(2,1)S(1)}, u32[]{:S(2)}, u32[]{:S(2)}) async-start(bf16[16,56,1152]{2,1,0:T(8,128)(2,1)} %broadcast_in_dim.11), calls=%async_computation | async-start | bytes 4128768 | tf_op jit(solution)/shard_map/all_to_all | solution.py:199
  74.9 161.7 %all-gather.2.cloned.1.call-start = ((), (), s32[]{:S(2)}) async-start(), calls=%async_computation.5 | async-start | bytes 2820096 | tf_op jit(solution)/shard_map/all_gather | solution.py:183
  74.9 11.2 %copy-start.17 = (f32[2,2,72]{2,1,0:T(2,128)S(1)}, f32[2,2,72]{2,1,0:T(2,128)}, u32[]{:S(2)}) copy-start(f32[2,2,72]{2,1,0:T(2,128)} %param.13) | copy-start | bytes 3460
  78.9 8.2 %collective-permute-start.7 = (bf16[288,1152]{1,0:T(8,128)(2,1)}, bf16[288,1152]{1,0:T(8,128)(2,1)S(1)}, u32[]{:S(2)}, u32[]{:S(2)}) collective-permute-start(bf16[288,1152]{1,0:T(8,128)(2,1)} %add_add_fusion), channel_id=1, source_target_pairs={{0,32},{32,0},{1,33},{33,1},{2,34},{34,2},{3,35},{35,3},{4,36},{36... | collective-permute-start | bytes 1990664 | tf_op jit(solution)/shard_map/ppermute | solution.py:173
  92.2 2.3 copy-start.5
  99.8 1.0 copy-start.1
  100.8 1.0 copy-start.2
  101.8 0.9 copy-start.3
  112.3 1.4 copy-start
  113.7 52.3 %all-to-all-start.3 = ((bf16[16,56,1152]{2,1,0:T(8,128)(2,1)}), bf16[16,56,1152]{2,1,0:T(8,128)(2,1)}, u32[]{:S(2)}, u32[]{:S(2)}) async-start(bf16[16,56,1152]{2,1,0:T(8,128)(2,1)} %bitcast.68), calls=%async_computation.3 | async-start | bytes 4128768 | tf_op jit(solution)/shard_map/all_to_all | solution.py:207
  137.1 30.8 %copy-start.7 = (bf16[1,56,1152]{2,1,0:T(8,128)(2,1)S(1)}, bf16[1,56,1152]{2,1,0:T(8,128)(2,1)}, u32[]{:S(2)}) copy-start(bf16[1,56,1152]{2,1,0:T(8,128)(2,1)} %param.7) | copy-start | bytes 387076
  137.2 31.1 %copy-start.14 = (f32[1152]{0:T(1024)S(1)}, f32[1152]{0:T(1024)}, u32[]{:S(2)}) copy-start(f32[1152]{0:T(1024)} %get-tuple-element.13) | copy-start | bytes 13828
  137.2 31.1 %copy-start.15 = (f32[1152]{0:T(1024)S(1)}, f32[1152]{0:T(1024)}, u32[]{:S(2)}) copy-start(f32[1152]{0:T(1024)} %get-tuple-element.14) | copy-start | bytes 13828
  137.2 76.7 %collective-permute-start.8 = (bf16[216,1152]{1,0:T(8,128)(2,1)S(1)}, bf16[216,1152]{1,0:T(8,128)(2,1)S(1)}, u32[]{:S(2)}, u32[]{:S(2)}) collective-permute-start(bf16[216,1152]{1,0:T(8,128)(2,1)S(1)} %bitcast.70), channel_id=1, source_target_pairs={{0,32},{32,0},{1,33},{33,1},{2,34},{34,2},{3,35},{35,3},{4,36},{36... | collective-permute-start | bytes 1493000 | tf_op jit(solution)/shard_map/ppermute | solution.py:185
  217.4 12.4 %collective-permute-start.9 = (bf16[3,448,72]{2,1,0:T(8,128)(2,1)S(1)}, bf16[3,448,72]{2,1,0:T(8,128)(2,1)S(1)}, u32[]{:S(2)}, u32[]{:S(2)}) collective-permute-start(bf16[3,448,72]{2,1,0:T(8,128)(2,1)S(1)} %get-tuple-element.8), channel_id=1, source_target_pairs={{0,32},{32,0},{1,33},{33,1},{2,34},{34,2},{3,35},{35,3},{4,36},{36... | collective-permute-start | bytes 580616 | tf_op jit(solution)/shard_map/ppermute | solution.py:214
  232.9 19.6 %all-to-all-start.4 = ((bf16[16,56,72]{2,1,0:T(8,128)(2,1)}), bf16[16,56,72]{2,1,0:T(8,128)(2,1)S(1)}, u32[]{:S(2)}, u32[]{:S(2)}) async-start(bf16[16,56,72]{2,1,0:T(8,128)(2,1)} %bitcast.22), calls=%async_computation.4 | async-start | bytes 458752 | tf_op jit(solution)/shard_map/all_to_all | solution.py:218
Sparse Core Ops, SparseCore 0:
  85.3 121.4 all-gather.1

commit v2 on v1

v2 whole, which is shorter than its diff:
```python
import functools

import jax
import jax.numpy as jnp
from jax import lax
from jax.experimental import pallas as pl
from jax.experimental.pallas import tpu as pltpu
from jax.sharding import Mesh
from jax.sharding import PartitionSpec as P

HEAD_DIM = 72
EPS = 1e-06
AXES = ("z", "c", "x", "y", "h")
SIZES = (8, 2, 4, 4, 2)
ROWS = 56
PLANE = 16
QBLOCK = 4 * ROWS
NEG = -1e30
VMEM_LIMIT = 48 * 1024 * 1024
NT = (((1,), (1,)), ((), ()))


def normed(values, shift, scale):
    center = jnp.mean(values, axis=-1, keepdims=True)
    spread = jnp.mean(jnp.square(values - center), axis=-1, keepdims=True)
    unit = (values - center) * lax.rsqrt(spread + EPS)
    return (unit * (1.0 + scale) + shift).astype(jnp.bfloat16)


def head_norm(values, gain):
    factor = lax.rsqrt(jnp.mean(values * values, axis=-1, keepdims=True) + EPS)
    return (values * factor * gain).astype(jnp.bfloat16)


def dot(a, b, dims=(((1,), (0,)), ((), ()))):
    return lax.dot_general(a, b, dims, preferred_element_type=jnp.float32)


def call(kernel, args, out_shape, name, scratch=(), flops=0, moved=0, trans=0, grid=None, specs=None):
    extra = {} if grid is None else {"grid": grid, "in_specs": specs[0], "out_specs": specs[1]}
    return pl.pallas_call(
        kernel,
        out_shape=out_shape,
        scratch_shapes=list(scratch),
        compiler_params=pltpu.CompilerParams(vmem_limit_bytes=VMEM_LIMIT),
        cost_estimate=pl.CostEstimate(flops=flops, bytes_accessed=moved, transcendentals=trans),
        name=name,
        **extra,
    )(*args)


def modulate_kernel(x, mod, out):
    out[...] = normed(x[...].astype(jnp.float32), mod[0:1], mod[1:2])


def modulate(x, mod):
    shape = jax.ShapeDtypeStruct(x.shape, jnp.bfloat16)
    return call(modulate_kernel, (x, mod), shape, "modulate", moved=300_000)


def qkv_kernel(*refs):
    toks, (w, gain, out) = refs[:-3], refs[-3:]
    rows = toks[0].shape[0]
    for i, tok in enumerate(toks):
        raw = dot(tok[...], w[...], NT)
        at = slice(i * rows, (i + 1) * rows)
        out[0, at] = head_norm(raw[:, :HEAD_DIM], gain[0:1])
        out[1, at] = head_norm(raw[:, HEAD_DIM : 2 * HEAD_DIM], gain[1:2])
        out[2, at] = raw[:, 2 * HEAD_DIM :].astype(jnp.bfloat16)


def qkv(toks, w, gain):
    rows = sum(t.shape[0] for t in toks)
    shape = jax.ShapeDtypeStruct((3, rows, HEAD_DIM), jnp.bfloat16)
    flops = 2 * rows * w.shape[0] * w.shape[1]
    return call(qkv_kernel, (*toks, w, gain), shape, "qkv", flops=flops, moved=3_000_000)


def spatial_kernel(order, q, old, rowp, colp, w, out, vals_s, old_s, part_s):
    step = pl.program_id(0)
    factor = HEAD_DIM ** (-0.5)

    @pl.when(step == 0)
    def _():
        raw = old[...].astype(jnp.float32)
        vals_s[:, :, :56] = raw[:, :56, HEAD_DIM:]
        for j in range(7):
            vals_s[:, 8 * j : 8 * j + 8, 56:72] = raw[:, 56:, 16 * j : 16 * j + 16]
        old_s[...] = raw[:, :56, :HEAD_DIM].reshape(old_s.shape).astype(jnp.bfloat16)

    at = pl.ds(pl.multiple_of(step * QBLOCK, QBLOCK), QBLOCK)
    query, key, value = q[0, at], q[1, at], q[2, at]
    old_values = vals_s[...].reshape(old_s.shape).astype(jnp.bfloat16)
    far = dot(query, old_s[...], NT)
    far = jnp.where(rowp[at] == colp[...], NEG, far)
    near = dot(query, key, NT)
    r_id = lax.broadcasted_iota(jnp.int32, (QBLOCK, QBLOCK), 0) // ROWS
    c_id = lax.broadcasted_iota(jnp.int32, (QBLOCK, QBLOCK), 1) // ROWS
    near = jnp.where(r_id == c_id, near, NEG)
    top = jnp.maximum(jnp.max(far, axis=1, keepdims=True), jnp.max(near, axis=1, keepdims=True))
    e_far = jnp.exp((far - top) * factor)
    e_near = jnp.exp((near - top) * factor)
    total = jnp.sum(e_far, axis=1, keepdims=True) + jnp.sum(e_near, axis=1, keepdims=True)
    mixed = dot(e_far.astype(jnp.bfloat16), old_values) + dot(e_near.astype(jnp.bfloat16), value)
    part_s[...] = dot((mixed / total).astype(jnp.bfloat16), w[...])
    for j in range(QBLOCK // ROWS):
        piece = part_s[j * ROWS : (j + 1) * ROWS].astype(jnp.bfloat16)
        out[order[step * (QBLOCK // ROWS) + j]] = piece


def spatial(order, q, old, rowp, colp, w):
    rows = q.shape[1]
    whole = lambda a: pl.BlockSpec(a.shape, lambda i: (0,) * a.ndim)
    out = jax.ShapeDtypeStruct((PLANE, ROWS, w.shape[1]), jnp.bfloat16)
    args = (q, old, rowp, colp, w)
    specs = (
        [pl.BlockSpec(memory_space=pltpu.SMEM)] + [whole(a) for a in args],
        pl.BlockSpec(out.shape, lambda i: (0, 0, 0)),
    )
    scratch = (
        pltpu.VMEM((2 * PLANE, ROWS, HEAD_DIM), jnp.float32),
        pltpu.VMEM((2 * PLANE * ROWS, HEAD_DIM), jnp.bfloat16),
        pltpu.VMEM((QBLOCK, w.shape[1]), jnp.float32),
    )
    return call(
        spatial_kernel, (order, *args), out, "spatial", scratch, flops=600_000_000, moved=2_000_000,
        trans=1_800_000, grid=(rows // QBLOCK,), specs=specs,
    )


def combine_kernel(part, resid, mod, middle, hmod):
    summed = part[0].astype(jnp.float32)
    for i in range(1, part.shape[0]):
        summed = summed + part[i].astype(jnp.float32)
    mid = (resid[...].astype(jnp.float32) + mod[0:1] * summed).astype(jnp.bfloat16)
    middle[...] = mid
    hmod[...] = normed(mid.astype(jnp.float32), mod[1:2], mod[2:3])


def combine(part, resid, mod):
    out = jax.ShapeDtypeStruct(resid.shape, jnp.bfloat16)
    return call(combine_kernel, (part, resid, mod), (out, out), "combine", moved=2_500_000)


def project_kernel(heads, attn, w, resid, gate, out, attn_s):
    for g in range(PLANE):
        attn_s[:, g * HEAD_DIM : (g + 1) * HEAD_DIM] = attn[heads[g]].astype(jnp.float32)
    summed = dot(attn_s[...].astype(jnp.bfloat16), w[...])
    out[...] = (resid[...].astype(jnp.float32) + gate[...] * summed).astype(jnp.bfloat16)


def project(heads, attn, w, resid, gate):
    out = jax.ShapeDtypeStruct(resid.shape, jnp.bfloat16)
    vmem = pl.BlockSpec(memory_space=pltpu.VMEM)
    specs = ([pl.BlockSpec(memory_space=pltpu.SMEM)] + [vmem] * 4, vmem)
    return call(
        project_kernel, (heads, attn, w, resid, gate), out, "project", (pltpu.VMEM(resid.shape, jnp.float32),),
        flops=150_000_000, moved=3_200_000, grid=(), specs=specs,
    )


def temporal_kernel(place, own, other, out):
    factor = HEAD_DIM ** (-0.5)
    half = own.shape[1]
    size = 2 * half * 8
    r_id = lax.broadcasted_iota(jnp.int32, (size, size), 0) % 8
    c_id = lax.broadcasted_iota(jnp.int32, (size, size), 1) % 8
    same = r_id == c_id

    for g in range(ROWS // 8):
        at = slice(8 * g, 8 * g + 8)

        def pick(i):
            return jnp.concatenate(
                [r[i, f, at].astype(jnp.float32) for r in (own, other) for f in range(half)], axis=0
            ).astype(jnp.bfloat16)

        scores = jnp.where(same, dot(pick(0), pick(1), NT), NEG)
        top = jnp.max(scores, axis=1, keepdims=True)
        expo = jnp.exp((scores - top) * factor)
        weights = (expo / jnp.sum(expo, axis=1, keepdims=True)).astype(jnp.bfloat16)
        mixed = dot(weights, pick(2)).astype(jnp.bfloat16)
        for f in range(2 * half):
            out[place[f], at] = mixed[8 * f : 8 * f + 8]


def temporal(place, own, other):
    shape = jax.ShapeDtypeStruct((2 * own.shape[1],) + own.shape[2:], jnp.bfloat16)
    vmem = pl.BlockSpec(memory_space=pltpu.VMEM)
    specs = ([pl.BlockSpec(memory_space=pltpu.SMEM), vmem, vmem], vmem)
    return call(
        temporal_kernel, (place, own, other), shape, "temporal", flops=50_000_000, moved=1_000_000,
        trans=120_000, grid=(), specs=specs,
    )


def flat(z, c, x, y, h):
    index = 0
    for value, size in zip((z, c, x, y, h), SIZES):
        index = index * size + value
    return index


def turn(z):
    return 2 * z + 8 * (z % 2)


def shifted():
    pairs = []
    for x in range(4):
        for y in range(4):
            q = 4 * x + y
            for ring in range(16):
                step = (((q + turn(ring % 8)) % 16) // 2 - ring % 8) % 8
                if step > 4 or (step == 4 and ring // 2 % 2):
                    step -= 8
                a, b = (ring + step) % 16, ring
                pairs.append((flat(a % 8, q % 2, x, y, a // 8), flat(b % 8, q % 2, x, y, b // 8)))
    return pairs


def rolled():
    return [
        [flat(z, c, q // 4, q % 4, h) for q in ((i - turn(z)) % PLANE for i in range(PLANE))]
        for z in range(8)
        for c in range(2)
        for h in range(2)
    ]


SWAP = [(0, 1), (1, 0)]


def plane_gather(block):
    def by(part, axis):
        return [part] + [
            lax.ppermute(part, axis, [(i, i ^ k) for i in range(4)]) for k in (1, 2, 3)
        ]

    return by(jnp.concatenate(by(block, "x"), axis=0), "y")


def line_gather(block):
    def to(part, k):
        return lax.ppermute(part, "z", [(z, z ^ k) for z in range(8)])

    far, *near = [to(block, k) for k in (4, 3, 2, 1)]
    return [block, *near[::-1], far] + [to(far, k) for k in (1, 2, 3)]


def together(steps, always, *args):
    shapes = jax.eval_shape(steps, *args)
    blank = lambda *_: jax.tree.map(lambda s: jnp.zeros(s.shape, s.dtype), shapes)
    return lax.cond(always, steps, blank, *args)


def local(stream, stale_keys, stale_values, modulation, w_qkv, w_out, qk_gain):
    width = stream.shape[2]
    x, y, z, c, h = [lax.axis_index(a) for a in ("x", "y", "z", "c", "h")]
    column = 4 * x + y
    mine = column % 2 == c
    blocks = jnp.arange(16, dtype=jnp.int32)

    main = jnp.concatenate([stale_keys, stale_values[:, :, :56]], axis=2)
    tail = stale_values[:, :, 56:].reshape(16, 7, 8, 16).transpose(0, 2, 1, 3).reshape(16, 8, 112)
    tail = jnp.pad(tail, ((0, 0), (0, 0), (0, 16)))
    chunk = jnp.concatenate([main, tail], axis=1)
    chunk = jnp.broadcast_to(chunk[:, None], (16, 2, 64, 128)).reshape(32, 64, 128)
    old = lax.all_to_all(chunk, ("z", "c", "h"), 0, 0, tiled=True)

    def gathered(first, rows):
        have = lax.ppermute(rows, AXES, shifted())
        return (*plane_gather(modulate(first, modulation[0])), have)

    rows = jnp.concatenate([w_qkv[0].reshape(3 * HEAD_DIM, width), w_out[0], w_out[1]], axis=0)
    toks = together(gathered, z >= 0, stream[0], rows)
    old, toks = lax.optimization_barrier((old, toks))
    old = lax.all_to_all(
        old.reshape(16, 2, 64, 128), AXES, 0, 0, axis_index_groups=rolled(), tiled=True
    )
    w_col = jnp.where(mine, toks[4], lax.ppermute(toks[4], "c", SWAP))
    w_last = lax.all_gather(w_col[4 * HEAD_DIM :], ("x", "y"), axis=0).reshape(width, width)
    w_own = w_qkv[1].reshape(3 * HEAD_DIM, width)
    order = 4 * (x ^ (blocks % 4)) + (y ^ (blocks // 4))
    fresh = qkv(toks[:4], w_col[: 3 * HEAD_DIM], qk_gain[0])
    rowp = jnp.repeat(2 * order + h, ROWS)[:, None]
    colp = jnp.repeat((lax.iota(jnp.int32, 2 * PLANE) - 2 * turn(z)) % (2 * PLANE), ROWS)[None, :]
    w_head = w_col[3 * HEAD_DIM : 4 * HEAD_DIM]
    part = spatial(order, fresh, old.reshape(2 * PLANE, 64, 128), rowp, colp, w_head)
    part = lax.all_to_all(part, ("x", "y"), 0, 0, tiled=True)
    middle, hmod = combine(part, stream[0], jnp.concatenate([modulation[0, 2:], modulation[1, :2]]))

    toks = [jnp.concatenate(line_gather(hmod), axis=0)]
    w_sib = lax.ppermute(w_own, "c", SWAP)
    sib = qkv(toks, w_sib, qk_gain[1])
    other = lax.ppermute(sib, "c", SWAP)
    own = qkv(toks, w_own, qk_gain[1])
    shape = (3, 8, ROWS, HEAD_DIM)
    place = 2 * (z ^ (blocks % 8)) + (c ^ (blocks // 8))
    attn = temporal(place, own.reshape(shape), other.reshape(shape))
    attn = lax.all_to_all(attn, ("z", "c"), 0, 0, tiled=True)
    out = project((blocks + turn(z)) % 16, attn, w_last, middle, modulation[1, 2:])
    return out[None]


def solution(mesh):
    wide = Mesh(mesh.devices.reshape(SIZES), AXES)
    tm, patch = ("z", "c"), ("x", "y", "h")
    placed = (
        P(tm, patch, None),
        P(None, patch, tm),
        P(None, patch, tm),
        P(),
        P(None, None, tm, None),
        P(None, tm, None),
        P(),
    )
    return jax.shard_map(
        local, mesh=wide, in_specs=placed, out_specs=P(tm, patch, None), check_vma=False
    )
```

time: 263 us -> 233 us (0.89)
  blocking collectives: 45.5 us -> 0 us
  starting transfers between devices: 83.4 us -> 108 us
  other arithmetic: 11.7 us -> 2.4 us
  local copies, waits for them, and re-layouts: 14.8 us -> 6.16 us
  Pallas kernels: 15.5 us -> 21.9 us
  waiting for transfers between devices: 74.7 us -> 79.4 us
  matrix products: 3.04 us -> 0 us
    ppermute x8 -> x15, starting transfers between devices: 15.2 us -> 62.7 us  [the longest x7 37 us: to(): return lax.ppermute(part, 'z', [(z, z ^ k) for z in range(8)])]
    all_gather x1 -> x0, blocking collectives: 45.5 us -> none  [local(): tok = lax.all_gather(hmod, 'z', axis=0).reshape(8 * ROWS, width)]
    ppermute x8 -> x15, waiting for transfers between devices: 0.94 us -> 35.4 us  [the longest x6 27.3 us: by(): lax.ppermute(part, axis, [(i, i ^ k) for i in range(4)])]
    all_to_all x3 -> x2, starting transfers between devices: 34.1 us -> 9.42 us  [the longest x1 5.05 us: local(): lax.all_to_all(old.reshape(16, 2, 64, 128), AXES, 0, 0, axis_index_groups...]
    all_to_all x1, waiting for transfers between devices: 19.7 us -> 0.01 us  [local(): old = lax.all_to_all(chunk, ('z', 'c', 'h'), 0, 0, tiled=True)]
    all_to_all x3 -> x2, waiting for transfers between devices: 37 us -> 28.2 us  [the longest x1 23.8 us: local(): part = lax.all_to_all(part, ('x', 'y'), 0, 0, tiled=True)]
    pallas_call x3 -> x8, Pallas kernels: 15.5 us -> 21.9 us  [call(): pl.pallas_call(kernel, out_shape=out_shape, scratch_shapes=list(scratch),...]
    all_to_all x1, starting transfers between devices: 3.69 us -> 9.79 us  [local(): attn = lax.all_to_all(attn, ('z', 'c'), 0, 0, tiled=True)]
  transfers between devices with their start and end apart: 16 -> 22, of which waited for: 7 -> 11; matrix products, arithmetic and copies ran while one was open for 8% -> 1% of each run, Pallas kernels for 6% -> 9%
where the time goes in v2:
time: 233 us; the launch traced here: 232 us
  starting transfers between devices  108 us (46%)
  waiting for transfers between devices  79.4 us (34%)
  Pallas kernels  21.9 us (9%)
  between operations  13.8 us (6%)
  local copies, waits for them, and re-layouts  6.16 us (3%)
  other arithmetic  2.4 us (1%)
    ppermute x7, starting transfers between devices, to(): return lax.ppermute(part, 'z', [(z, z ^ k) for z in range(8)])  37 us
    ppermute x6, waiting for transfers between devices, by(): lax.ppermute(part, axis, [(i, i ^ k) for i in range(4)])  27.3 us
    all_to_all x1, waiting for transfers between devices, local(): part = lax.all_to_all(part, ('x', 'y'), 0, 0, tiled=True)  23.8 us
    pallas_call x8, Pallas kernels, call(): pl.pallas_call(kernel, out_shape=out_shape, scratch_shapes=list(scratch),...  21.9 us
    ppermute x6, starting transfers between devices, by(): lax.ppermute(part, axis, [(i, i ^ k) for i in range(4)])  19.2 us
    all_to_all x1, starting transfers between devices, local(): old = lax.all_to_all(chunk, ('z', 'c', 'h'), 0, 0, tiled=True)  16.8 us
    all_to_all x1, waiting for transfers between devices, local(): attn = lax.all_to_all(attn, ('z', 'c'), 0, 0, tiled=True)  15.8 us
    all_to_all x1, starting transfers between devices, local(): attn = lax.all_to_all(attn, ('z', 'c'), 0, 0, tiled=True)  9.79 us
  transfers between devices with their start and end apart: 22, of which 11 were waited for; matrix products, arithmetic and copies ran while one was open for 1% of the time, Pallas kernels for 9%

profile of v2, /device:TPU:1, one launch (start us, length us, event | category | flops | bytes accessed | tf_op | source)
XLA Modules:
  0.0 232.0 jit_solution(810470209861449059)
XLA Ops:
  6.5 1.1 slice_bitcast_fusion.1
  7.9 1.3 fusion.1
  9.2 0.9 broadcast_in_dim.15
  10.1 16.8 %all-to-all-start = ((bf16[32,64,128]{2,1,0:T(8,128)(2,1)}), bf16[32,64,128]{2,1,0:T(8,128)(2,1)}, u32[]{:S(2)}, u32[]{:S(2)}) async-start(bf16[32,64,128]{2,1,0:T(8,128)(2,1)} %bitcast.3), calls=%async_computation | async-start | bytes 1048576 | tf_op jit(solution)/shard_map/all_to_all | solution.py:269
  27.1 0.7 copy-done.2
  27.9 49.3 %conditional.1 = (bf16[224,1152]{1,0:T(8,128)(2,1)}, bf16[224,1152]{1,0:T(8,128)(2,1)}, bf16[224,1152]{1,0:T(8,128)(2,1)}, bf16[224,1152]{1,0:T(8,128)(2,1)}, bf16[360,1152]{1,0:T(8,128)(2,1)}) conditional(s32[]{:T(128)} %convert_element_type.5, () %tuple.14, (f32[2,3,1152]{2,0,1:T(2,128)S(1)}, bf16[56,1152]{1,0:T(8,128)(2,1)S(1)}, ...), branch_computations={%region_0.1_spmd, %region_1.2_spmd} | conditional | flops 2064384 | bytes 12474656 | solution.py:254
  27.9 0.2 modulate.1
  28.1 3.1 %collective-permute-start = (bf16[56,1152]{1,0:T(8,128)(2,1)S(1)}, bf16[56,1152]{1,0:T(8,128)(2,1)S(1)}, u32[]{:S(2)}, u32[]{:S(2)}) collective-permute-start(bf16[56,1152]{1,0:T(8,128)(2,1)S(1)} %modulate.1), channel_id=1, source_target_pairs={{0,8},{8,0},{16,24},{24,16},{1,9},{9,1},{17,25},{25,17},{2,10},{10... | collective-permute-start | bytes 387080 | tf_op jit(solution)/shard_map/cond/branch_1_fun/ppermute | solution.py:237
  31.2 4.4 %collective-permute-start.1 = (bf16[56,1152]{1,0:T(8,128)(2,1)S(1)}, bf16[56,1152]{1,0:T(8,128)(2,1)S(1)}, u32[]{:S(2)}, u32[]{:S(2)}) collective-permute-start(bf16[56,1152]{1,0:T(8,128)(2,1)S(1)} %modulate.1), channel_id=1, source_target_pairs={{0,16},{8,24},{16,0},{24,8},{1,17},{9,25},{17,1},{25,9},{2,18},{10... | collective-permute-start | bytes 387080 | tf_op jit(solution)/shard_map/cond/branch_1_fun/ppermute | solution.py:237
  35.6 2.1 collective-permute-start.2
  37.7 1.6 collective-permute-start.6
  39.3 0.5 collective-permute-done.1
  39.8 3.1 %collective-permute-done.2 = bf16[56,1152]{1,0:T(8,128)(2,1)S(1)} collective-permute-done((bf16[56,1152]{1,0:T(8,128)(2,1)S(1)}, bf16[56,1152]{1,0:T(8,128)(2,1)S(1)}, u32[]{:S(2)}, u32[]{:S(2)}) %collective-permute-start.2) | collective-permute-done | bytes 129056 | tf_op jit(solution)/shard_map/cond/branch_1_fun/ppermute | solution.py:237
  42.9 0.8 pad_maximum_fusion
  43.8 3.2 %collective-permute-start.3 = (bf16[224,1152]{1,0:T(8,128)(2,1)}, bf16[224,1152]{1,0:T(8,128)(2,1)}, u32[]{:S(2)}, u32[]{:S(2)}) collective-permute-start(bf16[224,1152]{1,0:T(8,128)(2,1)} %pad_maximum_fusion), channel_id=1, source_target_pairs={{0,2},{2,0},{4,6},{6,4},{1,3},{3,1},{5,7},{7,5},{8,10},{10,8},{12,... | collective-permute-start | bytes 1548296 | tf_op jit(solution)/shard_map/cond/branch_1_fun/ppermute | solution.py:237
  47.0 4.5 %collective-permute-start.4 = (bf16[224,1152]{1,0:T(8,128)(2,1)}, bf16[224,1152]{1,0:T(8,128)(2,1)}, u32[]{:S(2)}, u32[]{:S(2)}) collective-permute-start(bf16[224,1152]{1,0:T(8,128)(2,1)} %pad_maximum_fusion), channel_id=1, source_target_pairs={{0,4},{2,6},{4,0},{6,2},{1,5},{3,7},{5,1},{7,3},{8,12},{10,14},{12... | collective-permute-start | bytes 1548296 | tf_op jit(solution)/shard_map/cond/branch_1_fun/ppermute | solution.py:237
  51.5 1.9 collective-permute-start.5
  53.4 4.1 %collective-permute-done.3 = bf16[224,1152]{1,0:T(8,128)(2,1)} collective-permute-done((bf16[224,1152]{1,0:T(8,128)(2,1)}, bf16[224,1152]{1,0:T(8,128)(2,1)}, u32[]{:S(2)}, u32[]{:S(2)}) %collective-permute-start.3) | collective-permute-done | bytes 516128 | tf_op jit(solution)/shard_map/cond/branch_1_fun/ppermute | solution.py:237
  57.5 13.6 %collective-permute-done.4 = bf16[224,1152]{1,0:T(8,128)(2,1)} collective-permute-done((bf16[224,1152]{1,0:T(8,128)(2,1)}, bf16[224,1152]{1,0:T(8,128)(2,1)}, u32[]{:S(2)}, u32[]{:S(2)}) %collective-permute-start.4) | collective-permute-done | bytes 516128 | tf_op jit(solution)/shard_map/cond/branch_1_fun/ppermute | solution.py:237
  71.1 6.1 %collective-permute-done.5 = bf16[224,1152]{1,0:T(8,128)(2,1)} collective-permute-done((bf16[224,1152]{1,0:T(8,128)(2,1)}, bf16[224,1152]{1,0:T(8,128)(2,1)}, u32[]{:S(2)}, u32[]{:S(2)}) %collective-permute-start.5) | collective-permute-done | bytes 516128 | tf_op jit(solution)/shard_map/cond/branch_1_fun/ppermute | solution.py:237
  77.2 4.9 %collective-permute-start.7 = (bf16[360,1152]{1,0:T(8,128)(2,1)}, bf16[360,1152]{1,0:T(8,128)(2,1)S(1)}, u32[]{:S(2)}, u32[]{:S(2)}) collective-permute-start(bf16[360,1152]{1,0:T(8,128)(2,1)} %get-tuple-element.36), channel_id=1, source_target_pairs={{0,32},{32,0},{1,33},{33,1},{2,34},{34,2},{3,35},{35,3},{4,36},{36... | collective-permute-start | bytes 2488328 | tf_op jit(solution)/shard_map/ppermute | solution.py:281
  82.1 5.0 %all-to-all-start.1 = ((bf16[16,2,64,128]{3,2,1,0:T(8,128)(2,1)}), bf16[16,2,64,128]{3,2,1,0:T(8,128)(2,1)S(1)}, u32[]{:S(2)}, u32[]{:S(2)}) async-start(bf16[16,2,64,128]{3,2,1,0:T(8,128)(2,1)} %bitcast.9), calls=%async_computation.1 | async-start | bytes 1048576 | tf_op jit(solution)/shard_map/all_to_all | solution.py:278
  87.4 0.7 fusion.13
  88.6 4.2 %qkv.3.q = bf16[3,896,72]{2,1,0:T(8,128)(2,1)S(1)} custom-call(bf16[224,1152]{1,0:T(8,128)(2,1)} %get-tuple-element.32.refs_0_, bf16[224,1152]{1,0:T(8,128)(2,1)} %get-tuple-element.33.refs_1_, bf16[224,1152]{1,0:T(8,128)(2,1)} %get-tuple-element.34.refs_2_, bf16[224,1152]{1,0:T(8,128)(2,1)} %get-tuple-element.35.refs_3_, ...), custom_call_target="tpu_custom_call" | custom-call | flops 445906944 | bytes 3000000 | tf_op jit(solution)/shard_map/qkv/pallas_call | solution.py:41
  92.8 4.5 %all-to-all-done.1 = bf16[16,2,64,128]{3,2,1,0:T(8,128)(2,1)S(1)} async-done(((bf16[16,2,64,128]{3,2,1,0:T(8,128)(2,1)}), bf16[16,2,64,128]{3,2,1,0:T(8,128)(2,1)S(1)}, u32[]{:S(2)}, u32[]{:S(2)}) %all-to-all-start.1) | async-done | bytes 524320 | tf_op jit(solution)/shard_map/all_to_all | solution.py:278
  97.3 7.7 %spatial.1 = bf16[16,56,1152]{2,1,0:T(8,128)(2,1)} custom-call(s32[16]{0:T(128)S(1)} %get-tuple-element.47.order, bf16[3,896,72]{2,1,0:T(8,128)(2,1)S(1)} %qkv.3.q, bf16[32,64,128]{2,1,0:T(8,128)(2,1)S(1)} %bitcast.32, s32[896,1]{1,0:T(8,128)S(1)} %broadcast_in_dim_reshape.8.rowp, s32[1,1792]{1,0:T(1,128)S(1)} %broadcast_in_dim_reshape.7.colp, ...), custom_call_target="tpu_custom_call" | custom-call | flops 600000000 | bytes 2000000 | tf_op jit(solution)/shard_map/spatial/pallas_call | solution.py:41
  105.0 4.4 %all-to-all-start.2 = ((bf16[16,56,1152]{2,1,0:T(8,128)(2,1)}), bf16[16,56,1152]{2,1,0:T(8,128)(2,1)S(1)}, u32[]{:S(2)}, u32[]{:S(2)}) async-start(bf16[16,56,1152]{2,1,0:T(8,128)(2,1)} %spatial.1), calls=%async_computation.2 | async-start | bytes 4128768 | tf_op jit(solution)/shard_map/all_to_all | solution.py:290
  109.4 3.6 %collective-permute-start.15 = (bf16[216,1152]{1,0:T(8,128)(2,1)S(1)}, bf16[216,1152]{1,0:T(8,128)(2,1)S(1)}, u32[]{:S(2)}, u32[]{:S(2)}) collective-permute-start(bf16[216,1152]{1,0:T(8,128)(2,1)S(1)} %bitcast.33), channel_id=1, source_target_pairs={{0,32},{32,0},{1,33},{33,1},{2,34},{34,2},{3,35},{35,3},{4,36},{36... | collective-permute-start | bytes 1493000 | tf_op jit(solution)/shard_map/ppermute | solution.py:294
  113.0 23.8 %all-to-all-done.2.part = bf16[16,56,1152]{2,1,0:T(8,128)(2,1)S(1)} async-done(((bf16[16,56,1152]{2,1,0:T(8,128)(2,1)}), bf16[16,56,1152]{2,1,0:T(8,128)(2,1)S(1)}, u32[]{:S(2)}, u32[]{:S(2)}) %all-to-all-start.2) | async-done | bytes 2064416 | tf_op jit(solution)/shard_map/all_to_all | solution.py:290
  136.8 0.5 combine.1
  137.3 3.4 %collective-permute-start.8 = (bf16[56,1152]{1,0:T(8,128)(2,1)S(1)}, bf16[56,1152]{1,0:T(8,128)(2,1)S(1)}, u32[]{:S(2)}, u32[]{:S(2)}) collective-permute-start(bf16[56,1152]{1,0:T(8,128)(2,1)S(1)} %get-tuple-element.38), channel_id=1, source_target_pairs={{0,64},{64,0},{128,192},{192,128},{256,320},{320,256},{384,448},{4... | collective-permute-start | bytes 387080 | tf_op jit(solution)/shard_map/ppermute | solution.py:245
  140.7 5.9 %collective-permute-start.9 = (bf16[56,1152]{1,0:T(8,128)(2,1)S(1)}, bf16[56,1152]{1,0:T(8,128)(2,1)S(1)}, u32[]{:S(2)}, u32[]{:S(2)}) collective-permute-start(bf16[56,1152]{1,0:T(8,128)(2,1)S(1)} %get-tuple-element.38), channel_id=1, source_target_pairs={{0,128},{64,192},{128,0},{192,64},{256,384},{320,448},{384,256},{4... | collective-permute-start | bytes 387080 | tf_op jit(solution)/shard_map/ppermute | solution.py:245
  146.7 3.1 %collective-permute-start.10 = (bf16[56,1152]{1,0:T(8,128)(2,1)S(1)}, bf16[56,1152]{1,0:T(8,128)(2,1)S(1)}, u32[]{:S(2)}, u32[]{:S(2)}) collective-permute-start(bf16[56,1152]{1,0:T(8,128)(2,1)S(1)} %get-tuple-element.38), channel_id=1, source_target_pairs={{0,192},{64,128},{128,64},{192,0},{256,448},{320,384},{384,320},{4... | collective-permute-start | bytes 387080 | tf_op jit(solution)/shard_map/ppermute | solution.py:245
  149.8 7.7 %collective-permute-start.11 = (bf16[56,1152]{1,0:T(8,128)(2,1)S(1)}, bf16[56,1152]{1,0:T(8,128)(2,1)S(1)}, u32[]{:S(2)}, u32[]{:S(2)}) collective-permute-start(bf16[56,1152]{1,0:T(8,128)(2,1)S(1)} %get-tuple-element.38), channel_id=1, source_target_pairs={{0,256},{64,320},{128,384},{192,448},{256,0},{320,64},{384,128},{4... | collective-permute-start | bytes 387080 | tf_op jit(solution)/shard_map/ppermute | solution.py:245
  157.5 2.6 %collective-permute-done.11 = bf16[56,1152]{1,0:T(8,128)(2,1)S(1)} collective-permute-done((bf16[56,1152]{1,0:T(8,128)(2,1)S(1)}, bf16[56,1152]{1,0:T(8,128)(2,1)S(1)}, u32[]{:S(2)}, u32[]{:S(2)}) %collective-permute-start.11) | collective-permute-done | bytes 129056 | tf_op jit(solution)/shard_map/ppermute | solution.py:245
  160.1 10.9 %collective-permute-start.12 = (bf16[56,1152]{1,0:T(8,128)(2,1)S(1)}, bf16[56,1152]{1,0:T(8,128)(2,1)S(1)}, u32[]{:S(2)}, u32[]{:S(2)}) collective-permute-start(bf16[56,1152]{1,0:T(8,128)(2,1)S(1)} %collective-permute-done.11), channel_id=1, source_target_pairs={{0,64},{64,0},{128,192},{192,128},{256,320},{320,256},{384,448},{4... | collective-permute-start | bytes 387080 | tf_op jit(solution)/shard_map/ppermute | solution.py:245
  171.0 3.9 %collective-permute-start.13 = (bf16[56,1152]{1,0:T(8,128)(2,1)S(1)}, bf16[56,1152]{1,0:T(8,128)(2,1)S(1)}, u32[]{:S(2)}, u32[]{:S(2)}) collective-permute-start(bf16[56,1152]{1,0:T(8,128)(2,1)S(1)} %collective-permute-done.11), channel_id=1, source_target_pairs={{0,128},{64,192},{128,0},{192,64},{256,384},{320,448},{384,256},{4... | collective-permute-start | bytes 387080 | tf_op jit(solution)/shard_map/ppermute | solution.py:245
  175.0 2.0 collective-permute-start.14
  177.1 1.7 collective-permute-done.13
  178.9 3.7 %collective-permute-done.14 = bf16[56,1152]{1,0:T(8,128)(2,1)S(1)} collective-permute-done((bf16[56,1152]{1,0:T(8,128)(2,1)S(1)}, bf16[56,1152]{1,0:T(8,128)(2,1)S(1)}, u32[]{:S(2)}, u32[]{:S(2)}) %collective-permute-start.14) | collective-permute-done | bytes 129056 | tf_op jit(solution)/shard_map/ppermute | solution.py:245
  182.6 1.9 qkv.5
  184.5 5.9 %collective-permute-start.16 = (bf16[3,448,72]{2,1,0:T(8,128)(2,1)S(1)}, bf16[3,448,72]{2,1,0:T(8,128)(2,1)S(1)}, u32[]{:S(2)}, u32[]{:S(2)}) collective-permute-start(bf16[3,448,72]{2,1,0:T(8,128)(2,1)S(1)} %qkv.5), channel_id=1, source_target_pairs={{0,32},{32,0},{1,33},{33,1},{2,34},{34,2},{3,35},{35,3},{4,36},{36... | collective-permute-start | bytes 580616 | tf_op jit(solution)/shard_map/ppermute | solution.py:296
  190.4 1.9 qkv.4
  192.3 3.6 %temporal.1 = bf16[16,56,72]{2,1,0:T(8,128)(2,1)} custom-call(s32[16]{0:T(128)S(1)} %fusion.4.place, bf16[3,8,56,72]{3,2,1,0:T(8,128)(2,1)S(1)} %bitcast.35, bf16[3,8,56,72]{3,2,1,0:T(8,128)(2,1)S(1)} %bitcast.36), custom_call_target="tpu_custom_call" | custom-call | flops 50000000 | bytes 1000000 | tf_op jit(solution)/shard_map/temporal/pallas_call | solution.py:41
  195.9 9.8 %all-to-all-start.3 = ((bf16[16,56,72]{2,1,0:T(8,128)(2,1)}), bf16[16,56,72]{2,1,0:T(8,128)(2,1)S(1)}, u32[]{:S(2)}, u32[]{:S(2)}) async-start(bf16[16,56,72]{2,1,0:T(8,128)(2,1)} %temporal.1), calls=%async_computation.3 | async-start | bytes 458752 | tf_op jit(solution)/shard_map/all_to_all | solution.py:301
  205.7 15.8 %all-to-all-done.3.attn = bf16[16,56,72]{2,1,0:T(8,128)(2,1)S(1)} async-done(((bf16[16,56,72]{2,1,0:T(8,128)(2,1)}), bf16[16,56,72]{2,1,0:T(8,128)(2,1)S(1)}, u32[]{:S(2)}, u32[]{:S(2)}) %all-to-all-start.3) | async-done | bytes 129056 | tf_op jit(solution)/shard_map/all_to_all | solution.py:301
  221.5 1.7 copy-done
  223.3 1.8 project.1
  (53 shorter events, 1.4 us)
Async XLA Ops:
  7.6 19.3 %copy-start.3 = (bf16[2,72,1152]{2,1,0:T(8,128)(2,1)S(1)}, bf16[2,72,1152]{2,1,0:T(8,128)(2,1)}, u32[]{:S(2)}) copy-start(bf16[2,72,1152]{2,1,0:T(8,128)(2,1)} %param.14) | copy-start | bytes 995332
  7.9 19.1 %copy-start.1 = (bf16[2,3,72,1152]{3,2,1,0:T(8,128)(2,1)S(1)}, bf16[2,3,72,1152]{3,2,1,0:T(8,128)(2,1)}, u32[]{:S(2)}) copy-start(bf16[2,3,72,1152]{3,2,1,0:T(8,128)(2,1)} %param.13) | copy-start | bytes 2985988
  10.1 67.1 %all-to-all-start = ((bf16[32,64,128]{2,1,0:T(8,128)(2,1)}), bf16[32,64,128]{2,1,0:T(8,128)(2,1)}, u32[]{:S(2)}, u32[]{:S(2)}) async-start(bf16[32,64,128]{2,1,0:T(8,128)(2,1)} %bitcast.3), calls=%async_computation | async-start | bytes 1048576 | tf_op jit(solution)/shard_map/all_to_all | solution.py:269
  27.0 0.9 copy-start.2
  27.0 0.9 copy-start.4
  28.1 11.2 %collective-permute-start = (bf16[56,1152]{1,0:T(8,128)(2,1)S(1)}, bf16[56,1152]{1,0:T(8,128)(2,1)S(1)}, u32[]{:S(2)}, u32[]{:S(2)}) collective-permute-start(bf16[56,1152]{1,0:T(8,128)(2,1)S(1)} %modulate.1), channel_id=1, source_target_pairs={{0,8},{8,0},{16,24},{24,16},{1,9},{9,1},{17,25},{25,17},{2,10},{10... | collective-permute-start | bytes 387080 | tf_op jit(solution)/shard_map/cond/branch_1_fun/ppermute | solution.py:237
  31.2 8.6 %collective-permute-start.1 = (bf16[56,1152]{1,0:T(8,128)(2,1)S(1)}, bf16[56,1152]{1,0:T(8,128)(2,1)S(1)}, u32[]{:S(2)}, u32[]{:S(2)}) collective-permute-start(bf16[56,1152]{1,0:T(8,128)(2,1)S(1)} %modulate.1), channel_id=1, source_target_pairs={{0,16},{8,24},{16,0},{24,8},{1,17},{9,25},{17,1},{25,9},{2,18},{10... | collective-permute-start | bytes 387080 | tf_op jit(solution)/shard_map/cond/branch_1_fun/ppermute | solution.py:237
  35.6 7.3 %collective-permute-start.2 = (bf16[56,1152]{1,0:T(8,128)(2,1)S(1)}, bf16[56,1152]{1,0:T(8,128)(2,1)S(1)}, u32[]{:S(2)}, u32[]{:S(2)}) collective-permute-start(bf16[56,1152]{1,0:T(8,128)(2,1)S(1)} %modulate.1), channel_id=1, source_target_pairs={{0,24},{8,16},{16,8},{24,0},{1,25},{9,17},{17,9},{25,1},{2,26},{10... | collective-permute-start | bytes 387080 | tf_op jit(solution)/shard_map/cond/branch_1_fun/ppermute | solution.py:237
  37.7 39.4 %collective-permute-start.6 = (bf16[360,1152]{1,0:T(8,128)(2,1)S(1)}, bf16[360,1152]{1,0:T(8,128)(2,1)}, u32[]{:S(2)}, u32[]{:S(2)}) collective-permute-start(bf16[360,1152]{1,0:T(8,128)(2,1)S(1)} %get-tuple-element.13), channel_id=1, source_target_pairs={{0,0},{320,64},{128,128},{449,192},{256,256},{65,320},{384,384},{1... | collective-permute-start | bytes 2488328 | tf_op jit(solution)/shard_map/cond/branch_1_fun/ppermute | solution.py:272
  43.8 13.8 %collective-permute-start.3 = (bf16[224,1152]{1,0:T(8,128)(2,1)}, bf16[224,1152]{1,0:T(8,128)(2,1)}, u32[]{:S(2)}, u32[]{:S(2)}) collective-permute-start(bf16[224,1152]{1,0:T(8,128)(2,1)} %pad_maximum_fusion), channel_id=1, source_target_pairs={{0,2},{2,0},{4,6},{6,4},{1,3},{3,1},{5,7},{7,5},{8,10},{10,8},{12,... | collective-permute-start | bytes 1548296 | tf_op jit(solution)/shard_map/cond/branch_1_fun/ppermute | solution.py:237
  47.0 24.1 %collective-permute-start.4 = (bf16[224,1152]{1,0:T(8,128)(2,1)}, bf16[224,1152]{1,0:T(8,128)(2,1)}, u32[]{:S(2)}, u32[]{:S(2)}) collective-permute-start(bf16[224,1152]{1,0:T(8,128)(2,1)} %pad_maximum_fusion), channel_id=1, source_target_pairs={{0,4},{2,6},{4,0},{6,2},{1,5},{3,7},{5,1},{7,3},{8,12},{10,14},{12... | collective-permute-start | bytes 1548296 | tf_op jit(solution)/shard_map/cond/branch_1_fun/ppermute | solution.py:237
  51.5 25.7 %collective-permute-start.5 = (bf16[224,1152]{1,0:T(8,128)(2,1)}, bf16[224,1152]{1,0:T(8,128)(2,1)}, u32[]{:S(2)}, u32[]{:S(2)}) collective-permute-start(bf16[224,1152]{1,0:T(8,128)(2,1)} %pad_maximum_fusion), channel_id=1, source_target_pairs={{0,6},{2,4},{4,2},{6,0},{1,7},{3,5},{5,3},{7,1},{8,14},{10,12},{12... | collective-permute-start | bytes 1548296 | tf_op jit(solution)/shard_map/cond/branch_1_fun/ppermute | solution.py:237
  77.2 10.0 %collective-permute-start.7 = (bf16[360,1152]{1,0:T(8,128)(2,1)}, bf16[360,1152]{1,0:T(8,128)(2,1)S(1)}, u32[]{:S(2)}, u32[]{:S(2)}) collective-permute-start(bf16[360,1152]{1,0:T(8,128)(2,1)} %get-tuple-element.36), channel_id=1, source_target_pairs={{0,32},{32,0},{1,33},{33,1},{2,34},{34,2},{3,35},{35,3},{4,36},{36... | collective-permute-start | bytes 2488328 | tf_op jit(solution)/shard_map/ppermute | solution.py:281
  82.1 15.2 %all-to-all-start.1 = ((bf16[16,2,64,128]{3,2,1,0:T(8,128)(2,1)}), bf16[16,2,64,128]{3,2,1,0:T(8,128)(2,1)S(1)}, u32[]{:S(2)}, u32[]{:S(2)}) async-start(bf16[16,2,64,128]{3,2,1,0:T(8,128)(2,1)} %bitcast.9), calls=%async_computation.1 | async-start | bytes 1048576 | tf_op jit(solution)/shard_map/all_to_all | solution.py:278
  87.1 1.4 copy-start.5
  87.1 134.4 %all-gather.3.cloned.1.call-start = ((), (), s32[]{:S(2)}) async-start(), calls=%async_computation.4 | async-start | bytes 2820096 | tf_op jit(solution)/shard_map/all_gather | solution.py:282
  105.0 31.8 %all-to-all-start.2 = ((bf16[16,56,1152]{2,1,0:T(8,128)(2,1)}), bf16[16,56,1152]{2,1,0:T(8,128)(2,1)S(1)}, u32[]{:S(2)}, u32[]{:S(2)}) async-start(bf16[16,56,1152]{2,1,0:T(8,128)(2,1)} %spatial.1), calls=%async_computation.2 | async-start | bytes 4128768 | tf_op jit(solution)/shard_map/all_to_all | solution.py:290
  109.4 73.2 %collective-permute-start.15 = (bf16[216,1152]{1,0:T(8,128)(2,1)S(1)}, bf16[216,1152]{1,0:T(8,128)(2,1)S(1)}, u32[]{:S(2)}, u32[]{:S(2)}) collective-permute-start(bf16[216,1152]{1,0:T(8,128)(2,1)S(1)} %bitcast.33), channel_id=1, source_target_pairs={{0,32},{32,0},{1,33},{33,1},{2,34},{34,2},{3,35},{35,3},{4,36},{36... | collective-permute-start | bytes 1493000 | tf_op jit(solution)/shard_map/ppermute | solution.py:294
  137.3 33.8 %collective-permute-start.8 = (bf16[56,1152]{1,0:T(8,128)(2,1)S(1)}, bf16[56,1152]{1,0:T(8,128)(2,1)S(1)}, u32[]{:S(2)}, u32[]{:S(2)}) collective-permute-start(bf16[56,1152]{1,0:T(8,128)(2,1)S(1)} %get-tuple-element.38), channel_id=1, source_target_pairs={{0,64},{64,0},{128,192},{192,128},{256,320},{320,256},{384,448},{4... | collective-permute-start | bytes 387080 | tf_op jit(solution)/shard_map/ppermute | solution.py:245
  140.7 34.3 %collective-permute-start.9 = (bf16[56,1152]{1,0:T(8,128)(2,1)S(1)}, bf16[56,1152]{1,0:T(8,128)(2,1)S(1)}, u32[]{:S(2)}, u32[]{:S(2)}) collective-permute-start(bf16[56,1152]{1,0:T(8,128)(2,1)S(1)} %get-tuple-element.38), channel_id=1, source_target_pairs={{0,128},{64,192},{128,0},{192,64},{256,384},{320,448},{384,256},{4... | collective-permute-start | bytes 387080 | tf_op jit(solution)/shard_map/ppermute | solution.py:245
  146.7 30.4 %collective-permute-start.10 = (bf16[56,1152]{1,0:T(8,128)(2,1)S(1)}, bf16[56,1152]{1,0:T(8,128)(2,1)S(1)}, u32[]{:S(2)}, u32[]{:S(2)}) collective-permute-start(bf16[56,1152]{1,0:T(8,128)(2,1)S(1)} %get-tuple-element.38), channel_id=1, source_target_pairs={{0,192},{64,128},{128,64},{192,0},{256,448},{320,384},{384,320},{4... | collective-permute-start | bytes 387080 | tf_op jit(solution)/shard_map/ppermute | solution.py:245
  149.8 10.3 %collective-permute-start.11 = (bf16[56,1152]{1,0:T(8,128)(2,1)S(1)}, bf16[56,1152]{1,0:T(8,128)(2,1)S(1)}, u32[]{:S(2)}, u32[]{:S(2)}) collective-permute-start(bf16[56,1152]{1,0:T(8,128)(2,1)S(1)} %get-tuple-element.38), channel_id=1, source_target_pairs={{0,256},{64,320},{128,384},{192,448},{256,0},{320,64},{384,128},{4... | collective-permute-start | bytes 387080 | tf_op jit(solution)/shard_map/ppermute | solution.py:245
  160.1 17.0 %collective-permute-start.12 = (bf16[56,1152]{1,0:T(8,128)(2,1)S(1)}, bf16[56,1152]{1,0:T(8,128)(2,1)S(1)}, u32[]{:S(2)}, u32[]{:S(2)}) collective-permute-start(bf16[56,1152]{1,0:T(8,128)(2,1)S(1)} %collective-permute-done.11), channel_id=1, source_target_pairs={{0,64},{64,0},{128,192},{192,128},{256,320},{320,256},{384,448},{4... | collective-permute-start | bytes 387080 | tf_op jit(solution)/shard_map/ppermute | solution.py:245
  171.0 7.8 %collective-permute-start.13 = (bf16[56,1152]{1,0:T(8,128)(2,1)S(1)}, bf16[56,1152]{1,0:T(8,128)(2,1)S(1)}, u32[]{:S(2)}, u32[]{:S(2)}) collective-permute-start(bf16[56,1152]{1,0:T(8,128)(2,1)S(1)} %collective-permute-done.11), channel_id=1, source_target_pairs={{0,128},{64,192},{128,0},{192,64},{256,384},{320,448},{384,256},{4... | collective-permute-start | bytes 387080 | tf_op jit(solution)/shard_map/ppermute | solution.py:245
  175.0 7.6 %collective-permute-start.14 = (bf16[56,1152]{1,0:T(8,128)(2,1)S(1)}, bf16[56,1152]{1,0:T(8,128)(2,1)S(1)}, u32[]{:S(2)}, u32[]{:S(2)}) collective-permute-start(bf16[56,1152]{1,0:T(8,128)(2,1)S(1)} %collective-permute-done.11), channel_id=1, source_target_pairs={{0,192},{64,128},{128,64},{192,0},{256,448},{320,384},{384,320},{4... | collective-permute-start | bytes 387080 | tf_op jit(solution)/shard_map/ppermute | solution.py:245
  184.5 7.8 %collective-permute-start.16 = (bf16[3,448,72]{2,1,0:T(8,128)(2,1)S(1)}, bf16[3,448,72]{2,1,0:T(8,128)(2,1)S(1)}, u32[]{:S(2)}, u32[]{:S(2)}) collective-permute-start(bf16[3,448,72]{2,1,0:T(8,128)(2,1)S(1)} %qkv.5), channel_id=1, source_target_pairs={{0,32},{32,0},{1,33},{33,1},{2,34},{34,2},{3,35},{35,3},{4,36},{36... | collective-permute-start | bytes 580616 | tf_op jit(solution)/shard_map/ppermute | solution.py:296
  195.9 25.6 %all-to-all-start.3 = ((bf16[16,56,72]{2,1,0:T(8,128)(2,1)}), bf16[16,56,72]{2,1,0:T(8,128)(2,1)S(1)}, u32[]{:S(2)}, u32[]{:S(2)}) async-start(bf16[16,56,72]{2,1,0:T(8,128)(2,1)} %temporal.1), calls=%async_computation.3 | async-start | bytes 458752 | tf_op jit(solution)/shard_map/all_to_all | solution.py:301
  221.5 1.8 copy-start
Sparse Core Ops, SparseCore 0:
  91.1 79.8 all-gather.2

commit v3 on v2

--- a/solution.py
+++ b/solution.py
@@ -58,11 +58,10 @@
     return call(modulate_kernel, (x, mod), shape, "modulate", moved=300_000)
 
 
-def qkv_kernel(*refs):
-    toks, (w, gain, out) = refs[:-3], refs[-3:]
-    rows = toks[0].shape[0]
-    for i, tok in enumerate(toks):
-        raw = dot(tok[...], w[...], NT)
+def qkv_kernel(toks, w, gain, out):
+    rows = toks.shape[1]
+    for i in range(toks.shape[0]):
+        raw = dot(toks[i], w[...], NT)
         at = slice(i * rows, (i + 1) * rows)
         out[0, at] = head_norm(raw[:, :HEAD_DIM], gain[0:1])
         out[1, at] = head_norm(raw[:, HEAD_DIM : 2 * HEAD_DIM], gain[1:2])
@@ -70,13 +69,13 @@
 
 
 def qkv(toks, w, gain):
-    rows = sum(t.shape[0] for t in toks)
+    rows = toks.shape[0] * toks.shape[1]
     shape = jax.ShapeDtypeStruct((3, rows, HEAD_DIM), jnp.bfloat16)
     flops = 2 * rows * w.shape[0] * w.shape[1]
-    return call(qkv_kernel, (*toks, w, gain), shape, "qkv", flops=flops, moved=3_000_000)
-
-
-def spatial_kernel(order, q, old, rowp, colp, w, out, vals_s, old_s, part_s):
+    return call(qkv_kernel, (toks, w, gain), shape, "qkv", flops=flops, moved=3_000_000)
+
+
+def spatial_kernel(q, old, rowp, colp, out, vals_s, old_s, attn_s):
     step = pl.program_id(0)
     factor = HEAD_DIM ** (-0.5)
 
@@ -102,30 +101,40 @@
     e_near = jnp.exp((near - top) * factor)
     total = jnp.sum(e_far, axis=1, keepdims=True) + jnp.sum(e_near, axis=1, keepdims=True)
     mixed = dot(e_far.astype(jnp.bfloat16), old_values) + dot(e_near.astype(jnp.bfloat16), value)
-    part_s[...] = dot((mixed / total).astype(jnp.bfloat16), w[...])
-    for j in range(QBLOCK // ROWS):
-        piece = part_s[j * ROWS : (j + 1) * ROWS].astype(jnp.bfloat16)
-        out[order[step * (QBLOCK // ROWS) + j]] = piece
-
-
-def spatial(order, q, old, rowp, colp, w):
+    attn_s[...] = mixed / total
+    for j in range(4):
+        out[j, step] = attn_s[j * ROWS : (j + 1) * ROWS].astype(jnp.bfloat16)
+
+
+def spatial(q, old, rowp, colp):
     rows = q.shape[1]
-    whole = lambda a: pl.BlockSpec(a.shape, lambda i: (0,) * a.ndim)
-    out = jax.ShapeDtypeStruct((PLANE, ROWS, w.shape[1]), jnp.bfloat16)
-    args = (q, old, rowp, colp, w)
+    whole = lambda a: pl.BlockSpec(a.shape, lambda i: (0,) * len(a.shape))
+    out = jax.ShapeDtypeStruct((4, 4, ROWS, HEAD_DIM), jnp.bfloat16)
+    args = (q, old, rowp, colp)
     specs = (
-        [pl.BlockSpec(memory_space=pltpu.SMEM)] + [whole(a) for a in args],
-        pl.BlockSpec(out.shape, lambda i: (0, 0, 0)),
+        [whole(a) for a in args],
+        whole(out),
     )
     scratch = (
         pltpu.VMEM((2 * PLANE, ROWS, HEAD_DIM), jnp.float32),
         pltpu.VMEM((2 * PLANE * ROWS, HEAD_DIM), jnp.bfloat16),
-        pltpu.VMEM((QBLOCK, w.shape[1]), jnp.float32),
+        pltpu.VMEM((QBLOCK, HEAD_DIM), jnp.float32),
     )
     return call(
-        spatial_kernel, (order, *args), out, "spatial", scratch, flops=600_000_000, moved=2_000_000,
+        spatial_kernel, args, out, "spatial", scratch, flops=600_000_000, moved=2_000_000,
         trans=1_800_000, grid=(rows // QBLOCK,), specs=specs,
     )
+
+
+def heads_out_kernel(attn, w, out):
+    for i in range(4):
+        total = sum(dot(attn[k, i * ROWS : (i + 1) * ROWS], w[k]) for k in range(4))
+        out[i] = total.astype(jnp.bfloat16)
+
+
+def heads_out(attn, w):
+    out = jax.ShapeDtypeStruct((4, ROWS, w.shape[2]), jnp.bfloat16)
+    return call(heads_out_kernel, (attn, w), out, "heads_out", flops=150_000_000, moved=1_200_000)
 
 
 def combine_kernel(part, resid, mod, middle, hmod):
@@ -231,13 +240,8 @@
 SWAP = [(0, 1), (1, 0)]
 
 
-def plane_gather(block):
-    def by(part, axis):
-        return [part] + [
-            lax.ppermute(part, axis, [(i, i ^ k) for i in range(4)]) for k in (1, 2, 3)
-        ]
-
-    return by(jnp.concatenate(by(block, "x"), axis=0), "y")
+def xor_gather(block, axis):
+    return [block] + [lax.ppermute(block, axis, [(i, i ^ k) for i in range(4)]) for k in (1, 2, 3)]
 
 
 def line_gather(block):
@@ -245,21 +249,17 @@
         return lax.ppermute(part, "z", [(z, z ^ k) for z in range(8)])
 
     far, *near = [to(block, k) for k in (4, 3, 2, 1)]
-    return [block, *near[::-1], far] + [to(far, k) for k in (1, 2, 3)]
-
-
-def together(steps, always, *args):
-    shapes = jax.eval_shape(steps, *args)
-    blank = lambda *_: jax.tree.map(lambda s: jnp.zeros(s.shape, s.dtype), shapes)
-    return lax.cond(always, steps, blank, *args)
+    return lax.optimization_barrier([block, *near[::-1], far] + [to(far, k) for k in (1, 2, 3)])
 
 
 def local(stream, stale_keys, stale_values, modulation, w_qkv, w_out, qk_gain):
     width = stream.shape[2]
     x, y, z, c, h = [lax.axis_index(a) for a in ("x", "y", "z", "c", "h")]
-    column = 4 * x + y
-    mine = column % 2 == c
+    mine = y % 2 == c
     blocks = jnp.arange(16, dtype=jnp.int32)
+
+    hmod = modulate(stream[0], modulation[0])
+    toks = lax.all_gather(hmod, ("x", "y"), axis=0).reshape(4, QBLOCK, width)
 
     main = jnp.concatenate([stale_keys, stale_values[:, :, :56]], axis=2)
     tail = stale_values[:, :, 56:].reshape(16, 7, 8, 16).transpose(0, 2, 1, 3).reshape(16, 8, 112)
@@ -268,35 +268,39 @@
     chunk = jnp.broadcast_to(chunk[:, None], (16, 2, 64, 128)).reshape(32, 64, 128)
     old = lax.all_to_all(chunk, ("z", "c", "h"), 0, 0, tiled=True)
 
-    def gathered(first, rows):
-        have = lax.ppermute(rows, AXES, shifted())
-        return (*plane_gather(modulate(first, modulation[0])), have)
-
     rows = jnp.concatenate([w_qkv[0].reshape(3 * HEAD_DIM, width), w_out[0], w_out[1]], axis=0)
-    toks = together(gathered, z >= 0, stream[0], rows)
-    old, toks = lax.optimization_barrier((old, toks))
+    rows = lax.ppermute(rows, AXES, shifted())
+    rows = jnp.where(mine, rows, lax.ppermute(rows, "c", SWAP))
+    w_col, w_head, w_last = (
+        rows[: 3 * HEAD_DIM], rows[3 * HEAD_DIM : 4 * HEAD_DIM], rows[4 * HEAD_DIM :]
+    )
+    w_heads = lax.all_gather(w_head, "y", axis=0)
     old = lax.all_to_all(
         old.reshape(16, 2, 64, 128), AXES, 0, 0, axis_index_groups=rolled(), tiled=True
     )
-    w_col = jnp.where(mine, toks[4], lax.ppermute(toks[4], "c", SWAP))
-    w_last = lax.all_gather(w_col[4 * HEAD_DIM :], ("x", "y"), axis=0).reshape(width, width)
-    w_own = w_qkv[1].reshape(3 * HEAD_DIM, width)
-    order = 4 * (x ^ (blocks % 4)) + (y ^ (blocks // 4))
-    fresh = qkv(toks[:4], w_col[: 3 * HEAD_DIM], qk_gain[0])
-    rowp = jnp.repeat(2 * order + h, ROWS)[:, None]
+
+    fresh = qkv(toks, w_col, qk_gain[0])
+    rowp = jnp.repeat(2 * blocks + h, ROWS)[:, None]
     colp = jnp.repeat((lax.iota(jnp.int32, 2 * PLANE) - 2 * turn(z)) % (2 * PLANE), ROWS)[None, :]
-    w_head = w_col[3 * HEAD_DIM : 4 * HEAD_DIM]
-    part = spatial(order, fresh, old.reshape(2 * PLANE, 64, 128), rowp, colp, w_head)
-    part = lax.all_to_all(part, ("x", "y"), 0, 0, tiled=True)
+    old, w_heads = lax.optimization_barrier((old, w_heads))
+    attn = spatial(fresh, old.reshape(2 * PLANE, 64, 128), rowp, colp)
+    attn, w_last, w_own = lax.optimization_barrier(
+        (attn, w_last, w_qkv[1].reshape(3 * HEAD_DIM, width))
+    )
+    w_last = lax.all_gather(w_last, ("x", "y"), axis=0).reshape(width, width)
+    attn = lax.all_to_all(attn, "y", 0, 0, tiled=True)
+    part = heads_out(attn.reshape(4, QBLOCK, HEAD_DIM), w_heads)
+    part = lax.all_to_all(part, "x", 0, 0, tiled=True)
     middle, hmod = combine(part, stream[0], jnp.concatenate([modulation[0, 2:], modulation[1, :2]]))
 
-    toks = [jnp.concatenate(line_gather(hmod), axis=0)]
+    toks = jnp.concatenate(line_gather(hmod), axis=0)[None]
     w_sib = lax.ppermute(w_own, "c", SWAP)
     sib = qkv(toks, w_sib, qk_gain[1])
     other = lax.ppermute(sib, "c", SWAP)
     own = qkv(toks, w_own, qk_gain[1])
     shape = (3, 8, ROWS, HEAD_DIM)
     place = 2 * (z ^ (blocks % 8)) + (c ^ (blocks // 8))
+    other, w_last = lax.optimization_barrier((other, w_last))
     attn = temporal(place, own.reshape(shape), other.reshape(shape))
     attn = lax.all_to_all(attn, ("z", "c"), 0, 0, tiled=True)
     out = project((blocks + turn(z)) % 16, attn, w_last, middle, modulation[1, 2:])

time: 233 us -> 202 us (0.87)
  waiting for transfers between devices: 79.4 us -> 49.4 us
  starting transfers between devices: 108 us -> 83 us
  blocking collectives: 0 us -> 24.9 us
  local copies, waits for them, and re-layouts: 6.16 us -> 8.72 us
    ppermute x8 -> x2, waiting for transfers between devices: 27.3 us -> 1.63 us  [the longest x1 1.63 us: local(): rows = jnp.where(mine, rows, lax.ppermute(rows, 'c', SWAP))]
    ppermute x8 -> x2, starting transfers between devices: 25.7 us -> 3.06 us  [the longest x1 2.22 us: local(): rows = jnp.where(mine, rows, lax.ppermute(rows, 'c', SWAP))]
    all_to_all x1, waiting for transfers between devices: 0.01 us -> 22.3 us  [local(): old = lax.all_to_all(chunk, ('z', 'c', 'h'), 0, 0, tiled=True)]
    ppermute x7, starting transfers between devices: 37 us -> 20.5 us  [to(): return lax.ppermute(part, 'z', [(z, z ^ k) for z in range(8)])]
    all_gather x0 -> x1, blocking collectives: none -> 16.3 us  [local(): w_heads = lax.all_gather(w_head, 'y', axis=0)]
    all_to_all x1, waiting for transfers between devices: 23.8 us -> 8.43 us  [local(): part = lax.all_to_all(part, 'x', 0, 0, tiled=True)]
    all_to_all x1, starting transfers between devices: 5.05 us -> 14.3 us  [local(): lax.all_to_all(old.reshape(16, 2, 64, 128), AXES, 0, 0, axis_index_groups...]
    all_to_all x0 -> x1, blocking collectives: none -> 8.59 us  [local(): attn = lax.all_to_all(attn, 'y', 0, 0, tiled=True)]
  transfers between devices with their start and end apart: 22 -> 17, of which waited for: 11 -> 5; matrix products, arithmetic and copies ran while one was open for 1% -> 3% of each run, Pallas kernels for 9% -> 3%
where the time goes in v3:
time: 202 us; the launch traced here: 201 us
  starting transfers between devices  83 us (41%)
  waiting for transfers between devices  49.4 us (24%)
  blocking collectives  24.9 us (12%)
  Pallas kernels  19.7 us (10%)
  between operations  13.9 us (7%)
  local copies, waits for them, and re-layouts  8.72 us (4%)
    all_to_all x1, waiting for transfers between devices, local(): old = lax.all_to_all(chunk, ('z', 'c', 'h'), 0, 0, tiled=True)  22.3 us
    ppermute x7, starting transfers between devices, to(): return lax.ppermute(part, 'z', [(z, z ^ k) for z in range(8)])  20.5 us
    all_to_all x1, starting transfers between devices, local(): old = lax.all_to_all(chunk, ('z', 'c', 'h'), 0, 0, tiled=True)  19.9 us
    pallas_call x9, Pallas kernels, call(): pl.pallas_call(kernel, out_shape=out_shape, scratch_shapes=list(scratch),...  19.7 us
    all_gather x1, blocking collectives, local(): w_heads = lax.all_gather(w_head, 'y', axis=0)  16.3 us
    all_to_all x1, waiting for transfers between devices, local(): attn = lax.all_to_all(attn, ('z', 'c'), 0, 0, tiled=True)  15.8 us
    all_to_all x1, starting transfers between devices, local(): lax.all_to_all(old.reshape(16, 2, 64, 128), AXES, 0, 0, axis_index_groups...  14.3 us
    ppermute x1, starting transfers between devices, local(): w_sib = lax.ppermute(w_own, 'c', SWAP)  9.75 us
  transfers between devices with their start and end apart: 17, of which 5 were waited for; matrix products, arithmetic and copies ran while one was open for 3% of the time, Pallas kernels for 3%

profile of v3, /device:TPU:1, one launch (start us, length us, event | category | flops | bytes accessed | tf_op | source)
XLA Modules:
  0.0 201.1 jit_solution(10966169075806640353)
XLA Ops:
  6.5 0.8 slice.46
  7.3 0.9 copy-done.2
  8.2 0.9 modulate.1
  9.1 1.0 slice_bitcast_fusion.2
  10.2 0.1 fusion.8
  10.3 0.1 pad_maximum_fusion
  10.3 0.8 collective-permute-start
  11.2 0.1 slice_bitcast_fusion
  11.4 0.2 reshape.33
  11.6 0.1 fusion.1
  11.8 0.9 broadcast_in_dim.18
  12.7 19.9 %all-to-all-start = ((bf16[32,64,128]{2,1,0:T(8,128)(2,1)}), bf16[32,64,128]{2,1,0:T(8,128)(2,1)}, u32[]{:S(2)}, u32[]{:S(2)}) async-start(bf16[32,64,128]{2,1,0:T(8,128)(2,1)} %bitcast.9), calls=%async_computation | async-start | bytes 1048576 | tf_op jit(solution)/shard_map/all_to_all | solution.py:269
  32.6 2.2 %collective-permute-start.1 = (bf16[360,1152]{1,0:T(8,128)(2,1)S(1)}, bf16[360,1152]{1,0:T(8,128)(2,1)}, u32[]{:S(2)}, u32[]{:S(2)}) collective-permute-start(bf16[360,1152]{1,0:T(8,128)(2,1)S(1)} %collective-permute-done), channel_id=1, source_target_pairs={{0,32},{32,0},{1,33},{33,1},{2,34},{34,2},{3,35},{35,3},{4,36},{36... | collective-permute-start | bytes 2488328 | tf_op jit(solution)/shard_map/ppermute | solution.py:273
  34.9 0.1 broadcast_in_dim.19
  34.9 0.2 broadcast_in_dim_reshape.8.rowp
  35.2 0.1 broadcast_in_dim.20
  35.2 0.1 broadcast_in_dim_reshape.7.colp
  35.4 1.6 collective-permute-done.1
  37.0 1.2 broadcast_select_fusion
  38.3 22.3 %all-to-all-done = bf16[32,64,128]{2,1,0:T(8,128)(2,1)} async-done(((bf16[32,64,128]{2,1,0:T(8,128)(2,1)}), bf16[32,64,128]{2,1,0:T(8,128)(2,1)}, u32[]{:S(2)}, u32[]{:S(2)}) %all-to-all-start) | async-done | bytes 524320 | tf_op jit(solution)/shard_map/all_to_all | solution.py:269
  60.5 14.3 %all-to-all-start.1 = ((bf16[16,2,64,128]{3,2,1,0:T(8,128)(2,1)}), bf16[16,2,64,128]{3,2,1,0:T(8,128)(2,1)S(1)}, u32[]{:S(2)}, u32[]{:S(2)}) async-start(bf16[16,2,64,128]{3,2,1,0:T(8,128)(2,1)} %bitcast.10), calls=%async_computation.1 | async-start | bytes 1048576 | tf_op jit(solution)/shard_map/all_to_all | solution.py:278
  74.9 0.7 fusion.9
  75.6 16.3 %all-gather.1 = bf16[288,1152]{1,0:T(8,128)(2,1)S(1)} all-gather(bf16[72,1152]{1,0:T(8,128)(2,1)S(1)} %get-tuple-element.42), channel_id=3, replica_groups=mesh['z'=8,'c'=2,'x'=4,'y'=4,'h'=2] {'y'}, dimensions={0}, use_global_device_ids=true | all-gather | bytes 829440 | tf_op jit(solution)/shard_map/all_gather | solution.py:277
  91.9 1.6 copy-done.1
  93.5 2.7 %qkv.3.q = bf16[3,896,72]{2,1,0:T(8,128)(2,1)S(1)} custom-call(bf16[4,224,1152]{2,1,0:T(8,128)(2,1)S(1)} %bitcast.40, bf16[216,1152]{1,0:T(8,128)(2,1)S(1)} %slice.61.w, f32[2,72]{1,0:T(2,128)S(1)} %get-tuple-element.48.gain), custom_call_target="tpu_custom_call" | custom-call | flops 445906944 | bytes 3000000 | tf_op jit(solution)/shard_map/qkv/pallas_call | solution.py:41
  96.1 5.0 %spatial.1 = bf16[4,4,56,72]{3,2,1,0:T(8,128)(2,1)S(1)} custom-call(bf16[3,896,72]{2,1,0:T(8,128)(2,1)S(1)} %qkv.3.q, bf16[32,64,128]{2,1,0:T(8,128)(2,1)S(1)} %bitcast.45, s32[896,1]{1,0:T(8,128)S(1)} %broadcast_in_dim_reshape.8.rowp, s32[1,1792]{1,0:T(1,128)S(1)} %broadcast_in_dim_reshape.7.colp), custom_call_target="tpu_custom_call" | custom-call | flops 600000000 | bytes 2000000 | tf_op jit(solution)/shard_map/spatial/pallas_call | solution.py:41
  101.2 8.6 %all_to_all.25 = bf16[4,4,56,72]{3,2,1,0:T(8,128)(2,1)S(1)} all-to-all(bf16[4,4,56,72]{3,2,1,0:T(8,128)(2,1)S(1)} %spatial.1), channel_id=1, replica_groups=mesh['z'=8,'c'=2,'x'=4,'y'=4,'h'=2] {'y'}, dimensions={0} | all-to-all | bytes 258048 | tf_op jit(solution)/shard_map/all_to_all | solution.py:291
  109.8 1.5 heads_out.1
  111.3 3.5 %all-to-all-start.3 = ((bf16[4,56,1152]{2,1,0:T(8,128)(2,1)}), bf16[4,56,1152]{2,1,0:T(8,128)(2,1)S(1)}, u32[]{:S(2)}, u32[]{:S(2)}) async-start(bf16[4,56,1152]{2,1,0:T(8,128)(2,1)} %heads_out.1), calls=%async_computation.3 | async-start | bytes 1032192 | tf_op jit(solution)/shard_map/all_to_all | solution.py:293
  114.9 8.4 %all-to-all-done.3.part = bf16[4,56,1152]{2,1,0:T(8,128)(2,1)S(1)} async-done(((bf16[4,56,1152]{2,1,0:T(8,128)(2,1)}), bf16[4,56,1152]{2,1,0:T(8,128)(2,1)S(1)}, u32[]{:S(2)}, u32[]{:S(2)}) %all-to-all-start.3) | async-done | bytes 516128 | tf_op jit(solution)/shard_map/all_to_all | solution.py:293
  123.3 0.3 combine.1
  123.6 1.9 collective-permute-start.5
  125.6 2.6 %collective-permute-start.2 = (bf16[56,1152]{1,0:T(8,128)(2,1)S(1)}, bf16[56,1152]{1,0:T(8,128)(2,1)S(1)}, u32[]{:S(2)}, u32[]{:S(2)}) collective-permute-start(bf16[56,1152]{1,0:T(8,128)(2,1)S(1)} %get-tuple-element.26), channel_id=1, source_target_pairs={{0,64},{64,0},{128,192},{192,128},{256,320},{320,256},{384,448},{4... | collective-permute-start | bytes 387080 | tf_op jit(solution)/shard_map/ppermute | solution.py:249
  128.1 3.4 %collective-permute-start.3 = (bf16[56,1152]{1,0:T(8,128)(2,1)S(1)}, bf16[56,1152]{1,0:T(8,128)(2,1)S(1)}, u32[]{:S(2)}, u32[]{:S(2)}) collective-permute-start(bf16[56,1152]{1,0:T(8,128)(2,1)S(1)} %get-tuple-element.26), channel_id=1, source_target_pairs={{0,128},{64,192},{128,0},{192,64},{256,384},{320,448},{384,256},{4... | collective-permute-start | bytes 387080 | tf_op jit(solution)/shard_map/ppermute | solution.py:249
  131.5 3.3 %collective-permute-start.4 = (bf16[56,1152]{1,0:T(8,128)(2,1)S(1)}, bf16[56,1152]{1,0:T(8,128)(2,1)S(1)}, u32[]{:S(2)}, u32[]{:S(2)}) collective-permute-start(bf16[56,1152]{1,0:T(8,128)(2,1)S(1)} %get-tuple-element.26), channel_id=1, source_target_pairs={{0,192},{64,128},{128,64},{192,0},{256,448},{320,384},{384,320},{4... | collective-permute-start | bytes 387080 | tf_op jit(solution)/shard_map/ppermute | solution.py:249
  134.9 1.9 collective-permute-start.6
  136.8 4.1 %collective-permute-start.7 = (bf16[56,1152]{1,0:T(8,128)(2,1)S(1)}, bf16[56,1152]{1,0:T(8,128)(2,1)S(1)}, u32[]{:S(2)}, u32[]{:S(2)}) collective-permute-start(bf16[56,1152]{1,0:T(8,128)(2,1)S(1)} %collective-permute-done.5), channel_id=1, source_target_pairs={{0,128},{64,192},{128,0},{192,64},{256,384},{320,448},{384,256},{4... | collective-permute-start | bytes 387080 | tf_op jit(solution)/shard_map/ppermute | solution.py:249
  140.9 3.3 %collective-permute-start.8 = (bf16[56,1152]{1,0:T(8,128)(2,1)S(1)}, bf16[56,1152]{1,0:T(8,128)(2,1)S(1)}, u32[]{:S(2)}, u32[]{:S(2)}) collective-permute-start(bf16[56,1152]{1,0:T(8,128)(2,1)S(1)} %collective-permute-done.5), channel_id=1, source_target_pairs={{0,192},{64,128},{128,64},{192,0},{256,448},{320,384},{384,320},{4... | collective-permute-start | bytes 387080 | tf_op jit(solution)/shard_map/ppermute | solution.py:249
  144.2 9.8 %collective-permute-start.9 = (bf16[216,1152]{1,0:T(8,128)(2,1)S(1)}, bf16[216,1152]{1,0:T(8,128)(2,1)S(1)}, u32[]{:S(2)}, u32[]{:S(2)}) collective-permute-start(bf16[216,1152]{1,0:T(8,128)(2,1)S(1)} %bitcast.41), channel_id=1, source_target_pairs={{0,32},{32,0},{1,33},{33,1},{2,34},{34,2},{3,35},{35,3},{4,36},{36... | collective-permute-start | bytes 1493000 | tf_op jit(solution)/shard_map/ppermute | solution.py:297
  154.2 1.3 collective-permute-done.9.w
  155.4 1.9 qkv.5
  157.3 4.9 %collective-permute-start.10 = (bf16[3,448,72]{2,1,0:T(8,128)(2,1)S(1)}, bf16[3,448,72]{2,1,0:T(8,128)(2,1)S(1)}, u32[]{:S(2)}, u32[]{:S(2)}) collective-permute-start(bf16[3,448,72]{2,1,0:T(8,128)(2,1)S(1)} %qkv.5), channel_id=1, source_target_pairs={{0,32},{32,0},{1,33},{33,1},{2,34},{34,2},{3,35},{35,3},{4,36},{36... | collective-permute-start | bytes 580616 | tf_op jit(solution)/shard_map/ppermute | solution.py:299
  162.2 1.9 qkv.4
  164.2 3.6 %temporal.1 = bf16[16,56,72]{2,1,0:T(8,128)(2,1)} custom-call(s32[16]{0:T(128)S(1)} %fusion.4.place, bf16[3,8,56,72]{3,2,1,0:T(8,128)(2,1)S(1)} %bitcast.43, bf16[3,8,56,72]{3,2,1,0:T(8,128)(2,1)S(1)} %bitcast.48), custom_call_target="tpu_custom_call" | custom-call | flops 50000000 | bytes 1000000 | tf_op jit(solution)/shard_map/temporal/pallas_call | solution.py:41
  167.8 7.1 %all-to-all-start.4 = ((bf16[16,56,72]{2,1,0:T(8,128)(2,1)}), bf16[16,56,72]{2,1,0:T(8,128)(2,1)S(1)}, u32[]{:S(2)}, u32[]{:S(2)}) async-start(bf16[16,56,72]{2,1,0:T(8,128)(2,1)} %temporal.1), calls=%async_computation.4 | async-start | bytes 458752 | tf_op jit(solution)/shard_map/all_to_all | solution.py:305
  174.9 15.8 %all-to-all-done.4.attn = bf16[16,56,72]{2,1,0:T(8,128)(2,1)S(1)} async-done(((bf16[16,56,72]{2,1,0:T(8,128)(2,1)}), bf16[16,56,72]{2,1,0:T(8,128)(2,1)S(1)}, u32[]{:S(2)}, u32[]{:S(2)}) %all-to-all-start.4) | async-done | bytes 129056 | tf_op jit(solution)/shard_map/all_to_all | solution.py:305
  190.7 1.7 copy-done
  192.4 1.8 project.1
  (51 shorter events, 0.5 us)
Async XLA Ops:
  6.5 85.3 %all-gather.6.cloned.1.call-start = ((), (), s32[]{:S(2)}) async-start(), calls=%async_computation.5 | async-start | bytes 2193408 | tf_op jit(solution)/shard_map/all_gather | solution.py:262
  7.3 0.9 copy-start.2
  8.2 1.9 copy-start.4
  10.2 1.0 copy-start.5
  10.3 1.3 copy-start.6
  10.3 22.3 %collective-permute-start = (bf16[360,1152]{1,0:T(8,128)(2,1)S(1)}, bf16[360,1152]{1,0:T(8,128)(2,1)S(1)}, u32[]{:S(2)}, u32[]{:S(2)}) collective-permute-start(bf16[360,1152]{1,0:T(8,128)(2,1)S(1)} %pad_maximum_fusion), channel_id=1, source_target_pairs={{0,0},{320,64},{128,128},{449,192},{256,256},{65,320},{384,384},{1... | collective-permute-start | bytes 2488328 | tf_op jit(solution)/shard_map/ppermute | solution.py:272
  11.6 23.8 %copy-start.8 = (f32[2,2,72]{2,1,0:T(2,128)S(1)}, f32[2,2,72]{2,1,0:T(2,128)}, u32[]{:S(2)}) copy-start(f32[2,2,72]{2,1,0:T(2,128)} %param.13) | copy-start | bytes 3460
  12.7 47.9 %all-to-all-start = ((bf16[32,64,128]{2,1,0:T(8,128)(2,1)}), bf16[32,64,128]{2,1,0:T(8,128)(2,1)}, u32[]{:S(2)}, u32[]{:S(2)}) async-start(bf16[32,64,128]{2,1,0:T(8,128)(2,1)} %bitcast.9), calls=%async_computation | async-start | bytes 1048576 | tf_op jit(solution)/shard_map/all_to_all | solution.py:269
  32.6 4.4 %collective-permute-start.1 = (bf16[360,1152]{1,0:T(8,128)(2,1)S(1)}, bf16[360,1152]{1,0:T(8,128)(2,1)}, u32[]{:S(2)}, u32[]{:S(2)}) collective-permute-start(bf16[360,1152]{1,0:T(8,128)(2,1)S(1)} %collective-permute-done), channel_id=1, source_target_pairs={{0,32},{32,0},{1,33},{33,1},{2,34},{34,2},{3,35},{35,3},{4,36},{36... | collective-permute-start | bytes 2488328 | tf_op jit(solution)/shard_map/ppermute | solution.py:273
  60.5 31.3 %all-to-all-start.1 = ((bf16[16,2,64,128]{3,2,1,0:T(8,128)(2,1)}), bf16[16,2,64,128]{3,2,1,0:T(8,128)(2,1)S(1)}, u32[]{:S(2)}, u32[]{:S(2)}) async-start(bf16[16,2,64,128]{3,2,1,0:T(8,128)(2,1)} %bitcast.10), calls=%async_computation.1 | async-start | bytes 1048576 | tf_op jit(solution)/shard_map/all_to_all | solution.py:278
  74.9 89.3 %all-gather.8.cloned.1.call-start = ((), (), s32[]{:S(2)}) async-start(), calls=%async_computation.6 | async-start | bytes 2820096 | tf_op jit(solution)/shard_map/all_gather | solution.py:290
  91.9 1.6 copy-start.1
  101.2 13.7 %copy-start.7 = (f32[2,3,1152]{2,0,1:T(2,128)S(1)}, f32[2,3,1152]{2,0,1:T(2,128)}, u32[]{:S(2)}) copy-start(f32[2,3,1152]{2,0,1:T(2,128)} %param.10) | copy-start | bytes 82948
  101.2 22.2 %copy-start.3 = (bf16[1,56,1152]{2,1,0:T(8,128)(2,1)S(1)}, bf16[1,56,1152]{2,1,0:T(8,128)(2,1)}, u32[]{:S(2)}) copy-start(bf16[1,56,1152]{2,1,0:T(8,128)(2,1)} %param.7) | copy-start | bytes 387076
  111.3 12.0 %all-to-all-start.3 = ((bf16[4,56,1152]{2,1,0:T(8,128)(2,1)}), bf16[4,56,1152]{2,1,0:T(8,128)(2,1)S(1)}, u32[]{:S(2)}, u32[]{:S(2)}) async-start(bf16[4,56,1152]{2,1,0:T(8,128)(2,1)} %heads_out.1), calls=%async_computation.3 | async-start | bytes 1032192 | tf_op jit(solution)/shard_map/all_to_all | solution.py:293
  123.6 11.2 %collective-permute-start.5 = (bf16[56,1152]{1,0:T(8,128)(2,1)S(1)}, bf16[56,1152]{1,0:T(8,128)(2,1)S(1)}, u32[]{:S(2)}, u32[]{:S(2)}) collective-permute-start(bf16[56,1152]{1,0:T(8,128)(2,1)S(1)} %get-tuple-element.26), channel_id=1, source_target_pairs={{0,256},{64,320},{128,384},{192,448},{256,0},{320,64},{384,128},{4... | collective-permute-start | bytes 387080 | tf_op jit(solution)/shard_map/ppermute | solution.py:249
  125.6 15.3 %collective-permute-start.2 = (bf16[56,1152]{1,0:T(8,128)(2,1)S(1)}, bf16[56,1152]{1,0:T(8,128)(2,1)S(1)}, u32[]{:S(2)}, u32[]{:S(2)}) collective-permute-start(bf16[56,1152]{1,0:T(8,128)(2,1)S(1)} %get-tuple-element.26), channel_id=1, source_target_pairs={{0,64},{64,0},{128,192},{192,128},{256,320},{320,256},{384,448},{4... | collective-permute-start | bytes 387080 | tf_op jit(solution)/shard_map/ppermute | solution.py:249
  128.1 16.1 %collective-permute-start.3 = (bf16[56,1152]{1,0:T(8,128)(2,1)S(1)}, bf16[56,1152]{1,0:T(8,128)(2,1)S(1)}, u32[]{:S(2)}, u32[]{:S(2)}) collective-permute-start(bf16[56,1152]{1,0:T(8,128)(2,1)S(1)} %get-tuple-element.26), channel_id=1, source_target_pairs={{0,128},{64,192},{128,0},{192,64},{256,384},{320,448},{384,256},{4... | collective-permute-start | bytes 387080 | tf_op jit(solution)/shard_map/ppermute | solution.py:249
  131.5 22.4 %collective-permute-start.4 = (bf16[56,1152]{1,0:T(8,128)(2,1)S(1)}, bf16[56,1152]{1,0:T(8,128)(2,1)S(1)}, u32[]{:S(2)}, u32[]{:S(2)}) collective-permute-start(bf16[56,1152]{1,0:T(8,128)(2,1)S(1)} %get-tuple-element.26), channel_id=1, source_target_pairs={{0,192},{64,128},{128,64},{192,0},{256,448},{320,384},{384,320},{4... | collective-permute-start | bytes 387080 | tf_op jit(solution)/shard_map/ppermute | solution.py:249
  134.9 19.1 %collective-permute-start.6 = (bf16[56,1152]{1,0:T(8,128)(2,1)S(1)}, bf16[56,1152]{1,0:T(8,128)(2,1)S(1)}, u32[]{:S(2)}, u32[]{:S(2)}) collective-permute-start(bf16[56,1152]{1,0:T(8,128)(2,1)S(1)} %collective-permute-done.5), channel_id=1, source_target_pairs={{0,64},{64,0},{128,192},{192,128},{256,320},{320,256},{384,448},{4... | collective-permute-start | bytes 387080 | tf_op jit(solution)/shard_map/ppermute | solution.py:249
  136.8 17.2 %collective-permute-start.7 = (bf16[56,1152]{1,0:T(8,128)(2,1)S(1)}, bf16[56,1152]{1,0:T(8,128)(2,1)S(1)}, u32[]{:S(2)}, u32[]{:S(2)}) collective-permute-start(bf16[56,1152]{1,0:T(8,128)(2,1)S(1)} %collective-permute-done.5), channel_id=1, source_target_pairs={{0,128},{64,192},{128,0},{192,64},{256,384},{320,448},{384,256},{4... | collective-permute-start | bytes 387080 | tf_op jit(solution)/shard_map/ppermute | solution.py:249
  140.9 13.1 %collective-permute-start.8 = (bf16[56,1152]{1,0:T(8,128)(2,1)S(1)}, bf16[56,1152]{1,0:T(8,128)(2,1)S(1)}, u32[]{:S(2)}, u32[]{:S(2)}) collective-permute-start(bf16[56,1152]{1,0:T(8,128)(2,1)S(1)} %collective-permute-done.5), channel_id=1, source_target_pairs={{0,192},{64,128},{128,64},{192,0},{256,448},{320,384},{384,320},{4... | collective-permute-start | bytes 387080 | tf_op jit(solution)/shard_map/ppermute | solution.py:249
  144.2 11.2 %collective-permute-start.9 = (bf16[216,1152]{1,0:T(8,128)(2,1)S(1)}, bf16[216,1152]{1,0:T(8,128)(2,1)S(1)}, u32[]{:S(2)}, u32[]{:S(2)}) collective-permute-start(bf16[216,1152]{1,0:T(8,128)(2,1)S(1)} %bitcast.41), channel_id=1, source_target_pairs={{0,32},{32,0},{1,33},{33,1},{2,34},{34,2},{3,35},{35,3},{4,36},{36... | collective-permute-start | bytes 1493000 | tf_op jit(solution)/shard_map/ppermute | solution.py:297
  157.3 6.8 %collective-permute-start.10 = (bf16[3,448,72]{2,1,0:T(8,128)(2,1)S(1)}, bf16[3,448,72]{2,1,0:T(8,128)(2,1)S(1)}, u32[]{:S(2)}, u32[]{:S(2)}) collective-permute-start(bf16[3,448,72]{2,1,0:T(8,128)(2,1)S(1)} %qkv.5), channel_id=1, source_target_pairs={{0,32},{32,0},{1,33},{33,1},{2,34},{34,2},{3,35},{35,3},{4,36},{36... | collective-permute-start | bytes 580616 | tf_op jit(solution)/shard_map/ppermute | solution.py:299
  167.8 22.9 %all-to-all-start.4 = ((bf16[16,56,72]{2,1,0:T(8,128)(2,1)}), bf16[16,56,72]{2,1,0:T(8,128)(2,1)S(1)}, u32[]{:S(2)}, u32[]{:S(2)}) async-start(bf16[16,56,72]{2,1,0:T(8,128)(2,1)} %temporal.1), calls=%async_computation.4 | async-start | bytes 458752 | tf_op jit(solution)/shard_map/all_to_all | solution.py:305
  190.7 1.8 copy-start
Sparse Core Ops, SparseCore 0:
  10.4 64.6 all-gather.5
  101.3 57.8 all-gather.7

commit v4 on v3

--- a/solution.py
+++ b/solution.py
@@ -16,7 +16,7 @@
 PLANE = 16
 QBLOCK = 4 * ROWS
 NEG = -1e30
-VMEM_LIMIT = 48 * 1024 * 1024
+VMEM_LIMIT = 20 * 1024 * 1024
 NT = (((1,), (1,)), ((), ()))
 
 
@@ -56,6 +56,30 @@
 def modulate(x, mod):
     shape = jax.ShapeDtypeStruct(x.shape, jnp.bfloat16)
     return call(modulate_kernel, (x, mod), shape, "modulate", moved=300_000)
+
+
+def pack_kernel(keys, values, out, scratch):
+    old = values[...].astype(jnp.float32)
+    scratch[:, :ROWS, :HEAD_DIM] = keys[...].astype(jnp.float32)
+    scratch[:, :ROWS, HEAD_DIM:] = old[:, :, :56]
+    scratch[:, ROWS:] = jnp.zeros_like(scratch[:, ROWS:])
+    for j in range(7):
+        scratch[:, ROWS:, 16 * j : 16 * j + 16] = old[:, 8 * j : 8 * j + 8, 56:]
+    chunk = scratch[...].astype(jnp.bfloat16)
+    for i in range(2):
+        out[:, i] = chunk
+
+
+def pack(keys, values):
+    frames, step = keys.shape[0], 4
+    out = jax.ShapeDtypeStruct((frames, 2, 64, 128), jnp.bfloat16)
+    block = pl.BlockSpec((step, ROWS, HEAD_DIM), lambda i: (i, 0, 0))
+    specs = ([block, block], pl.BlockSpec((step, 2, 64, 128), lambda i: (i, 0, 0, 0)))
+    packed = call(
+        pack_kernel, (keys, values), out, "pack", (pltpu.VMEM((step, 64, 128), jnp.float32),),
+        moved=1_000_000, grid=(frames // step,), specs=specs,
+    )
+    return packed.reshape(2 * frames, 64, 128)
 
 
 def qkv_kernel(toks, w, gain, out):
@@ -126,15 +150,20 @@
     )
 
 
-def heads_out_kernel(attn, w, out):
+def heads_out_kernel(place, attn, w0, w1, w2, w3, out):
     for i in range(4):
-        total = sum(dot(attn[k, i * ROWS : (i + 1) * ROWS], w[k]) for k in range(4))
+        total = sum(dot(attn[place[k], i * ROWS : (i + 1) * ROWS], w[w.shape[0] - HEAD_DIM :]) for k, w in enumerate((w0, w1, w2, w3)))
         out[i] = total.astype(jnp.bfloat16)
 
 
-def heads_out(attn, w):
-    out = jax.ShapeDtypeStruct((4, ROWS, w.shape[2]), jnp.bfloat16)
-    return call(heads_out_kernel, (attn, w), out, "heads_out", flops=150_000_000, moved=1_200_000)
+def heads_out(place, attn, ws):
+    out = jax.ShapeDtypeStruct((4, ROWS, ws[0].shape[1]), jnp.bfloat16)
+    vmem = pl.BlockSpec(memory_space=pltpu.VMEM)
+    specs = ([pl.BlockSpec(memory_space=pltpu.SMEM)] + [vmem] * 5, vmem)
+    return call(
+        heads_out_kernel, (place, attn, *ws), out, "heads_out", flops=150_000_000, moved=1_200_000,
+        grid=(), specs=specs,
+    )
 
 
 def combine_kernel(part, resid, mod, middle, hmod):
@@ -152,23 +181,39 @@
 
 
 def project_kernel(heads, attn, w, resid, gate, out, attn_s):
-    for g in range(PLANE):
-        attn_s[:, g * HEAD_DIM : (g + 1) * HEAD_DIM] = attn[heads[g]].astype(jnp.float32)
+    @pl.when(pl.program_id(0) == 0)
+    def _():
+        for g in range(PLANE):
+            piece = attn[heads[g]].astype(jnp.float32)
+            at = g * HEAD_DIM
+            attn_s[:32, at : at + 72] = piece[:, :72]
+            attn_s[32:, at : at + 56] = piece[:24, 72:]
+            for j in range(3):
+                attn_s[32 + 8 * j : 40 + 8 * j, at + 56 : at + 72] = piece[24:, 72 + 16 * j : 88 + 16 * j]
+
     summed = dot(attn_s[...].astype(jnp.bfloat16), w[...])
     out[...] = (resid[...].astype(jnp.float32) + gate[...] * summed).astype(jnp.bfloat16)
 
 
 def project(heads, attn, w, resid, gate):
     out = jax.ShapeDtypeStruct(resid.shape, jnp.bfloat16)
-    vmem = pl.BlockSpec(memory_space=pltpu.VMEM)
-    specs = ([pl.BlockSpec(memory_space=pltpu.SMEM)] + [vmem] * 4, vmem)
+    part = w.shape[1] // 3
+    columns = lambda a: pl.BlockSpec((a.shape[0], part), lambda i: (0, i))
+    specs = (
+        [
+            pl.BlockSpec(memory_space=pltpu.SMEM),
+            pl.BlockSpec(attn.shape, lambda i: (0, 0, 0)),
+            columns(w), columns(resid), columns(gate),
+        ],
+        columns(resid),
+    )
     return call(
         project_kernel, (heads, attn, w, resid, gate), out, "project", (pltpu.VMEM(resid.shape, jnp.float32),),
-        flops=150_000_000, moved=3_200_000, grid=(), specs=specs,
-    )
-
-
-def temporal_kernel(place, own, other, out):
+        flops=150_000_000, moved=3_200_000, grid=(3,), specs=specs,
+    )
+
+
+def temporal_kernel(place, own, other, out, packed):
     factor = HEAD_DIM ** (-0.5)
     half = own.shape[1]
     size = 2 * half * 8
@@ -188,18 +233,26 @@
         top = jnp.max(scores, axis=1, keepdims=True)
         expo = jnp.exp((scores - top) * factor)
         weights = (expo / jnp.sum(expo, axis=1, keepdims=True)).astype(jnp.bfloat16)
-        mixed = dot(weights, pick(2)).astype(jnp.bfloat16)
-        for f in range(2 * half):
-            out[place[f], at] = mixed[8 * f : 8 * f + 8]
+        mixed = dot(weights, pick(2)).reshape(2 * half, 8, HEAD_DIM)
+        if g < 4:
+            packed[:, at, :72] = mixed
+        else:
+            packed[:, slice(8 * g - 32, 8 * g - 24), 72:] = mixed[:, :, :56]
+            packed[:, 24:, 72 + 16 * (g - 4) : 88 + 16 * (g - 4)] = mixed[:, :, 56:]
+
+    packed[:, 24:, 120:] = jnp.zeros_like(packed[:, 24:, 120:])
+    for f in range(2 * half):
+        out[place[f]] = packed[f].astype(jnp.bfloat16)
 
 
 def temporal(place, own, other):
-    shape = jax.ShapeDtypeStruct((2 * own.shape[1],) + own.shape[2:], jnp.bfloat16)
+    frames = 2 * own.shape[1]
+    shape = jax.ShapeDtypeStruct((frames, 32, 128), jnp.bfloat16)
     vmem = pl.BlockSpec(memory_space=pltpu.VMEM)
     specs = ([pl.BlockSpec(memory_space=pltpu.SMEM), vmem, vmem], vmem)
     return call(
-        temporal_kernel, (place, own, other), shape, "temporal", flops=50_000_000, moved=1_000_000,
-        trans=120_000, grid=(), specs=specs,
+        temporal_kernel, (place, own, other), shape, "temporal", (pltpu.VMEM((frames, 32, 128), jnp.float32),),
+        flops=50_000_000, moved=1_000_000, trans=120_000, grid=(), specs=specs,
     )
 
 
@@ -244,12 +297,15 @@
     return [block] + [lax.ppermute(block, axis, [(i, i ^ k) for i in range(4)]) for k in (1, 2, 3)]
 
 
+def xor_gather(block, axis):
+    return [block] + [lax.ppermute(block, axis, [(i, i ^ k) for i in range(4)]) for k in (1, 2, 3)]
+
+
+LOOP = (0, 2, 4, 6, 7, 5, 3, 1)
+
+
 def line_gather(block):
-    def to(part, k):
-        return lax.ppermute(part, "z", [(z, z ^ k) for z in range(8)])
-
-    far, *near = [to(block, k) for k in (4, 3, 2, 1)]
-    return lax.optimization_barrier([block, *near[::-1], far] + [to(far, k) for k in (1, 2, 3)])
+    return lax.all_gather(block, "z", axis=0, axis_index_groups=[list(LOOP)])
 
 
 def local(stream, stale_keys, stale_values, modulation, w_qkv, w_out, qk_gain):
@@ -261,11 +317,7 @@
     hmod = modulate(stream[0], modulation[0])
     toks = lax.all_gather(hmod, ("x", "y"), axis=0).reshape(4, QBLOCK, width)
 
-    main = jnp.concatenate([stale_keys, stale_values[:, :, :56]], axis=2)
-    tail = stale_values[:, :, 56:].reshape(16, 7, 8, 16).transpose(0, 2, 1, 3).reshape(16, 8, 112)
-    tail = jnp.pad(tail, ((0, 0), (0, 0), (0, 16)))
-    chunk = jnp.concatenate([main, tail], axis=1)
-    chunk = jnp.broadcast_to(chunk[:, None], (16, 2, 64, 128)).reshape(32, 64, 128)
+    chunk = pack(stale_keys, stale_values)
     old = lax.all_to_all(chunk, ("z", "c", "h"), 0, 0, tiled=True)
 
     rows = jnp.concatenate([w_qkv[0].reshape(3 * HEAD_DIM, width), w_out[0], w_out[1]], axis=0)
@@ -274,7 +326,6 @@
     w_col, w_head, w_last = (
         rows[: 3 * HEAD_DIM], rows[3 * HEAD_DIM : 4 * HEAD_DIM], rows[4 * HEAD_DIM :]
     )
-    w_heads = lax.all_gather(w_head, "y", axis=0)
     old = lax.all_to_all(
         old.reshape(16, 2, 64, 128), AXES, 0, 0, axis_index_groups=rolled(), tiled=True
     )
@@ -282,24 +333,24 @@
     fresh = qkv(toks, w_col, qk_gain[0])
     rowp = jnp.repeat(2 * blocks + h, ROWS)[:, None]
     colp = jnp.repeat((lax.iota(jnp.int32, 2 * PLANE) - 2 * turn(z)) % (2 * PLANE), ROWS)[None, :]
-    old, w_heads = lax.optimization_barrier((old, w_heads))
+    w_heads = xor_gather(rows[3 * HEAD_DIM - 0 : 4 * HEAD_DIM], "y")
     attn = spatial(fresh, old.reshape(2 * PLANE, 64, 128), rowp, colp)
-    attn, w_last, w_own = lax.optimization_barrier(
-        (attn, w_last, w_qkv[1].reshape(3 * HEAD_DIM, width))
+    attn, w_heads, w_last, w_own = lax.optimization_barrier(
+        (attn, w_heads, w_last, w_qkv[1].reshape(3 * HEAD_DIM, width))
     )
     w_last = lax.all_gather(w_last, ("x", "y"), axis=0).reshape(width, width)
     attn = lax.all_to_all(attn, "y", 0, 0, tiled=True)
-    part = heads_out(attn.reshape(4, QBLOCK, HEAD_DIM), w_heads)
+    part = heads_out(y ^ blocks[:4], attn.reshape(4, QBLOCK, HEAD_DIM), w_heads)
     part = lax.all_to_all(part, "x", 0, 0, tiled=True)
     middle, hmod = combine(part, stream[0], jnp.concatenate([modulation[0, 2:], modulation[1, :2]]))
 
-    toks = jnp.concatenate(line_gather(hmod), axis=0)[None]
+    toks = line_gather(hmod).reshape(1, 8 * ROWS, width)
     w_sib = lax.ppermute(w_own, "c", SWAP)
     sib = qkv(toks, w_sib, qk_gain[1])
     other = lax.ppermute(sib, "c", SWAP)
     own = qkv(toks, w_own, qk_gain[1])
     shape = (3, 8, ROWS, HEAD_DIM)
-    place = 2 * (z ^ (blocks % 8)) + (c ^ (blocks // 8))
+    place = 2 * jnp.array(LOOP * 2, jnp.int32) + (c ^ (blocks // 8))
     other, w_last = lax.optimization_barrier((other, w_last))
     attn = temporal(place, own.reshape(shape), other.reshape(shape))
     attn = lax.all_to_all(attn, ("z", "c"), 0, 0, tiled=True)

time: 202 us -> 197 us (0.975)
  starting transfers between devices: 83 us -> 75.8 us
  Pallas kernels: 19.7 us -> 23.4 us
  waiting for transfers between devices: 49.4 us -> 46.9 us
  blocking collectives: 24.9 us -> 27.3 us
    all_gather x1, blocking collectives: 16.3 us -> 27.3 us  [line_gather(): return lax.all_gather(block, 'z', axis=0, axis_index_groups=[list(LOOP)])]
    ppermute x7 -> x3, starting transfers between devices: 20.5 us -> 9.57 us  [xor_gather(): lax.ppermute(block, axis, [(i, i ^ k) for i in range(4)])]
    all_to_all x1 -> x0, blocking collectives: 8.59 us -> none  [local(): attn = lax.all_to_all(attn, 'y', 0, 0, tiled=True)]
    ppermute x1, starting transfers between devices: 9.75 us -> 3.64 us  [local(): w_sib = lax.ppermute(w_own, 'c', SWAP)]
    all_to_all x0 -> x1, waiting for transfers between devices: none -> 5.8 us  [local(): attn = lax.all_to_all(attn, 'y', 0, 0, tiled=True)]
    ppermute x1, starting transfers between devices: 4.88 us -> 9.78 us  [local(): other = lax.ppermute(sib, 'c', SWAP)]
    all_to_all x1, waiting for transfers between devices: 8.43 us -> 4.55 us  [local(): part = lax.all_to_all(part, 'x', 0, 0, tiled=True)]
    all_to_all x1, waiting for transfers between devices: 15.8 us -> 12 us  [local(): attn = lax.all_to_all(attn, ('z', 'c'), 0, 0, tiled=True)]
  transfers between devices with their start and end apart: 17 -> 14, of which waited for: 5 -> 6; matrix products, arithmetic and copies ran while one was open for 3% -> 2% of each run, Pallas kernels for 3% -> 8%
where the time goes in v4:
time: 197 us; the launch traced here: 196 us
  starting transfers between devices  75.8 us (38%)
  waiting for transfers between devices  46.9 us (24%)
  blocking collectives  27.3 us (14%)
  Pallas kernels  23.4 us (12%)
  between operations  13.8 us (7%)
  local copies, waits for them, and re-layouts  7.3 us (4%)
    all_gather x1, blocking collectives, line_gather(): return lax.all_gather(block, 'z', axis=0, axis_index_groups=[list(LOOP)])  27.3 us
    pallas_call x10, Pallas kernels, call(): pl.pallas_call(kernel, out_shape=out_shape, scratch_shapes=list(scratch),...  23.4 us
    all_to_all x1, waiting for transfers between devices, local(): old = lax.all_to_all(chunk, ('z', 'c', 'h'), 0, 0, tiled=True)  22.3 us
    all_to_all x1, starting transfers between devices, local(): old = lax.all_to_all(chunk, ('z', 'c', 'h'), 0, 0, tiled=True)  19.9 us
    all_to_all x1, starting transfers between devices, local(): lax.all_to_all(old.reshape(16, 2, 64, 128), AXES, 0, 0, axis_index_groups...  14 us
    all_to_all x1, waiting for transfers between devices, local(): attn = lax.all_to_all(attn, ('z', 'c'), 0, 0, tiled=True)  12 us
    ppermute x1, starting transfers between devices, local(): other = lax.ppermute(sib, 'c', SWAP)  9.78 us
    ppermute x3, starting transfers between devices, xor_gather(): lax.ppermute(block, axis, [(i, i ^ k) for i in range(4)])  9.57 us
  transfers between devices with their start and end apart: 14, of which 6 were waited for; matrix products, arithmetic and copies ran while one was open for 2% of the time, Pallas kernels for 8%

profile of v4, /device:TPU:1, one launch (start us, length us, event | category | flops | bytes accessed | tf_op | source)
XLA Modules:
  0.0 195.8 jit_solution(9523148037222997633)
XLA Ops:
  6.5 0.8 slice.44
  7.3 0.9 copy-done.2
  8.2 0.9 modulate.1
  9.1 0.0 all-gather.6.cloned.1.call-update
  9.1 1.0 slice_bitcast_fusion.1
  10.2 0.1 fusion.4
  10.3 0.1 pad_maximum_fusion
  10.3 0.8 collective-permute-start
  11.2 1.7 pack.1
  12.9 19.9 %all-to-all-start = ((bf16[32,64,128]{2,1,0:T(8,128)(2,1)}), bf16[32,64,128]{2,1,0:T(8,128)(2,1)}, u32[]{:S(2)}, u32[]{:S(2)}) async-start(bf16[32,64,128]{2,1,0:T(8,128)(2,1)} %bitcast.7), calls=%async_computation | async-start | bytes 1048576 | tf_op jit(solution)/shard_map/all_to_all | solution.py:321
  32.9 2.2 %collective-permute-start.1 = (bf16[360,1152]{1,0:T(8,128)(2,1)S(1)}, bf16[360,1152]{1,0:T(8,128)(2,1)}, u32[]{:S(2)}, u32[]{:S(2)}) collective-permute-start(bf16[360,1152]{1,0:T(8,128)(2,1)S(1)} %collective-permute-done), channel_id=1, source_target_pairs={{0,32},{32,0},{1,33},{33,1},{2,34},{34,2},{3,35},{35,3},{4,36},{36... | collective-permute-start | bytes 2488328 | tf_op jit(solution)/shard_map/ppermute | solution.py:325
  35.1 0.1 broadcast_in_dim.10
  35.2 0.1 broadcast_in_dim_reshape.7.colp
  35.3 1.9 collective-permute-done.1
  37.2 1.3 broadcast_select_fusion
  38.5 22.3 %all-to-all-done = bf16[32,64,128]{2,1,0:T(8,128)(2,1)} async-done(((bf16[32,64,128]{2,1,0:T(8,128)(2,1)}), bf16[32,64,128]{2,1,0:T(8,128)(2,1)}, u32[]{:S(2)}, u32[]{:S(2)}) %all-to-all-start) | async-done | bytes 524320 | tf_op jit(solution)/shard_map/all_to_all | solution.py:321
  60.8 14.0 %all-to-all-start.1 = ((bf16[16,2,64,128]{3,2,1,0:T(8,128)(2,1)}), bf16[16,2,64,128]{3,2,1,0:T(8,128)(2,1)S(1)}, u32[]{:S(2)}, u32[]{:S(2)}) async-start(bf16[16,2,64,128]{3,2,1,0:T(8,128)(2,1)} %bitcast.8), calls=%async_computation.1 | async-start | bytes 1048576 | tf_op jit(solution)/shard_map/all_to_all | solution.py:329
  74.8 0.0 all-gather.8.cloned.1.call-start
  74.9 0.7 fusion.5
  75.6 3.3 %collective-permute-start.2 = (bf16[72,1152]{1,0:T(8,128)(2,1)S(1)}, bf16[72,1152]{1,0:T(8,128)(2,1)S(1)}, u32[]{:S(2)}, u32[]{:S(2)}) collective-permute-start(bf16[72,1152]{1,0:T(8,128)(2,1)S(1)} %get-tuple-element.17.w0), channel_id=1, source_target_pairs={{0,2},{2,0},{4,6},{6,4},{1,3},{3,1},{5,7},{7,5},{8,10},{10,8},{12,... | collective-permute-start | bytes 497672 | tf_op jit(solution)/shard_map/ppermute | solution.py:301
  78.8 4.3 %collective-permute-start.3 = (bf16[72,1152]{1,0:T(8,128)(2,1)S(1)}, bf16[72,1152]{1,0:T(8,128)(2,1)S(1)}, u32[]{:S(2)}, u32[]{:S(2)}) collective-permute-start(bf16[72,1152]{1,0:T(8,128)(2,1)S(1)} %get-tuple-element.17.w0), channel_id=1, source_target_pairs={{0,4},{2,6},{4,0},{6,2},{1,5},{3,7},{5,1},{7,3},{8,12},{10,14},{12... | collective-permute-start | bytes 497672 | tf_op jit(solution)/shard_map/ppermute | solution.py:301
  83.1 2.0 %collective-permute-start.4 = (bf16[72,1152]{1,0:T(8,128)(2,1)S(1)}, bf16[72,1152]{1,0:T(8,128)(2,1)S(1)}, u32[]{:S(2)}, u32[]{:S(2)}) collective-permute-start(bf16[72,1152]{1,0:T(8,128)(2,1)S(1)} %get-tuple-element.17.w0), channel_id=1, source_target_pairs={{0,6},{2,4},{4,2},{6,0},{1,7},{3,5},{5,3},{7,1},{8,14},{10,12},{12... | collective-permute-start | bytes 497672 | tf_op jit(solution)/shard_map/ppermute | solution.py:301
  85.2 0.1 broadcast_in_dim.9
  85.2 0.2 broadcast_in_dim_reshape.8.rowp
  85.5 0.0 all-gather.6.cloned.1.call-done
  85.5 1.6 copy-done.1
  87.1 2.7 %qkv.3.q = bf16[3,896,72]{2,1,0:T(8,128)(2,1)S(1)} custom-call(bf16[4,224,1152]{2,1,0:T(8,128)(2,1)S(1)} %bitcast.32, bf16[216,1152]{1,0:T(8,128)(2,1)S(1)} %slice.57.w, f32[2,72]{1,0:T(2,128)S(1)} %get-tuple-element.36.gain), custom_call_target="tpu_custom_call" | custom-call | flops 445906944 | bytes 3000000 | tf_op jit(solution)/shard_map/qkv/pallas_call | solution.py:41
  89.8 5.7 %spatial.1 = bf16[4,4,56,72]{3,2,1,0:T(8,128)(2,1)} custom-call(bf16[3,896,72]{2,1,0:T(8,128)(2,1)S(1)} %qkv.3.q, bf16[32,64,128]{2,1,0:T(8,128)(2,1)S(1)} %bitcast.37, s32[896,1]{1,0:T(8,128)S(1)} %broadcast_in_dim_reshape.8.rowp, s32[1,1792]{1,0:T(1,128)S(1)} %broadcast_in_dim_reshape.7.colp), custom_call_target="tpu_custom_call" | custom-call | flops 600000000 | bytes 2000000 | tf_op jit(solution)/shard_map/spatial/pallas_call | solution.py:41
  95.5 0.3 collective-permute-done.4.w3
  95.8 0.0 all-gather.8.cloned.1.call-update
  95.8 3.7 %all-to-all-start.2 = ((bf16[4,4,56,72]{3,2,1,0:T(8,128)(2,1)}), bf16[4,4,56,72]{3,2,1,0:T(8,128)(2,1)S(1)}, u32[]{:S(2)}, u32[]{:S(2)}) async-start(bf16[4,4,56,72]{3,2,1,0:T(8,128)(2,1)} %spatial.1), calls=%async_computation.2 | async-start | bytes 458752 | tf_op jit(solution)/shard_map/all_to_all | solution.py:342
  99.5 5.8 %all-to-all-done.2 = bf16[4,4,56,72]{3,2,1,0:T(8,128)(2,1)S(1)} async-done(((bf16[4,4,56,72]{3,2,1,0:T(8,128)(2,1)}), bf16[4,4,56,72]{3,2,1,0:T(8,128)(2,1)S(1)}, u32[]{:S(2)}, u32[]{:S(2)}) %all-to-all-start.2) | async-done | bytes 129056 | tf_op jit(solution)/shard_map/all_to_all | solution.py:342
  105.3 2.1 %heads_out.1 = bf16[4,56,1152]{2,1,0:T(8,128)(2,1)} custom-call(s32[4]{0:T(128)S(1)} %slice_xor_fusion.place, bf16[4,224,72]{2,1,0:T(8,128)(2,1)S(1)} %bitcast.36, bf16[72,1152]{1,0:T(8,128)(2,1)S(1)} %get-tuple-element.17.w0, bf16[72,1152]{1,0:T(8,128)(2,1)S(1)} %collective-permute-done.2.w1, bf16[72,1152]{1,0:T(8,128)(2,1)S(1)} %collective-permute-done.3.w2, ...), custom_call_target="tpu_custom_call" | custom-call | flops 150000000 | bytes 1200000 | tf_op jit(solution)/shard_map/heads_out/pallas_call | solution.py:41
  107.4 4.0 %all-to-all-start.3 = ((bf16[4,56,1152]{2,1,0:T(8,128)(2,1)}), bf16[4,56,1152]{2,1,0:T(8,128)(2,1)S(1)}, u32[]{:S(2)}, u32[]{:S(2)}) async-start(bf16[4,56,1152]{2,1,0:T(8,128)(2,1)} %heads_out.1), calls=%async_computation.3 | async-start | bytes 1032192 | tf_op jit(solution)/shard_map/all_to_all | solution.py:344
  111.5 3.6 %collective-permute-start.5 = (bf16[216,1152]{1,0:T(8,128)(2,1)S(1)}, bf16[216,1152]{1,0:T(8,128)(2,1)S(1)}, u32[]{:S(2)}, u32[]{:S(2)}) collective-permute-start(bf16[216,1152]{1,0:T(8,128)(2,1)S(1)} %bitcast.33), channel_id=1, source_target_pairs={{0,32},{32,0},{1,33},{33,1},{2,34},{34,2},{3,35},{35,3},{4,36},{36... | collective-permute-start | bytes 1493000 | tf_op jit(solution)/shard_map/ppermute | solution.py:348
  115.1 4.6 %all-to-all-done.3.part = bf16[4,56,1152]{2,1,0:T(8,128)(2,1)S(1)} async-done(((bf16[4,56,1152]{2,1,0:T(8,128)(2,1)}), bf16[4,56,1152]{2,1,0:T(8,128)(2,1)S(1)}, u32[]{:S(2)}, u32[]{:S(2)}) %all-to-all-start.3) | async-done | bytes 516128 | tf_op jit(solution)/shard_map/all_to_all | solution.py:344
  119.7 0.3 combine.1
  120.0 0.0 copy-start.9
  120.0 27.3 %all-gather.1 = bf16[448,1152]{1,0:T(8,128)(2,1)S(1)} all-gather(bf16[56,1152]{1,0:T(8,128)(2,1)S(1)} %get-tuple-element.21), channel_id=3, replica_groups={{0,128,256,384,448,320,192,64},{1,129,257,385,449,321,193,65},{2,130,25..., dimensions={0}, use_global_device_ids=true | all-gather | bytes 1161216 | tf_op jit(solution)/shard_map/all_gather | solution.py:308
  147.3 1.9 qkv.5
  149.2 9.8 %collective-permute-start.6 = (bf16[3,448,72]{2,1,0:T(8,128)(2,1)S(1)}, bf16[3,448,72]{2,1,0:T(8,128)(2,1)S(1)}, u32[]{:S(2)}, u32[]{:S(2)}) collective-permute-start(bf16[3,448,72]{2,1,0:T(8,128)(2,1)S(1)} %qkv.5), channel_id=1, source_target_pairs={{0,32},{32,0},{1,33},{33,1},{2,34},{34,2},{3,35},{35,3},{4,36},{36... | collective-permute-start | bytes 580616 | tf_op jit(solution)/shard_map/ppermute | solution.py:350
  159.0 1.9 qkv.4
  160.9 0.0 all-gather.8.cloned.1.call-done.w
  161.0 3.7 %temporal.1 = bf16[16,32,128]{2,1,0:T(8,128)(2,1)} custom-call(s32[16]{0:T(128)S(1)} %fusion.1.place, bf16[3,8,56,72]{3,2,1,0:T(8,128)(2,1)S(1)} %bitcast.35, bf16[3,8,56,72]{3,2,1,0:T(8,128)(2,1)S(1)} %bitcast.40), custom_call_target="tpu_custom_call" | custom-call | flops 50000000 | bytes 1000000 | tf_op jit(solution)/shard_map/temporal/pallas_call | solution.py:41
  164.6 8.0 %all-to-all-start.4 = ((bf16[16,32,128]{2,1,0:T(8,128)(2,1)}), bf16[16,32,128]{2,1,0:T(8,128)(2,1)S(1)}, u32[]{:S(2)}, u32[]{:S(2)}) async-start(bf16[16,32,128]{2,1,0:T(8,128)(2,1)} %temporal.1), calls=%async_computation.4 | async-start | bytes 262144 | tf_op jit(solution)/shard_map/all_to_all | solution.py:356
  172.7 12.0 %all-to-all-done.4.attn = bf16[16,32,128]{2,1,0:T(8,128)(2,1)S(1)} async-done(((bf16[16,32,128]{2,1,0:T(8,128)(2,1)}), bf16[16,32,128]{2,1,0:T(8,128)(2,1)S(1)}, u32[]{:S(2)}, u32[]{:S(2)}) %all-to-all-start.4) | async-done | bytes 131104 | tf_op jit(solution)/shard_map/all_to_all | solution.py:356
  184.7 1.7 copy-done
  186.4 2.6 %project.1 = bf16[56,1152]{1,0:T(8,128)(2,1)} custom-call(s32[16]{0:T(128)S(1)} %and_select_fusion.2.heads, bf16[16,32,128]{2,1,0:T(8,128)(2,1)S(1)} %all-to-all-done.4.attn, bf16[1152,1152]{1,0:T(8,128)(2,1)S(1)} %copy-done, bf16[56,1152]{1,0:T(8,128)(2,1)S(1)} %get-tuple-element.26.resid, f32[1,1152]{1,0:T(1,128)S(1)} %get-tuple-element.33.gate), custom_call_target="tpu_custom_call" | custom-call | flops 150000000 | bytes 3200000 | tf_op jit(solution)/shard_map/project/pallas_call | solution.py:41
  (36 shorter events, 0.2 us)
Async XLA Ops:
  6.5 79.0 %all-gather.6.cloned.1.call-start = ((), (), s32[]{:S(2)}) async-start(), calls=%async_computation.5 | async-start | bytes 2193408 | tf_op jit(solution)/shard_map/all_gather | solution.py:318
  7.3 0.9 copy-start.2
  8.2 1.9 copy-start.6
  10.2 1.1 copy-start.4
  10.2 1.1 copy-start.5
  10.3 25.0 %copy-start.8 = (f32[2,2,72]{2,1,0:T(2,128)S(1)}, f32[2,2,72]{2,1,0:T(2,128)}, u32[]{:S(2)}) copy-start(f32[2,2,72]{2,1,0:T(2,128)} %param.14) | copy-start | bytes 3460
  10.3 22.5 %collective-permute-start = (bf16[360,1152]{1,0:T(8,128)(2,1)S(1)}, bf16[360,1152]{1,0:T(8,128)(2,1)S(1)}, u32[]{:S(2)}, u32[]{:S(2)}) collective-permute-start(bf16[360,1152]{1,0:T(8,128)(2,1)S(1)} %pad_maximum_fusion), channel_id=1, source_target_pairs={{0,0},{320,64},{128,128},{449,192},{256,256},{65,320},{384,384},{1... | collective-permute-start | bytes 2488328 | tf_op jit(solution)/shard_map/ppermute | solution.py:324
  12.9 47.9 %all-to-all-start = ((bf16[32,64,128]{2,1,0:T(8,128)(2,1)}), bf16[32,64,128]{2,1,0:T(8,128)(2,1)}, u32[]{:S(2)}, u32[]{:S(2)}) async-start(bf16[32,64,128]{2,1,0:T(8,128)(2,1)} %bitcast.7), calls=%async_computation | async-start | bytes 1048576 | tf_op jit(solution)/shard_map/all_to_all | solution.py:321
  32.9 4.4 %collective-permute-start.1 = (bf16[360,1152]{1,0:T(8,128)(2,1)S(1)}, bf16[360,1152]{1,0:T(8,128)(2,1)}, u32[]{:S(2)}, u32[]{:S(2)}) collective-permute-start(bf16[360,1152]{1,0:T(8,128)(2,1)S(1)} %collective-permute-done), channel_id=1, source_target_pairs={{0,32},{32,0},{1,33},{33,1},{2,34},{34,2},{3,35},{35,3},{4,36},{36... | collective-permute-start | bytes 2488328 | tf_op jit(solution)/shard_map/ppermute | solution.py:325
  60.8 29.0 %all-to-all-start.1 = ((bf16[16,2,64,128]{3,2,1,0:T(8,128)(2,1)}), bf16[16,2,64,128]{3,2,1,0:T(8,128)(2,1)S(1)}, u32[]{:S(2)}, u32[]{:S(2)}) async-start(bf16[16,2,64,128]{3,2,1,0:T(8,128)(2,1)} %bitcast.8), calls=%async_computation.1 | async-start | bytes 1048576 | tf_op jit(solution)/shard_map/all_to_all | solution.py:329
  74.8 86.1 %all-gather.8.cloned.1.call-start = ((), (), s32[]{:S(2)}) async-start(), calls=%async_computation.6 | async-start | bytes 2820096 | tf_op jit(solution)/shard_map/all_gather | solution.py:341
  75.6 19.9 %collective-permute-start.2 = (bf16[72,1152]{1,0:T(8,128)(2,1)S(1)}, bf16[72,1152]{1,0:T(8,128)(2,1)S(1)}, u32[]{:S(2)}, u32[]{:S(2)}) collective-permute-start(bf16[72,1152]{1,0:T(8,128)(2,1)S(1)} %get-tuple-element.17.w0), channel_id=1, source_target_pairs={{0,2},{2,0},{4,6},{6,4},{1,3},{3,1},{5,7},{7,5},{8,10},{10,8},{12,... | collective-permute-start | bytes 497672 | tf_op jit(solution)/shard_map/ppermute | solution.py:301
  78.8 16.7 %collective-permute-start.3 = (bf16[72,1152]{1,0:T(8,128)(2,1)S(1)}, bf16[72,1152]{1,0:T(8,128)(2,1)S(1)}, u32[]{:S(2)}, u32[]{:S(2)}) collective-permute-start(bf16[72,1152]{1,0:T(8,128)(2,1)S(1)} %get-tuple-element.17.w0), channel_id=1, source_target_pairs={{0,4},{2,6},{4,0},{6,2},{1,5},{3,7},{5,1},{7,3},{8,12},{10,14},{12... | collective-permute-start | bytes 497672 | tf_op jit(solution)/shard_map/ppermute | solution.py:301
  83.1 12.7 %collective-permute-start.4 = (bf16[72,1152]{1,0:T(8,128)(2,1)S(1)}, bf16[72,1152]{1,0:T(8,128)(2,1)S(1)}, u32[]{:S(2)}, u32[]{:S(2)}) collective-permute-start(bf16[72,1152]{1,0:T(8,128)(2,1)S(1)} %get-tuple-element.17.w0), channel_id=1, source_target_pairs={{0,6},{2,4},{4,2},{6,0},{1,7},{3,5},{5,3},{7,1},{8,14},{10,12},{12... | collective-permute-start | bytes 497672 | tf_op jit(solution)/shard_map/ppermute | solution.py:301
  85.5 1.6 copy-start.1
  95.5 15.9 %copy-start.7 = (f32[2,3,1152]{2,0,1:T(2,128)S(1)}, f32[2,3,1152]{2,0,1:T(2,128)}, u32[]{:S(2)}) copy-start(f32[2,3,1152]{2,0,1:T(2,128)} %param.11) | copy-start | bytes 82948
  95.5 24.2 %copy-start.3 = (bf16[1,56,1152]{2,1,0:T(8,128)(2,1)S(1)}, bf16[1,56,1152]{2,1,0:T(8,128)(2,1)}, u32[]{:S(2)}) copy-start(bf16[1,56,1152]{2,1,0:T(8,128)(2,1)} %param.8) | copy-start | bytes 387076
  95.8 9.5 %all-to-all-start.2 = ((bf16[4,4,56,72]{3,2,1,0:T(8,128)(2,1)}), bf16[4,4,56,72]{3,2,1,0:T(8,128)(2,1)S(1)}, u32[]{:S(2)}, u32[]{:S(2)}) async-start(bf16[4,4,56,72]{3,2,1,0:T(8,128)(2,1)} %spatial.1), calls=%async_computation.2 | async-start | bytes 458752 | tf_op jit(solution)/shard_map/all_to_all | solution.py:342
  107.4 12.3 %all-to-all-start.3 = ((bf16[4,56,1152]{2,1,0:T(8,128)(2,1)}), bf16[4,56,1152]{2,1,0:T(8,128)(2,1)S(1)}, u32[]{:S(2)}, u32[]{:S(2)}) async-start(bf16[4,56,1152]{2,1,0:T(8,128)(2,1)} %heads_out.1), calls=%async_computation.3 | async-start | bytes 1032192 | tf_op jit(solution)/shard_map/all_to_all | solution.py:344
  111.5 35.8 %collective-permute-start.5 = (bf16[216,1152]{1,0:T(8,128)(2,1)S(1)}, bf16[216,1152]{1,0:T(8,128)(2,1)S(1)}, u32[]{:S(2)}, u32[]{:S(2)}) collective-permute-start(bf16[216,1152]{1,0:T(8,128)(2,1)S(1)} %bitcast.33), channel_id=1, source_target_pairs={{0,32},{32,0},{1,33},{33,1},{2,34},{34,2},{3,35},{35,3},{4,36},{36... | collective-permute-start | bytes 1493000 | tf_op jit(solution)/shard_map/ppermute | solution.py:348
  120.0 39.0 %copy-start.9 = (s32[16]{0:T(128)S(1)}, s32[16]{0:T(128)}, u32[]{:S(2)}) copy-start(s32[16]{0:T(128)} %constant.91) | copy-start | bytes 196
  149.2 11.7 %collective-permute-start.6 = (bf16[3,448,72]{2,1,0:T(8,128)(2,1)S(1)}, bf16[3,448,72]{2,1,0:T(8,128)(2,1)S(1)}, u32[]{:S(2)}, u32[]{:S(2)}) collective-permute-start(bf16[3,448,72]{2,1,0:T(8,128)(2,1)S(1)} %qkv.5), channel_id=1, source_target_pairs={{0,32},{32,0},{1,33},{33,1},{2,34},{34,2},{3,35},{35,3},{4,36},{36... | collective-permute-start | bytes 580616 | tf_op jit(solution)/shard_map/ppermute | solution.py:350
  164.6 20.1 %all-to-all-start.4 = ((bf16[16,32,128]{2,1,0:T(8,128)(2,1)}), bf16[16,32,128]{2,1,0:T(8,128)(2,1)S(1)}, u32[]{:S(2)}, u32[]{:S(2)}) async-start(bf16[16,32,128]{2,1,0:T(8,128)(2,1)} %temporal.1), calls=%async_computation.4 | async-start | bytes 262144 | tf_op jit(solution)/shard_map/all_to_all | solution.py:356
  184.7 1.8 copy-start
Sparse Core Ops, SparseCore 0:
  10.4 64.6 all-gather.5
  96.0 58.4 all-gather.7

commit v5 on v4

--- a/solution.py
+++ b/solution.py
@@ -17,6 +17,7 @@
 QBLOCK = 4 * ROWS
 NEG = -1e30
 VMEM_LIMIT = 20 * 1024 * 1024
+VMEM_ALL = 60 * 1024 * 1024
 NT = (((1,), (1,)), ((), ()))
 
 
@@ -36,13 +37,15 @@
     return lax.dot_general(a, b, dims, preferred_element_type=jnp.float32)
 
 
-def call(kernel, args, out_shape, name, scratch=(), flops=0, moved=0, trans=0, grid=None, specs=None):
+def call(
+    kernel, args, out_shape, name, scratch=(), flops=0, moved=0, trans=0, grid=None, specs=None, limit=VMEM_LIMIT
+):
     extra = {} if grid is None else {"grid": grid, "in_specs": specs[0], "out_specs": specs[1]}
     return pl.pallas_call(
         kernel,
         out_shape=out_shape,
         scratch_shapes=list(scratch),
-        compiler_params=pltpu.CompilerParams(vmem_limit_bytes=VMEM_LIMIT),
+        compiler_params=pltpu.CompilerParams(vmem_limit_bytes=limit),
         cost_estimate=pl.CostEstimate(flops=flops, bytes_accessed=moved, transcendentals=trans),
         name=name,
         **extra,
@@ -180,36 +183,41 @@
     return call(combine_kernel, (part, resid, mod), (out, out), "combine", moved=2_500_000)
 
 
-def project_kernel(heads, attn, w, resid, gate, out, attn_s):
-    @pl.when(pl.program_id(0) == 0)
-    def _():
-        for g in range(PLANE):
-            piece = attn[heads[g]].astype(jnp.float32)
-            at = g * HEAD_DIM
-            attn_s[:32, at : at + 72] = piece[:, :72]
-            attn_s[32:, at : at + 56] = piece[:24, 72:]
-            for j in range(3):
-                attn_s[32 + 8 * j : 40 + 8 * j, at + 56 : at + 72] = piece[24:, 72 + 16 * j : 88 + 16 * j]
-
-    summed = dot(attn_s[...].astype(jnp.bfloat16), w[...])
+def project_kernel(heads, attn, w, resid, gate, out, attn_s, w_s, sems):
+    part = w.shape[0] // 3
+    pieces = [pl.ds(i * part, part) for i in range(3)]
+    copies = [pltpu.make_async_copy(w.at[at], w_s.at[at], sems.at[i]) for i, at in enumerate(pieces)]
+    for copy in copies:
+        copy.start()
+    for g in range(PLANE):
+        piece = attn[heads[g]].astype(jnp.float32)
+        at = g * HEAD_DIM
+        attn_s[:32, at : at + 72] = piece[:, :72]
+        attn_s[32:, at : at + 56] = piece[:24, 72:]
+        for j in range(3):
+            attn_s[32 + 8 * j : 40 + 8 * j, at + 56 : at + 72] = piece[24:, 72 + 16 * j : 88 + 16 * j]
+    summed = jnp.zeros(out.shape, jnp.float32)
+    for copy, at in zip(copies, pieces):
+        copy.wait()
+        summed = summed + dot(attn_s[:, at].astype(jnp.bfloat16), w_s[at])
     out[...] = (resid[...].astype(jnp.float32) + gate[...] * summed).astype(jnp.bfloat16)
 
 
 def project(heads, attn, w, resid, gate):
     out = jax.ShapeDtypeStruct(resid.shape, jnp.bfloat16)
-    part = w.shape[1] // 3
-    columns = lambda a: pl.BlockSpec((a.shape[0], part), lambda i: (0, i))
+    vmem = pl.BlockSpec(memory_space=pltpu.VMEM)
     specs = (
-        [
-            pl.BlockSpec(memory_space=pltpu.SMEM),
-            pl.BlockSpec(attn.shape, lambda i: (0, 0, 0)),
-            columns(w), columns(resid), columns(gate),
-        ],
-        columns(resid),
+        [pl.BlockSpec(memory_space=pltpu.SMEM), vmem, pl.BlockSpec(memory_space=pl.ANY), vmem, vmem],
+        vmem,
+    )
+    scratch = (
+        pltpu.VMEM(resid.shape, jnp.float32),
+        pltpu.VMEM(w.shape, w.dtype),
+        pltpu.SemaphoreType.DMA((3,)),
     )
     return call(
-        project_kernel, (heads, attn, w, resid, gate), out, "project", (pltpu.VMEM(resid.shape, jnp.float32),),
-        flops=150_000_000, moved=3_200_000, grid=(3,), specs=specs,
+        project_kernel, (heads, attn, w, resid, gate), out, "project", scratch, flops=150_000_000,
+        moved=3_200_000, grid=(), specs=specs, limit=VMEM_ALL,
     )
 
 
@@ -335,11 +343,12 @@
     colp = jnp.repeat((lax.iota(jnp.int32, 2 * PLANE) - 2 * turn(z)) % (2 * PLANE), ROWS)[None, :]
     w_heads = xor_gather(rows[3 * HEAD_DIM - 0 : 4 * HEAD_DIM], "y")
     attn = spatial(fresh, old.reshape(2 * PLANE, 64, 128), rowp, colp)
-    attn, w_heads, w_last, w_own = lax.optimization_barrier(
-        (attn, w_heads, w_last, w_qkv[1].reshape(3 * HEAD_DIM, width))
+    attn, w_heads = lax.optimization_barrier((attn, w_heads))
+    attn = lax.all_to_all(attn, "y", 0, 0, tiled=True)
+    attn, w_last, w_own = lax.optimization_barrier(
+        (attn, w_last, w_qkv[1].reshape(3 * HEAD_DIM, width))
     )
     w_last = lax.all_gather(w_last, ("x", "y"), axis=0).reshape(width, width)
-    attn = lax.all_to_all(attn, "y", 0, 0, tiled=True)
     part = heads_out(y ^ blocks[:4], attn.reshape(4, QBLOCK, HEAD_DIM), w_heads)
     part = lax.all_to_all(part, "x", 0, 0, tiled=True)
     middle, hmod = combine(part, stream[0], jnp.concatenate([modulation[0, 2:], modulation[1, :2]]))
@@ -351,7 +360,6 @@
     own = qkv(toks, w_own, qk_gain[1])
     shape = (3, 8, ROWS, HEAD_DIM)
     place = 2 * jnp.array(LOOP * 2, jnp.int32) + (c ^ (blocks // 8))
-    other, w_last = lax.optimization_barrier((other, w_last))
     attn = temporal(place, own.reshape(shape), other.reshape(shape))
     attn = lax.all_to_all(attn, ("z", "c"), 0, 0, tiled=True)
     out = project((blocks + turn(z)) % 16, attn, w_last, middle, modulation[1, 2:])

time: 197 us -> 194 us (0.985)
  blocking collectives: 27.3 us -> 34.3 us
  waiting for transfers between devices: 46.9 us -> 40.3 us
  starting transfers between devices: 75.8 us -> 72.3 us
    all_to_all x0 -> x1, blocking collectives: none -> 8.93 us  [local(): attn = lax.all_to_all(attn, 'y', 0, 0, tiled=True)]
    all_to_all x1 -> x0, waiting for transfers between devices: 5.8 us -> none  [local(): attn = lax.all_to_all(attn, 'y', 0, 0, tiled=True)]
    all_to_all x1 -> x0, starting transfers between devices: 3.68 us -> none  [local(): attn = lax.all_to_all(attn, 'y', 0, 0, tiled=True)]
    unnamed x22 -> x24, local copies, waits for them, and re-layouts: 4.27 us -> 3.18 us
  transfers between devices with their start and end apart: 14 -> 13, of which waited for: 6 -> 5; matrix products, arithmetic and copies ran while one was open for 2% -> 2% of each run, Pallas kernels for 8% -> 10%
where the time goes in v5:
time: 194 us; the launch traced here: 193 us
  starting transfers between devices  72.3 us (37%)
  waiting for transfers between devices  40.3 us (21%)
  blocking collectives  34.3 us (18%)
  Pallas kernels  24 us (12%)
  between operations  13.8 us (7%)
  local copies, waits for them, and re-layouts  6.81 us (4%)
  other arithmetic  1.94 us (1%)
    all_gather x1, blocking collectives, line_gather(): return lax.all_gather(block, 'z', axis=0, axis_index_groups=[list(LOOP)])  25.4 us
    pallas_call x10, Pallas kernels, call(): pl.pallas_call(kernel, out_shape=out_shape, scratch_shapes=list(scratch),...  24 us
    all_to_all x1, waiting for transfers between devices, local(): old = lax.all_to_all(chunk, ('z', 'c', 'h'), 0, 0, tiled=True)  22.3 us
    all_to_all x1, starting transfers between devices, local(): old = lax.all_to_all(chunk, ('z', 'c', 'h'), 0, 0, tiled=True)  19.9 us
    all_to_all x1, starting transfers between devices, local(): lax.all_to_all(old.reshape(16, 2, 64, 128), AXES, 0, 0, axis_index_groups...  14 us
    all_to_all x1, waiting for transfers between devices, local(): attn = lax.all_to_all(attn, ('z', 'c'), 0, 0, tiled=True)  11.5 us
    ppermute x1, starting transfers between devices, local(): other = lax.ppermute(sib, 'c', SWAP)  10.5 us
    ppermute x3, starting transfers between devices, xor_gather(): lax.ppermute(block, axis, [(i, i ^ k) for i in range(4)])  9.57 us
  transfers between devices with their start and end apart: 13, of which 5 were waited for; matrix products, arithmetic and copies ran while one was open for 2% of the time, Pallas kernels for 10%

profile of v5, /device:TPU:1, one launch (start us, length us, event | category | flops | bytes accessed | tf_op | source)
XLA Modules:
  0.0 193.5 jit_solution(8244326958278608775)
XLA Ops:
  6.5 0.8 slice.44
  7.3 0.9 copy-done.1
  8.2 0.9 modulate.1
  9.1 0.0 all-gather.6.cloned.1.call-update
  9.1 1.0 slice_bitcast_fusion.1
  10.2 0.1 fusion.4
  10.3 0.1 pad_maximum_fusion
  10.3 0.8 collective-permute-start
  11.2 1.7 pack.1
  12.9 19.9 %all-to-all-start = ((bf16[32,64,128]{2,1,0:T(8,128)(2,1)}), bf16[32,64,128]{2,1,0:T(8,128)(2,1)}, u32[]{:S(2)}, u32[]{:S(2)}) async-start(bf16[32,64,128]{2,1,0:T(8,128)(2,1)} %bitcast.7), calls=%async_computation | async-start | bytes 1048576 | tf_op jit(solution)/shard_map/all_to_all | solution.py:329
  32.9 2.2 %collective-permute-start.1 = (bf16[360,1152]{1,0:T(8,128)(2,1)S(1)}, bf16[360,1152]{1,0:T(8,128)(2,1)}, u32[]{:S(2)}, u32[]{:S(2)}) collective-permute-start(bf16[360,1152]{1,0:T(8,128)(2,1)S(1)} %collective-permute-done), channel_id=1, source_target_pairs={{0,32},{32,0},{1,33},{33,1},{2,34},{34,2},{3,35},{35,3},{4,36},{36... | collective-permute-start | bytes 2488328 | tf_op jit(solution)/shard_map/ppermute | solution.py:333
  35.1 0.1 broadcast_in_dim.10
  35.2 0.1 broadcast_in_dim_reshape.7.colp
  35.3 1.9 collective-permute-done.1
  37.3 1.3 broadcast_select_fusion
  38.6 22.3 %all-to-all-done = bf16[32,64,128]{2,1,0:T(8,128)(2,1)} async-done(((bf16[32,64,128]{2,1,0:T(8,128)(2,1)}), bf16[32,64,128]{2,1,0:T(8,128)(2,1)}, u32[]{:S(2)}, u32[]{:S(2)}) %all-to-all-start) | async-done | bytes 524320 | tf_op jit(solution)/shard_map/all_to_all | solution.py:329
  60.8 14.0 %all-to-all-start.1 = ((bf16[16,2,64,128]{3,2,1,0:T(8,128)(2,1)}), bf16[16,2,64,128]{3,2,1,0:T(8,128)(2,1)S(1)}, u32[]{:S(2)}, u32[]{:S(2)}) async-start(bf16[16,2,64,128]{3,2,1,0:T(8,128)(2,1)} %bitcast.8), calls=%async_computation.1 | async-start | bytes 1048576 | tf_op jit(solution)/shard_map/all_to_all | solution.py:337
  74.8 0.0 all-gather.8.cloned.1.call-start
  74.9 0.7 fusion.5
  75.6 3.3 %collective-permute-start.2 = (bf16[72,1152]{1,0:T(8,128)(2,1)S(1)}, bf16[72,1152]{1,0:T(8,128)(2,1)S(1)}, u32[]{:S(2)}, u32[]{:S(2)}) collective-permute-start(bf16[72,1152]{1,0:T(8,128)(2,1)S(1)} %get-tuple-element.17.w0), channel_id=1, source_target_pairs={{0,2},{2,0},{4,6},{6,4},{1,3},{3,1},{5,7},{7,5},{8,10},{10,8},{12,... | collective-permute-start | bytes 497672 | tf_op jit(solution)/shard_map/ppermute | solution.py:309
  78.8 4.3 %collective-permute-start.3 = (bf16[72,1152]{1,0:T(8,128)(2,1)S(1)}, bf16[72,1152]{1,0:T(8,128)(2,1)S(1)}, u32[]{:S(2)}, u32[]{:S(2)}) collective-permute-start(bf16[72,1152]{1,0:T(8,128)(2,1)S(1)} %get-tuple-element.17.w0), channel_id=1, source_target_pairs={{0,4},{2,6},{4,0},{6,2},{1,5},{3,7},{5,1},{7,3},{8,12},{10,14},{12... | collective-permute-start | bytes 497672 | tf_op jit(solution)/shard_map/ppermute | solution.py:309
  83.1 2.0 %collective-permute-start.4 = (bf16[72,1152]{1,0:T(8,128)(2,1)S(1)}, bf16[72,1152]{1,0:T(8,128)(2,1)S(1)}, u32[]{:S(2)}, u32[]{:S(2)}) collective-permute-start(bf16[72,1152]{1,0:T(8,128)(2,1)S(1)} %get-tuple-element.17.w0), channel_id=1, source_target_pairs={{0,6},{2,4},{4,2},{6,0},{1,7},{3,5},{5,3},{7,1},{8,14},{10,12},{12... | collective-permute-start | bytes 497672 | tf_op jit(solution)/shard_map/ppermute | solution.py:309
  85.2 0.1 broadcast_in_dim.9
  85.2 0.2 broadcast_in_dim_reshape.8.rowp
  85.5 0.0 all-gather.6.cloned.1.call-done
  85.5 1.6 copy-done
  87.1 2.7 %qkv.3.q = bf16[3,896,72]{2,1,0:T(8,128)(2,1)S(1)} custom-call(bf16[4,224,1152]{2,1,0:T(8,128)(2,1)S(1)} %bitcast.32, bf16[216,1152]{1,0:T(8,128)(2,1)S(1)} %slice.57.w, f32[2,72]{1,0:T(2,128)S(1)} %get-tuple-element.34.gain), custom_call_target="tpu_custom_call" | custom-call | flops 445906944 | bytes 3000000 | tf_op jit(solution)/shard_map/qkv/pallas_call | solution.py:44
  89.8 5.0 %spatial.1 = bf16[4,4,56,72]{3,2,1,0:T(8,128)(2,1)S(1)} custom-call(bf16[3,896,72]{2,1,0:T(8,128)(2,1)S(1)} %qkv.3.q, bf16[32,64,128]{2,1,0:T(8,128)(2,1)S(1)} %bitcast.37, s32[896,1]{1,0:T(8,128)S(1)} %broadcast_in_dim_reshape.8.rowp, s32[1,1792]{1,0:T(1,128)S(1)} %broadcast_in_dim_reshape.7.colp), custom_call_target="tpu_custom_call" | custom-call | flops 600000000 | bytes 2000000 | tf_op jit(solution)/shard_map/spatial/pallas_call | solution.py:44
  94.8 1.0 collective-permute-done.4.w3
  95.8 8.9 %all_to_all.25 = bf16[4,4,56,72]{3,2,1,0:T(8,128)(2,1)S(1)} all-to-all(bf16[4,4,56,72]{3,2,1,0:T(8,128)(2,1)S(1)} %spatial.1), channel_id=1, replica_groups=mesh['z'=8,'c'=2,'x'=4,'y'=4,'h'=2] {'y'}, dimensions={0} | all-to-all | bytes 258048 | tf_op jit(solution)/shard_map/all_to_all | solution.py:347
  104.7 0.0 all-gather.8.cloned.1.call-update
  104.8 2.1 %heads_out.1 = bf16[4,56,1152]{2,1,0:T(8,128)(2,1)} custom-call(s32[4]{0:T(128)S(1)} %slice_xor_fusion.place, bf16[4,224,72]{2,1,0:T(8,128)(2,1)S(1)} %bitcast.36, bf16[72,1152]{1,0:T(8,128)(2,1)S(1)} %get-tuple-element.17.w0, bf16[72,1152]{1,0:T(8,128)(2,1)S(1)} %collective-permute-done.2.w1, bf16[72,1152]{1,0:T(8,128)(2,1)S(1)} %collective-permute-done.3.w2, ...), custom_call_target="tpu_custom_call" | custom-call | flops 150000000 | bytes 1200000 | tf_op jit(solution)/shard_map/heads_out/pallas_call | solution.py:44
  106.9 4.0 %all-to-all-start.3 = ((bf16[4,56,1152]{2,1,0:T(8,128)(2,1)}), bf16[4,56,1152]{2,1,0:T(8,128)(2,1)S(1)}, u32[]{:S(2)}, u32[]{:S(2)}) async-start(bf16[4,56,1152]{2,1,0:T(8,128)(2,1)} %heads_out.1), calls=%async_computation.3 | async-start | bytes 1032192 | tf_op jit(solution)/shard_map/all_to_all | solution.py:353
  110.8 0.6 slice_bitcast_fusion.2
  111.5 3.4 %collective-permute-start.5 = (bf16[216,1152]{1,0:T(8,128)(2,1)S(1)}, bf16[216,1152]{1,0:T(8,128)(2,1)S(1)}, u32[]{:S(2)}, u32[]{:S(2)}) collective-permute-start(bf16[216,1152]{1,0:T(8,128)(2,1)S(1)} %bitcast.33), channel_id=1, source_target_pairs={{0,32},{32,0},{1,33},{33,1},{2,34},{34,2},{3,35},{35,3},{4,36},{36... | collective-permute-start | bytes 1493000 | tf_op jit(solution)/shard_map/ppermute | solution.py:357
  114.9 3.6 %all-to-all-done.3.part = bf16[4,56,1152]{2,1,0:T(8,128)(2,1)S(1)} async-done(((bf16[4,56,1152]{2,1,0:T(8,128)(2,1)}), bf16[4,56,1152]{2,1,0:T(8,128)(2,1)S(1)}, u32[]{:S(2)}, u32[]{:S(2)}) %all-to-all-start.3) | async-done | bytes 516128 | tf_op jit(solution)/shard_map/all_to_all | solution.py:353
  118.5 0.3 combine.1
  118.8 0.0 copy-start.10
  118.8 25.4 %all-gather.1 = bf16[448,1152]{1,0:T(8,128)(2,1)S(1)} all-gather(bf16[56,1152]{1,0:T(8,128)(2,1)S(1)} %get-tuple-element.21), channel_id=3, replica_groups={{0,128,256,384,448,320,192,64},{1,129,257,385,449,321,193,65},{2,130,25..., dimensions={0}, use_global_device_ids=true | all-gather | bytes 1161216 | tf_op jit(solution)/shard_map/all_gather | solution.py:316
  144.2 1.9 qkv.5
  146.1 10.5 %collective-permute-start.6 = (bf16[3,448,72]{2,1,0:T(8,128)(2,1)S(1)}, bf16[3,448,72]{2,1,0:T(8,128)(2,1)S(1)}, u32[]{:S(2)}, u32[]{:S(2)}) collective-permute-start(bf16[3,448,72]{2,1,0:T(8,128)(2,1)S(1)} %qkv.5), channel_id=1, source_target_pairs={{0,32},{32,0},{1,33},{33,1},{2,34},{34,2},{3,35},{35,3},{4,36},{36... | collective-permute-start | bytes 580616 | tf_op jit(solution)/shard_map/ppermute | solution.py:359
  156.7 1.9 qkv.4
  158.6 3.7 %temporal.1 = bf16[16,32,128]{2,1,0:T(8,128)(2,1)} custom-call(s32[16]{0:T(128)S(1)} %fusion.1.place, bf16[3,8,56,72]{3,2,1,0:T(8,128)(2,1)S(1)} %bitcast.35, bf16[3,8,56,72]{3,2,1,0:T(8,128)(2,1)S(1)} %bitcast.40), custom_call_target="tpu_custom_call" | custom-call | flops 50000000 | bytes 1000000 | tf_op jit(solution)/shard_map/temporal/pallas_call | solution.py:44
  162.3 7.8 %all-to-all-start.4 = ((bf16[16,32,128]{2,1,0:T(8,128)(2,1)}), bf16[16,32,128]{2,1,0:T(8,128)(2,1)S(1)}, u32[]{:S(2)}, u32[]{:S(2)}) async-start(bf16[16,32,128]{2,1,0:T(8,128)(2,1)} %temporal.1), calls=%async_computation.4 | async-start | bytes 262144 | tf_op jit(solution)/shard_map/all_to_all | solution.py:364
  170.1 0.5 and_select_fusion.2.heads
  170.6 11.5 %all-to-all-done.4.attn = bf16[16,32,128]{2,1,0:T(8,128)(2,1)S(1)} async-done(((bf16[16,32,128]{2,1,0:T(8,128)(2,1)}), bf16[16,32,128]{2,1,0:T(8,128)(2,1)S(1)}, u32[]{:S(2)}, u32[]{:S(2)}) %all-to-all-start.4) | async-done | bytes 131104 | tf_op jit(solution)/shard_map/all_to_all | solution.py:364
  182.1 0.6 copy-done.7
  182.8 3.9 %project.1 = bf16[56,1152]{1,0:T(8,128)(2,1)} custom-call(s32[16]{0:T(128)} %and_select_fusion.2.heads, bf16[16,32,128]{2,1,0:T(8,128)(2,1)} %copy-done.7, bf16[1152,1152]{1,0:T(8,128)(2,1)} %all-gather.8.cloned.1.call-done.w, bf16[56,1152]{1,0:T(8,128)(2,1)} %copy-done.5, f32[1,1152]{1,0:T(1,128)} %get-tuple-element.31.gate), custom_call_target="tpu_custom_call" | custom-call | flops 150000000 | bytes 3200000 | tf_op jit(solution)/shard_map/project/pallas_call | solution.py:44
  (37 shorter events, 0.2 us)
Async XLA Ops:
  6.5 79.0 %all-gather.6.cloned.1.call-start = ((), (), s32[]{:S(2)}) async-start(), calls=%async_computation.5 | async-start | bytes 2193408 | tf_op jit(solution)/shard_map/all_gather | solution.py:326
  7.3 0.9 copy-start.1
  8.2 1.9 copy-start.6
  10.2 1.1 copy-start.3
  10.2 1.1 copy-start.4
  10.3 25.1 %copy-start.9 = (f32[2,2,72]{2,1,0:T(2,128)S(1)}, f32[2,2,72]{2,1,0:T(2,128)}, u32[]{:S(2)}) copy-start(f32[2,2,72]{2,1,0:T(2,128)} %param.14) | copy-start | bytes 3460
  10.3 22.5 %collective-permute-start = (bf16[360,1152]{1,0:T(8,128)(2,1)S(1)}, bf16[360,1152]{1,0:T(8,128)(2,1)S(1)}, u32[]{:S(2)}, u32[]{:S(2)}) collective-permute-start(bf16[360,1152]{1,0:T(8,128)(2,1)S(1)} %pad_maximum_fusion), channel_id=1, source_target_pairs={{0,0},{320,64},{128,128},{449,192},{256,256},{65,320},{384,384},{1... | collective-permute-start | bytes 2488328 | tf_op jit(solution)/shard_map/ppermute | solution.py:332
  12.9 47.9 %all-to-all-start = ((bf16[32,64,128]{2,1,0:T(8,128)(2,1)}), bf16[32,64,128]{2,1,0:T(8,128)(2,1)}, u32[]{:S(2)}, u32[]{:S(2)}) async-start(bf16[32,64,128]{2,1,0:T(8,128)(2,1)} %bitcast.7), calls=%async_computation | async-start | bytes 1048576 | tf_op jit(solution)/shard_map/all_to_all | solution.py:329
  32.9 4.4 %collective-permute-start.1 = (bf16[360,1152]{1,0:T(8,128)(2,1)S(1)}, bf16[360,1152]{1,0:T(8,128)(2,1)}, u32[]{:S(2)}, u32[]{:S(2)}) collective-permute-start(bf16[360,1152]{1,0:T(8,128)(2,1)S(1)} %collective-permute-done), channel_id=1, source_target_pairs={{0,32},{32,0},{1,33},{33,1},{2,34},{34,2},{3,35},{35,3},{4,36},{36... | collective-permute-start | bytes 2488328 | tf_op jit(solution)/shard_map/ppermute | solution.py:333
  60.8 28.9 %all-to-all-start.1 = ((bf16[16,2,64,128]{3,2,1,0:T(8,128)(2,1)}), bf16[16,2,64,128]{3,2,1,0:T(8,128)(2,1)S(1)}, u32[]{:S(2)}, u32[]{:S(2)}) async-start(bf16[16,2,64,128]{3,2,1,0:T(8,128)(2,1)} %bitcast.8), calls=%async_computation.1 | async-start | bytes 1048576 | tf_op jit(solution)/shard_map/all_to_all | solution.py:337
  74.8 107.3 %all-gather.8.cloned.1.call-start = ((), (), s32[]{:S(2)}) async-start(), calls=%async_computation.6 | async-start | bytes 2820096 | tf_op jit(solution)/shard_map/all_gather | solution.py:351
  75.6 19.3 %collective-permute-start.2 = (bf16[72,1152]{1,0:T(8,128)(2,1)S(1)}, bf16[72,1152]{1,0:T(8,128)(2,1)S(1)}, u32[]{:S(2)}, u32[]{:S(2)}) collective-permute-start(bf16[72,1152]{1,0:T(8,128)(2,1)S(1)} %get-tuple-element.17.w0), channel_id=1, source_target_pairs={{0,2},{2,0},{4,6},{6,4},{1,3},{3,1},{5,7},{7,5},{8,10},{10,8},{12,... | collective-permute-start | bytes 497672 | tf_op jit(solution)/shard_map/ppermute | solution.py:309
  78.8 16.0 %collective-permute-start.3 = (bf16[72,1152]{1,0:T(8,128)(2,1)S(1)}, bf16[72,1152]{1,0:T(8,128)(2,1)S(1)}, u32[]{:S(2)}, u32[]{:S(2)}) collective-permute-start(bf16[72,1152]{1,0:T(8,128)(2,1)S(1)} %get-tuple-element.17.w0), channel_id=1, source_target_pairs={{0,4},{2,6},{4,0},{6,2},{1,5},{3,7},{5,1},{7,3},{8,12},{10,14},{12... | collective-permute-start | bytes 497672 | tf_op jit(solution)/shard_map/ppermute | solution.py:309
  83.1 12.7 %collective-permute-start.4 = (bf16[72,1152]{1,0:T(8,128)(2,1)S(1)}, bf16[72,1152]{1,0:T(8,128)(2,1)S(1)}, u32[]{:S(2)}, u32[]{:S(2)}) collective-permute-start(bf16[72,1152]{1,0:T(8,128)(2,1)S(1)} %get-tuple-element.17.w0), channel_id=1, source_target_pairs={{0,6},{2,4},{4,2},{6,0},{1,7},{3,5},{5,3},{7,1},{8,14},{10,12},{12... | collective-permute-start | bytes 497672 | tf_op jit(solution)/shard_map/ppermute | solution.py:309
  85.5 1.6 copy-start
  94.8 16.0 %copy-start.8 = (f32[2,3,1152]{2,0,1:T(2,128)S(1)}, f32[2,3,1152]{2,0,1:T(2,128)}, u32[]{:S(2)}) copy-start(f32[2,3,1152]{2,0,1:T(2,128)} %param.11) | copy-start | bytes 82948
  94.8 23.7 %copy-start.2 = (bf16[1,56,1152]{2,1,0:T(8,128)(2,1)S(1)}, bf16[1,56,1152]{2,1,0:T(8,128)(2,1)}, u32[]{:S(2)}) copy-start(bf16[1,56,1152]{2,1,0:T(8,128)(2,1)} %param.8) | copy-start | bytes 387076
  106.9 11.6 %all-to-all-start.3 = ((bf16[4,56,1152]{2,1,0:T(8,128)(2,1)}), bf16[4,56,1152]{2,1,0:T(8,128)(2,1)S(1)}, u32[]{:S(2)}, u32[]{:S(2)}) async-start(bf16[4,56,1152]{2,1,0:T(8,128)(2,1)} %heads_out.1), calls=%async_computation.3 | async-start | bytes 1032192 | tf_op jit(solution)/shard_map/all_to_all | solution.py:353
  111.5 32.8 %collective-permute-start.5 = (bf16[216,1152]{1,0:T(8,128)(2,1)S(1)}, bf16[216,1152]{1,0:T(8,128)(2,1)S(1)}, u32[]{:S(2)}, u32[]{:S(2)}) collective-permute-start(bf16[216,1152]{1,0:T(8,128)(2,1)S(1)} %bitcast.33), channel_id=1, source_target_pairs={{0,32},{32,0},{1,33},{33,1},{2,34},{34,2},{3,35},{35,3},{4,36},{36... | collective-permute-start | bytes 1493000 | tf_op jit(solution)/shard_map/ppermute | solution.py:357
  118.8 39.8 %copy-start.5 = (bf16[56,1152]{1,0:T(8,128)(2,1)}, bf16[56,1152]{1,0:T(8,128)(2,1)S(1)}, u32[]{:S(2)}) copy-start(bf16[56,1152]{1,0:T(8,128)(2,1)S(1)} %get-tuple-element.24.resid) | copy-start | bytes 387076
  118.8 37.9 %copy-start.10 = (s32[16]{0:T(128)S(1)}, s32[16]{0:T(128)}, u32[]{:S(2)}) copy-start(s32[16]{0:T(128)} %constant.91) | copy-start | bytes 196
  146.1 12.5 %collective-permute-start.6 = (bf16[3,448,72]{2,1,0:T(8,128)(2,1)S(1)}, bf16[3,448,72]{2,1,0:T(8,128)(2,1)S(1)}, u32[]{:S(2)}, u32[]{:S(2)}) collective-permute-start(bf16[3,448,72]{2,1,0:T(8,128)(2,1)S(1)} %qkv.5), channel_id=1, source_target_pairs={{0,32},{32,0},{1,33},{33,1},{2,34},{34,2},{3,35},{35,3},{4,36},{36... | collective-permute-start | bytes 580616 | tf_op jit(solution)/shard_map/ppermute | solution.py:359
  162.3 19.8 %all-to-all-start.4 = ((bf16[16,32,128]{2,1,0:T(8,128)(2,1)}), bf16[16,32,128]{2,1,0:T(8,128)(2,1)S(1)}, u32[]{:S(2)}, u32[]{:S(2)}) async-start(bf16[16,32,128]{2,1,0:T(8,128)(2,1)} %temporal.1), calls=%async_computation.4 | async-start | bytes 262144 | tf_op jit(solution)/shard_map/all_to_all | solution.py:364
  182.1 0.6 copy-start.7
Sparse Core Ops, SparseCore 0:
  10.4 64.6 all-gather.5
  104.9 57.4 all-gather.7

commit v6 on v5

--- a/solution.py
+++ b/solution.py
@@ -154,9 +154,9 @@
 
 
 def heads_out_kernel(place, attn, w0, w1, w2, w3, out):
+    total = sum(dot(attn[place[k]], w[...]) for k, w in enumerate((w0, w1, w2, w3)))
     for i in range(4):
-        total = sum(dot(attn[place[k], i * ROWS : (i + 1) * ROWS], w[w.shape[0] - HEAD_DIM :]) for k, w in enumerate((w0, w1, w2, w3)))
-        out[i] = total.astype(jnp.bfloat16)
+        out[i] = total[i * ROWS : (i + 1) * ROWS].astype(jnp.bfloat16)
 
 
 def heads_out(place, attn, ws):
@@ -301,12 +301,9 @@
 SWAP = [(0, 1), (1, 0)]
 
 
-def xor_gather(block, axis):
-    return [block] + [lax.ppermute(block, axis, [(i, i ^ k) for i in range(4)]) for k in (1, 2, 3)]
-
-
-def xor_gather(block, axis):
-    return [block] + [lax.ppermute(block, axis, [(i, i ^ k) for i in range(4)]) for k in (1, 2, 3)]
+def xor_gather(blocks, axis):
+    send = lambda k: lax.ppermute(blocks[k], axis, [(i, i ^ k) for i in range(4)])
+    return [blocks[0]] + [send(k) for k in (1, 2, 3)]
 
 
 LOOP = (0, 2, 4, 6, 7, 5, 3, 1)
@@ -338,10 +335,11 @@
         old.reshape(16, 2, 64, 128), AXES, 0, 0, axis_index_groups=rolled(), tiled=True
     )
 
+    toks, late = lax.optimization_barrier((toks, w_head))
+    w_heads = xor_gather((w_head, w_head, w_head, late), "y")
     fresh = qkv(toks, w_col, qk_gain[0])
     rowp = jnp.repeat(2 * blocks + h, ROWS)[:, None]
     colp = jnp.repeat((lax.iota(jnp.int32, 2 * PLANE) - 2 * turn(z)) % (2 * PLANE), ROWS)[None, :]
-    w_heads = xor_gather(rows[3 * HEAD_DIM - 0 : 4 * HEAD_DIM], "y")
     attn = spatial(fresh, old.reshape(2 * PLANE, 64, 128), rowp, colp)
     attn, w_heads = lax.optimization_barrier((attn, w_heads))
     attn = lax.all_to_all(attn, "y", 0, 0, tiled=True)

time: 194 us -> 193 us (level)
  starting transfers between devices: 72.3 us -> 70.3 us
  transfers between devices with their start and end apart: 13 -> 13, of which waited for: 5 -> 5; matrix products, arithmetic and copies ran while one was open for 2% -> 3% of each run, Pallas kernels for 10% -> 10%
where the time goes in v6:
time: 193 us; the launch traced here: 192 us
  starting transfers between devices  70.3 us (36%)
  waiting for transfers between devices  40.2 us (21%)
  blocking collectives  35.5 us (18%)
  Pallas kernels  23.9 us (12%)
  between operations  13.8 us (7%)
  local copies, waits for them, and re-layouts  6.81 us (4%)
  other arithmetic  1.97 us (1%)
    all_gather x1, blocking collectives, line_gather(): return lax.all_gather(block, 'z', axis=0, axis_index_groups=[list(LOOP)])  26.6 us
    pallas_call x10, Pallas kernels, call(): pl.pallas_call(kernel, out_shape=out_shape, scratch_shapes=list(scratch),...  23.9 us
    all_to_all x1, waiting for transfers between devices, local(): old = lax.all_to_all(chunk, ('z', 'c', 'h'), 0, 0, tiled=True)  22.2 us
    all_to_all x1, starting transfers between devices, local(): old = lax.all_to_all(chunk, ('z', 'c', 'h'), 0, 0, tiled=True)  19.9 us
    all_to_all x1, starting transfers between devices, local(): lax.all_to_all(old.reshape(16, 2, 64, 128), AXES, 0, 0, axis_index_groups...  14 us
    all_to_all x1, waiting for transfers between devices, local(): attn = lax.all_to_all(attn, ('z', 'c'), 0, 0, tiled=True)  11.5 us
    ppermute x1, starting transfers between devices, local(): other = lax.ppermute(sib, 'c', SWAP)  9.79 us
    ppermute x3, starting transfers between devices, xor_gather(): lax.ppermute(blocks[k], axis, [(i, i ^ k) for i in range(4)])  9.57 us
  transfers between devices with their start and end apart: 13, of which 5 were waited for; matrix products, arithmetic and copies ran while one was open for 3% of the time, Pallas kernels for 10%

profile of v6, /device:TPU:1, one launch (start us, length us, event | category | flops | bytes accessed | tf_op | source)
XLA Modules:
  0.0 192.4 jit_solution(11361636155411931023)
XLA Ops:
  6.5 0.8 slice.44
  7.3 0.9 copy-done.1
  8.2 0.9 modulate.1
  9.1 0.0 all-gather.6.cloned.1.call-update
  9.1 1.0 slice_bitcast_fusion.1
  10.2 0.1 fusion.4
  10.3 0.1 pad_maximum_fusion
  10.3 0.8 collective-permute-start
  11.2 1.7 pack.1
  12.9 19.9 %all-to-all-start = ((bf16[32,64,128]{2,1,0:T(8,128)(2,1)}), bf16[32,64,128]{2,1,0:T(8,128)(2,1)}, u32[]{:S(2)}, u32[]{:S(2)}) async-start(bf16[32,64,128]{2,1,0:T(8,128)(2,1)} %bitcast.7), calls=%async_computation | async-start | bytes 1048576 | tf_op jit(solution)/shard_map/all_to_all | solution.py:326
  32.9 2.2 %collective-permute-start.1 = (bf16[360,1152]{1,0:T(8,128)(2,1)S(1)}, bf16[360,1152]{1,0:T(8,128)(2,1)}, u32[]{:S(2)}, u32[]{:S(2)}) collective-permute-start(bf16[360,1152]{1,0:T(8,128)(2,1)S(1)} %collective-permute-done), channel_id=1, source_target_pairs={{0,32},{32,0},{1,33},{33,1},{2,34},{34,2},{3,35},{35,3},{4,36},{36... | collective-permute-start | bytes 2488328 | tf_op jit(solution)/shard_map/ppermute | solution.py:330
  35.1 0.1 broadcast_in_dim.10
  35.2 0.1 broadcast_in_dim_reshape.7.colp
  35.3 1.9 collective-permute-done.1
  37.3 1.3 broadcast_select_fusion
  38.6 22.2 %all-to-all-done = bf16[32,64,128]{2,1,0:T(8,128)(2,1)} async-done(((bf16[32,64,128]{2,1,0:T(8,128)(2,1)}), bf16[32,64,128]{2,1,0:T(8,128)(2,1)}, u32[]{:S(2)}, u32[]{:S(2)}) %all-to-all-start) | async-done | bytes 524320 | tf_op jit(solution)/shard_map/all_to_all | solution.py:326
  60.8 14.0 %all-to-all-start.1 = ((bf16[16,2,64,128]{3,2,1,0:T(8,128)(2,1)}), bf16[16,2,64,128]{3,2,1,0:T(8,128)(2,1)S(1)}, u32[]{:S(2)}, u32[]{:S(2)}) async-start(bf16[16,2,64,128]{3,2,1,0:T(8,128)(2,1)} %bitcast.8), calls=%async_computation.1 | async-start | bytes 1048576 | tf_op jit(solution)/shard_map/all_to_all | solution.py:334
  74.8 0.0 all-gather.8.cloned.1.call-start
  74.9 0.7 fusion.5
  75.6 3.3 %collective-permute-start.2 = (bf16[72,1152]{1,0:T(8,128)(2,1)S(1)}, bf16[72,1152]{1,0:T(8,128)(2,1)S(1)}, u32[]{:S(2)}, u32[]{:S(2)}) collective-permute-start(bf16[72,1152]{1,0:T(8,128)(2,1)S(1)} %get-tuple-element.21.w0), channel_id=1, source_target_pairs={{0,2},{2,0},{4,6},{6,4},{1,3},{3,1},{5,7},{7,5},{8,10},{10,8},{12,... | collective-permute-start | bytes 497672 | tf_op jit(solution)/shard_map/ppermute | solution.py:305
  78.8 4.3 %collective-permute-start.3 = (bf16[72,1152]{1,0:T(8,128)(2,1)S(1)}, bf16[72,1152]{1,0:T(8,128)(2,1)S(1)}, u32[]{:S(2)}, u32[]{:S(2)}) collective-permute-start(bf16[72,1152]{1,0:T(8,128)(2,1)S(1)} %get-tuple-element.21.w0), channel_id=1, source_target_pairs={{0,4},{2,6},{4,0},{6,2},{1,5},{3,7},{5,1},{7,3},{8,12},{10,14},{12... | collective-permute-start | bytes 497672 | tf_op jit(solution)/shard_map/ppermute | solution.py:305
  83.1 0.0 all-gather.6.cloned.1.call-done
  83.2 2.0 %collective-permute-start.4 = (bf16[72,1152]{1,0:T(8,128)(2,1)S(1)}, bf16[72,1152]{1,0:T(8,128)(2,1)S(1)}, u32[]{:S(2)}, u32[]{:S(2)}) collective-permute-start(bf16[72,1152]{1,0:T(8,128)(2,1)S(1)} %get-tuple-element.21.w0), channel_id=1, source_target_pairs={{0,6},{2,4},{4,2},{6,0},{1,7},{3,5},{5,3},{7,1},{8,14},{10,12},{12... | collective-permute-start | bytes 497672 | tf_op jit(solution)/shard_map/ppermute | solution.py:305
  85.2 0.1 broadcast_in_dim.9
  85.3 0.2 broadcast_in_dim_reshape.8.rowp
  85.5 1.6 copy-done
  87.1 2.7 %qkv.3.q = bf16[3,896,72]{2,1,0:T(8,128)(2,1)S(1)} custom-call(bf16[4,224,1152]{2,1,0:T(8,128)(2,1)S(1)} %bitcast.32, bf16[216,1152]{1,0:T(8,128)(2,1)S(1)} %slice.58.w, f32[2,72]{1,0:T(2,128)S(1)} %get-tuple-element.38.gain), custom_call_target="tpu_custom_call" | custom-call | flops 445906944 | bytes 3000000 | tf_op jit(solution)/shard_map/qkv/pallas_call | solution.py:44
  89.8 5.0 %spatial.1 = bf16[4,4,56,72]{3,2,1,0:T(8,128)(2,1)S(1)} custom-call(bf16[3,896,72]{2,1,0:T(8,128)(2,1)S(1)} %qkv.3.q, bf16[32,64,128]{2,1,0:T(8,128)(2,1)S(1)} %bitcast.37, s32[896,1]{1,0:T(8,128)S(1)} %broadcast_in_dim_reshape.8.rowp, s32[1,1792]{1,0:T(1,128)S(1)} %broadcast_in_dim_reshape.7.colp), custom_call_target="tpu_custom_call" | custom-call | flops 600000000 | bytes 2000000 | tf_op jit(solution)/shard_map/spatial/pallas_call | solution.py:44
  94.8 1.0 collective-permute-done.4.w3
  95.8 8.9 %all_to_all.25 = bf16[4,4,56,72]{3,2,1,0:T(8,128)(2,1)S(1)} all-to-all(bf16[4,4,56,72]{3,2,1,0:T(8,128)(2,1)S(1)} %spatial.1), channel_id=1, replica_groups=mesh['z'=8,'c'=2,'x'=4,'y'=4,'h'=2] {'y'}, dimensions={0} | all-to-all | bytes 258048 | tf_op jit(solution)/shard_map/all_to_all | solution.py:345
  104.7 0.0 all-gather.8.cloned.1.call-update
  104.8 2.0 %heads_out.1 = bf16[4,56,1152]{2,1,0:T(8,128)(2,1)} custom-call(s32[4]{0:T(128)S(1)} %slice_xor_fusion.place, bf16[4,224,72]{2,1,0:T(8,128)(2,1)S(1)} %bitcast.36, bf16[72,1152]{1,0:T(8,128)(2,1)S(1)} %get-tuple-element.21.w0, bf16[72,1152]{1,0:T(8,128)(2,1)S(1)} %collective-permute-done.2.w1, bf16[72,1152]{1,0:T(8,128)(2,1)S(1)} %collective-permute-done.3.w2, ...), custom_call_target="tpu_custom_call" | custom-call | flops 150000000 | bytes 1200000 | tf_op jit(solution)/shard_map/heads_out/pallas_call | solution.py:44
  106.8 3.8 %all-to-all-start.3 = ((bf16[4,56,1152]{2,1,0:T(8,128)(2,1)}), bf16[4,56,1152]{2,1,0:T(8,128)(2,1)S(1)}, u32[]{:S(2)}, u32[]{:S(2)}) async-start(bf16[4,56,1152]{2,1,0:T(8,128)(2,1)} %heads_out.1), calls=%async_computation.3 | async-start | bytes 1032192 | tf_op jit(solution)/shard_map/all_to_all | solution.py:351
  110.6 0.6 slice_bitcast_fusion.2
  111.3 3.5 %collective-permute-start.5 = (bf16[216,1152]{1,0:T(8,128)(2,1)S(1)}, bf16[216,1152]{1,0:T(8,128)(2,1)S(1)}, u32[]{:S(2)}, u32[]{:S(2)}) collective-permute-start(bf16[216,1152]{1,0:T(8,128)(2,1)S(1)} %bitcast.33), channel_id=1, source_target_pairs={{0,32},{32,0},{1,33},{33,1},{2,34},{34,2},{3,35},{35,3},{4,36},{36... | collective-permute-start | bytes 1493000 | tf_op jit(solution)/shard_map/ppermute | solution.py:355
  114.8 3.5 %all-to-all-done.3.part = bf16[4,56,1152]{2,1,0:T(8,128)(2,1)S(1)} async-done(((bf16[4,56,1152]{2,1,0:T(8,128)(2,1)}), bf16[4,56,1152]{2,1,0:T(8,128)(2,1)S(1)}, u32[]{:S(2)}, u32[]{:S(2)}) %all-to-all-start.3) | async-done | bytes 516128 | tf_op jit(solution)/shard_map/all_to_all | solution.py:351
  118.2 0.3 combine.1
  118.5 0.0 copy-start.10
  118.5 26.6 %all-gather.1 = bf16[448,1152]{1,0:T(8,128)(2,1)S(1)} all-gather(bf16[56,1152]{1,0:T(8,128)(2,1)S(1)} %get-tuple-element.25), channel_id=3, replica_groups={{0,128,256,384,448,320,192,64},{1,129,257,385,449,321,193,65},{2,130,25..., dimensions={0}, use_global_device_ids=true | all-gather | bytes 1161216 | tf_op jit(solution)/shard_map/all_gather | solution.py:313
  145.1 1.9 qkv.5
  147.1 9.8 %collective-permute-start.6 = (bf16[3,448,72]{2,1,0:T(8,128)(2,1)S(1)}, bf16[3,448,72]{2,1,0:T(8,128)(2,1)S(1)}, u32[]{:S(2)}, u32[]{:S(2)}) collective-permute-start(bf16[3,448,72]{2,1,0:T(8,128)(2,1)S(1)} %qkv.5), channel_id=1, source_target_pairs={{0,32},{32,0},{1,33},{33,1},{2,34},{34,2},{3,35},{35,3},{4,36},{36... | collective-permute-start | bytes 580616 | tf_op jit(solution)/shard_map/ppermute | solution.py:357
  156.9 1.9 qkv.4
  158.8 3.7 %temporal.1 = bf16[16,32,128]{2,1,0:T(8,128)(2,1)} custom-call(s32[16]{0:T(128)S(1)} %fusion.1.place, bf16[3,8,56,72]{3,2,1,0:T(8,128)(2,1)S(1)} %bitcast.35, bf16[3,8,56,72]{3,2,1,0:T(8,128)(2,1)S(1)} %bitcast.40), custom_call_target="tpu_custom_call" | custom-call | flops 50000000 | bytes 1000000 | tf_op jit(solution)/shard_map/temporal/pallas_call | solution.py:44
  162.5 6.6 %all-to-all-start.4 = ((bf16[16,32,128]{2,1,0:T(8,128)(2,1)}), bf16[16,32,128]{2,1,0:T(8,128)(2,1)S(1)}, u32[]{:S(2)}, u32[]{:S(2)}) async-start(bf16[16,32,128]{2,1,0:T(8,128)(2,1)} %temporal.1), calls=%async_computation.4 | async-start | bytes 262144 | tf_op jit(solution)/shard_map/all_to_all | solution.py:362
  169.1 0.5 and_select_fusion.2.heads
  169.6 11.5 %all-to-all-done.4.attn = bf16[16,32,128]{2,1,0:T(8,128)(2,1)S(1)} async-done(((bf16[16,32,128]{2,1,0:T(8,128)(2,1)}), bf16[16,32,128]{2,1,0:T(8,128)(2,1)S(1)}, u32[]{:S(2)}, u32[]{:S(2)}) %all-to-all-start.4) | async-done | bytes 131104 | tf_op jit(solution)/shard_map/all_to_all | solution.py:362
  181.1 0.6 copy-done.7
  181.7 3.9 %project.1 = bf16[56,1152]{1,0:T(8,128)(2,1)} custom-call(s32[16]{0:T(128)} %and_select_fusion.2.heads, bf16[16,32,128]{2,1,0:T(8,128)(2,1)} %copy-done.7, bf16[1152,1152]{1,0:T(8,128)(2,1)} %all-gather.8.cloned.1.call-done.w, bf16[56,1152]{1,0:T(8,128)(2,1)} %copy-done.5, f32[1,1152]{1,0:T(1,128)} %get-tuple-element.35.gate), custom_call_target="tpu_custom_call" | custom-call | flops 150000000 | bytes 3200000 | tf_op jit(solution)/shard_map/project/pallas_call | solution.py:44
  (37 shorter events, 0.2 us)
Async XLA Ops:
  6.5 76.6 %all-gather.6.cloned.1.call-start = ((), (), s32[]{:S(2)}) async-start(), calls=%async_computation.5 | async-start | bytes 2193408 | tf_op jit(solution)/shard_map/all_gather | solution.py:323
  7.3 0.9 copy-start.1
  8.2 1.9 %copy-start.6 = (bf16[2,3,72,1152]{3,2,1,0:T(8,128)(2,1)S(1)}, bf16[2,3,72,1152]{3,2,1,0:T(8,128)(2,1)}, u32[]{:S(2)}) copy-start(bf16[2,3,72,1152]{3,2,1,0:T(8,128)(2,1)} %param.12) | copy-start | bytes 2985988
  10.2 1.1 copy-start.3
  10.2 1.1 copy-start.4
  10.3 25.1 %copy-start.9 = (f32[2,2,72]{2,1,0:T(2,128)S(1)}, f32[2,2,72]{2,1,0:T(2,128)}, u32[]{:S(2)}) copy-start(f32[2,2,72]{2,1,0:T(2,128)} %param.14) | copy-start | bytes 3460
  10.3 22.5 %collective-permute-start = (bf16[360,1152]{1,0:T(8,128)(2,1)S(1)}, bf16[360,1152]{1,0:T(8,128)(2,1)S(1)}, u32[]{:S(2)}, u32[]{:S(2)}) collective-permute-start(bf16[360,1152]{1,0:T(8,128)(2,1)S(1)} %pad_maximum_fusion), channel_id=1, source_target_pairs={{0,0},{320,64},{128,128},{449,192},{256,256},{65,320},{384,384},{1... | collective-permute-start | bytes 2488328 | tf_op jit(solution)/shard_map/ppermute | solution.py:329
  12.9 47.9 %all-to-all-start = ((bf16[32,64,128]{2,1,0:T(8,128)(2,1)}), bf16[32,64,128]{2,1,0:T(8,128)(2,1)}, u32[]{:S(2)}, u32[]{:S(2)}) async-start(bf16[32,64,128]{2,1,0:T(8,128)(2,1)} %bitcast.7), calls=%async_computation | async-start | bytes 1048576 | tf_op jit(solution)/shard_map/all_to_all | solution.py:326
  32.9 4.4 %collective-permute-start.1 = (bf16[360,1152]{1,0:T(8,128)(2,1)S(1)}, bf16[360,1152]{1,0:T(8,128)(2,1)}, u32[]{:S(2)}, u32[]{:S(2)}) collective-permute-start(bf16[360,1152]{1,0:T(8,128)(2,1)S(1)} %collective-permute-done), channel_id=1, source_target_pairs={{0,32},{32,0},{1,33},{33,1},{2,34},{34,2},{3,35},{35,3},{4,36},{36... | collective-permute-start | bytes 2488328 | tf_op jit(solution)/shard_map/ppermute | solution.py:330
  60.8 29.0 %all-to-all-start.1 = ((bf16[16,2,64,128]{3,2,1,0:T(8,128)(2,1)}), bf16[16,2,64,128]{3,2,1,0:T(8,128)(2,1)S(1)}, u32[]{:S(2)}, u32[]{:S(2)}) async-start(bf16[16,2,64,128]{3,2,1,0:T(8,128)(2,1)} %bitcast.8), calls=%async_computation.1 | async-start | bytes 1048576 | tf_op jit(solution)/shard_map/all_to_all | solution.py:334
  74.8 106.3 %all-gather.8.cloned.1.call-start = ((), (), s32[]{:S(2)}) async-start(), calls=%async_computation.6 | async-start | bytes 2820096 | tf_op jit(solution)/shard_map/all_gather | solution.py:349
  75.6 19.3 %collective-permute-start.2 = (bf16[72,1152]{1,0:T(8,128)(2,1)S(1)}, bf16[72,1152]{1,0:T(8,128)(2,1)S(1)}, u32[]{:S(2)}, u32[]{:S(2)}) collective-permute-start(bf16[72,1152]{1,0:T(8,128)(2,1)S(1)} %get-tuple-element.21.w0), channel_id=1, source_target_pairs={{0,2},{2,0},{4,6},{6,4},{1,3},{3,1},{5,7},{7,5},{8,10},{10,8},{12,... | collective-permute-start | bytes 497672 | tf_op jit(solution)/shard_map/ppermute | solution.py:305
  78.8 16.0 %collective-permute-start.3 = (bf16[72,1152]{1,0:T(8,128)(2,1)S(1)}, bf16[72,1152]{1,0:T(8,128)(2,1)S(1)}, u32[]{:S(2)}, u32[]{:S(2)}) collective-permute-start(bf16[72,1152]{1,0:T(8,128)(2,1)S(1)} %get-tuple-element.21.w0), channel_id=1, source_target_pairs={{0,4},{2,6},{4,0},{6,2},{1,5},{3,7},{5,1},{7,3},{8,12},{10,14},{12... | collective-permute-start | bytes 497672 | tf_op jit(solution)/shard_map/ppermute | solution.py:305
  83.2 12.7 %collective-permute-start.4 = (bf16[72,1152]{1,0:T(8,128)(2,1)S(1)}, bf16[72,1152]{1,0:T(8,128)(2,1)S(1)}, u32[]{:S(2)}, u32[]{:S(2)}) collective-permute-start(bf16[72,1152]{1,0:T(8,128)(2,1)S(1)} %get-tuple-element.21.w0), channel_id=1, source_target_pairs={{0,6},{2,4},{4,2},{6,0},{1,7},{3,5},{5,3},{7,1},{8,14},{10,12},{12... | collective-permute-start | bytes 497672 | tf_op jit(solution)/shard_map/ppermute | solution.py:305
  85.5 1.6 copy-start
  94.8 15.8 %copy-start.8 = (f32[2,3,1152]{2,0,1:T(2,128)S(1)}, f32[2,3,1152]{2,0,1:T(2,128)}, u32[]{:S(2)}) copy-start(f32[2,3,1152]{2,0,1:T(2,128)} %param.11) | copy-start | bytes 82948
  94.8 23.4 %copy-start.2 = (bf16[1,56,1152]{2,1,0:T(8,128)(2,1)S(1)}, bf16[1,56,1152]{2,1,0:T(8,128)(2,1)}, u32[]{:S(2)}) copy-start(bf16[1,56,1152]{2,1,0:T(8,128)(2,1)} %param.8) | copy-start | bytes 387076
  106.8 11.4 %all-to-all-start.3 = ((bf16[4,56,1152]{2,1,0:T(8,128)(2,1)}), bf16[4,56,1152]{2,1,0:T(8,128)(2,1)S(1)}, u32[]{:S(2)}, u32[]{:S(2)}) async-start(bf16[4,56,1152]{2,1,0:T(8,128)(2,1)} %heads_out.1), calls=%async_computation.3 | async-start | bytes 1032192 | tf_op jit(solution)/shard_map/all_to_all | solution.py:351
  111.3 33.9 %collective-permute-start.5 = (bf16[216,1152]{1,0:T(8,128)(2,1)S(1)}, bf16[216,1152]{1,0:T(8,128)(2,1)S(1)}, u32[]{:S(2)}, u32[]{:S(2)}) collective-permute-start(bf16[216,1152]{1,0:T(8,128)(2,1)S(1)} %bitcast.33), channel_id=1, source_target_pairs={{0,32},{32,0},{1,33},{33,1},{2,34},{34,2},{3,35},{35,3},{4,36},{36... | collective-permute-start | bytes 1493000 | tf_op jit(solution)/shard_map/ppermute | solution.py:355
  118.5 40.3 %copy-start.5 = (bf16[56,1152]{1,0:T(8,128)(2,1)}, bf16[56,1152]{1,0:T(8,128)(2,1)S(1)}, u32[]{:S(2)}) copy-start(bf16[56,1152]{1,0:T(8,128)(2,1)S(1)} %get-tuple-element.28.resid) | copy-start | bytes 387076
  118.5 38.3 %copy-start.10 = (s32[16]{0:T(128)S(1)}, s32[16]{0:T(128)}, u32[]{:S(2)}) copy-start(s32[16]{0:T(128)} %constant.91) | copy-start | bytes 196
  147.1 11.8 %collective-permute-start.6 = (bf16[3,448,72]{2,1,0:T(8,128)(2,1)S(1)}, bf16[3,448,72]{2,1,0:T(8,128)(2,1)S(1)}, u32[]{:S(2)}, u32[]{:S(2)}) collective-permute-start(bf16[3,448,72]{2,1,0:T(8,128)(2,1)S(1)} %qkv.5), channel_id=1, source_target_pairs={{0,32},{32,0},{1,33},{33,1},{2,34},{34,2},{3,35},{35,3},{4,36},{36... | collective-permute-start | bytes 580616 | tf_op jit(solution)/shard_map/ppermute | solution.py:357
  162.5 18.6 %all-to-all-start.4 = ((bf16[16,32,128]{2,1,0:T(8,128)(2,1)}), bf16[16,32,128]{2,1,0:T(8,128)(2,1)S(1)}, u32[]{:S(2)}, u32[]{:S(2)}) async-start(bf16[16,32,128]{2,1,0:T(8,128)(2,1)} %temporal.1), calls=%async_computation.4 | async-start | bytes 262144 | tf_op jit(solution)/shard_map/all_to_all | solution.py:362
  181.1 0.6 copy-start.7
Sparse Core Ops, SparseCore 0:
  10.4 64.6 all-gather.5
  104.9 59.0 all-gather.7

commit v7 on v6

--- a/solution.py
+++ b/solution.py
@@ -1,4 +1,4 @@
-import functools
+import math
 
 import jax
 import jax.numpy as jnp
@@ -102,9 +102,9 @@
     return call(qkv_kernel, (toks, w, gain), shape, "qkv", flops=flops, moved=3_000_000)
 
 
-def spatial_kernel(q, old, rowp, colp, out, vals_s, old_s, attn_s):
+def spatial_kernel(q, old, rowp, colp, out, vals_s, old_s, val_s, attn_s):
     step = pl.program_id(0)
-    factor = HEAD_DIM ** (-0.5)
+    factor = HEAD_DIM ** (-0.5) * math.log2(math.e)
 
     @pl.when(step == 0)
     def _():
@@ -113,10 +113,10 @@
         for j in range(7):
             vals_s[:, 8 * j : 8 * j + 8, 56:72] = raw[:, 56:, 16 * j : 16 * j + 16]
         old_s[...] = raw[:, :56, :HEAD_DIM].reshape(old_s.shape).astype(jnp.bfloat16)
+        val_s[...] = vals_s[...].reshape(old_s.shape).astype(jnp.bfloat16)
 
     at = pl.ds(pl.multiple_of(step * QBLOCK, QBLOCK), QBLOCK)
     query, key, value = q[0, at], q[1, at], q[2, at]
-    old_values = vals_s[...].reshape(old_s.shape).astype(jnp.bfloat16)
     far = dot(query, old_s[...], NT)
     far = jnp.where(rowp[at] == colp[...], NEG, far)
     near = dot(query, key, NT)
@@ -124,10 +124,10 @@
     c_id = lax.broadcasted_iota(jnp.int32, (QBLOCK, QBLOCK), 1) // ROWS
     near = jnp.where(r_id == c_id, near, NEG)
     top = jnp.maximum(jnp.max(far, axis=1, keepdims=True), jnp.max(near, axis=1, keepdims=True))
-    e_far = jnp.exp((far - top) * factor)
-    e_near = jnp.exp((near - top) * factor)
+    e_far = jnp.exp2((far - top) * factor)
+    e_near = jnp.exp2((near - top) * factor)
     total = jnp.sum(e_far, axis=1, keepdims=True) + jnp.sum(e_near, axis=1, keepdims=True)
-    mixed = dot(e_far.astype(jnp.bfloat16), old_values) + dot(e_near.astype(jnp.bfloat16), value)
+    mixed = dot(e_far.astype(jnp.bfloat16), val_s[...]) + dot(e_near.astype(jnp.bfloat16), value)
     attn_s[...] = mixed / total
     for j in range(4):
         out[j, step] = attn_s[j * ROWS : (j + 1) * ROWS].astype(jnp.bfloat16)
@@ -144,6 +144,7 @@
     )
     scratch = (
         pltpu.VMEM((2 * PLANE, ROWS, HEAD_DIM), jnp.float32),
+        pltpu.VMEM((2 * PLANE * ROWS, HEAD_DIM), jnp.bfloat16),
         pltpu.VMEM((2 * PLANE * ROWS, HEAD_DIM), jnp.bfloat16),
         pltpu.VMEM((QBLOCK, HEAD_DIM), jnp.float32),
     )

time: 193 us -> 194 us (level)
  no operation moved by 1% of the time
where the time goes in v7:
time: 194 us; the launch traced here: 193 us
  starting transfers between devices  70.8 us (36%)
  waiting for transfers between devices  40.6 us (21%)
  blocking collectives  35.1 us (18%)
  Pallas kernels  23.7 us (12%)
  between operations  13.8 us (7%)
  local copies, waits for them, and re-layouts  6.81 us (4%)
  other arithmetic  1.97 us (1%)
    all_gather x1, blocking collectives, line_gather(): return lax.all_gather(block, 'z', axis=0, axis_index_groups=[list(LOOP)])  26.4 us
    pallas_call x10, Pallas kernels, call(): pl.pallas_call(kernel, out_shape=out_shape, scratch_shapes=list(scratch),...  23.7 us
    all_to_all x1, waiting for transfers between devices, local(): old = lax.all_to_all(chunk, ('z', 'c', 'h'), 0, 0, tiled=True)  22.2 us
    all_to_all x1, starting transfers between devices, local(): old = lax.all_to_all(chunk, ('z', 'c', 'h'), 0, 0, tiled=True)  19.9 us
    all_to_all x1, starting transfers between devices, local(): lax.all_to_all(old.reshape(16, 2, 64, 128), AXES, 0, 0, axis_index_groups...  14 us
    all_to_all x1, waiting for transfers between devices, local(): attn = lax.all_to_all(attn, ('z', 'c'), 0, 0, tiled=True)  11.5 us
    ppermute x1, starting transfers between devices, local(): other = lax.ppermute(sib, 'c', SWAP)  10 us
    ppermute x3, starting transfers between devices, xor_gather(): lax.ppermute(blocks[k], axis, [(i, i ^ k) for i in range(4)])  9.57 us
  transfers between devices with their start and end apart: 13, of which 5 were waited for; matrix products, arithmetic and copies ran while one was open for 3% of the time, Pallas kernels for 10%

profile of v7, /device:TPU:1, one launch (start us, length us, event | category | flops | bytes accessed | tf_op | source)
XLA Modules:
  0.0 192.7 jit_solution(5986039758965897385)
XLA Ops:
  6.5 0.8 slice.44
  7.3 0.9 copy-done.1
  8.2 0.9 modulate.1
  9.1 0.0 all-gather.6.cloned.1.call-update
  9.1 1.0 slice_bitcast_fusion.1
  10.2 0.1 fusion.4
  10.3 0.1 pad_maximum_fusion
  10.3 0.8 collective-permute-start
  11.2 1.7 pack.1
  12.9 19.9 %all-to-all-start = ((bf16[32,64,128]{2,1,0:T(8,128)(2,1)}), bf16[32,64,128]{2,1,0:T(8,128)(2,1)}, u32[]{:S(2)}, u32[]{:S(2)}) async-start(bf16[32,64,128]{2,1,0:T(8,128)(2,1)} %bitcast.7), calls=%async_computation | async-start | bytes 1048576 | tf_op jit(solution)/shard_map/all_to_all | solution.py:327
  32.9 2.2 %collective-permute-start.1 = (bf16[360,1152]{1,0:T(8,128)(2,1)S(1)}, bf16[360,1152]{1,0:T(8,128)(2,1)}, u32[]{:S(2)}, u32[]{:S(2)}) collective-permute-start(bf16[360,1152]{1,0:T(8,128)(2,1)S(1)} %collective-permute-done), channel_id=1, source_target_pairs={{0,32},{32,0},{1,33},{33,1},{2,34},{34,2},{3,35},{35,3},{4,36},{36... | collective-permute-start | bytes 2488328 | tf_op jit(solution)/shard_map/ppermute | solution.py:331
  35.1 0.1 broadcast_in_dim.10
  35.2 0.1 broadcast_in_dim_reshape.7.colp
  35.3 1.9 collective-permute-done.1
  37.3 1.3 broadcast_select_fusion
  38.6 22.2 %all-to-all-done = bf16[32,64,128]{2,1,0:T(8,128)(2,1)} async-done(((bf16[32,64,128]{2,1,0:T(8,128)(2,1)}), bf16[32,64,128]{2,1,0:T(8,128)(2,1)}, u32[]{:S(2)}, u32[]{:S(2)}) %all-to-all-start) | async-done | bytes 524320 | tf_op jit(solution)/shard_map/all_to_all | solution.py:327
  60.8 14.0 %all-to-all-start.1 = ((bf16[16,2,64,128]{3,2,1,0:T(8,128)(2,1)}), bf16[16,2,64,128]{3,2,1,0:T(8,128)(2,1)S(1)}, u32[]{:S(2)}, u32[]{:S(2)}) async-start(bf16[16,2,64,128]{3,2,1,0:T(8,128)(2,1)} %bitcast.8), calls=%async_computation.1 | async-start | bytes 1048576 | tf_op jit(solution)/shard_map/all_to_all | solution.py:335
  74.8 0.0 all-gather.8.cloned.1.call-start
  74.9 0.7 fusion.5
  75.6 3.3 %collective-permute-start.2 = (bf16[72,1152]{1,0:T(8,128)(2,1)S(1)}, bf16[72,1152]{1,0:T(8,128)(2,1)S(1)}, u32[]{:S(2)}, u32[]{:S(2)}) collective-permute-start(bf16[72,1152]{1,0:T(8,128)(2,1)S(1)} %get-tuple-element.21.w0), channel_id=1, source_target_pairs={{0,2},{2,0},{4,6},{6,4},{1,3},{3,1},{5,7},{7,5},{8,10},{10,8},{12,... | collective-permute-start | bytes 497672 | tf_op jit(solution)/shard_map/ppermute | solution.py:306
  78.8 4.3 %collective-permute-start.3 = (bf16[72,1152]{1,0:T(8,128)(2,1)S(1)}, bf16[72,1152]{1,0:T(8,128)(2,1)S(1)}, u32[]{:S(2)}, u32[]{:S(2)}) collective-permute-start(bf16[72,1152]{1,0:T(8,128)(2,1)S(1)} %get-tuple-element.21.w0), channel_id=1, source_target_pairs={{0,4},{2,6},{4,0},{6,2},{1,5},{3,7},{5,1},{7,3},{8,12},{10,14},{12... | collective-permute-start | bytes 497672 | tf_op jit(solution)/shard_map/ppermute | solution.py:306
  83.1 0.0 all-gather.6.cloned.1.call-done
  83.2 2.0 %collective-permute-start.4 = (bf16[72,1152]{1,0:T(8,128)(2,1)S(1)}, bf16[72,1152]{1,0:T(8,128)(2,1)S(1)}, u32[]{:S(2)}, u32[]{:S(2)}) collective-permute-start(bf16[72,1152]{1,0:T(8,128)(2,1)S(1)} %get-tuple-element.21.w0), channel_id=1, source_target_pairs={{0,6},{2,4},{4,2},{6,0},{1,7},{3,5},{5,3},{7,1},{8,14},{10,12},{12... | collective-permute-start | bytes 497672 | tf_op jit(solution)/shard_map/ppermute | solution.py:306
  85.2 0.1 broadcast_in_dim.9
  85.3 0.2 broadcast_in_dim_reshape.8.rowp
  85.5 1.6 copy-done
  87.1 2.7 %qkv.3.q = bf16[3,896,72]{2,1,0:T(8,128)(2,1)S(1)} custom-call(bf16[4,224,1152]{2,1,0:T(8,128)(2,1)S(1)} %bitcast.32, bf16[216,1152]{1,0:T(8,128)(2,1)S(1)} %slice.58.w, f32[2,72]{1,0:T(2,128)S(1)} %get-tuple-element.38.gain), custom_call_target="tpu_custom_call" | custom-call | flops 445906944 | bytes 3000000 | tf_op jit(solution)/shard_map/qkv/pallas_call | solution.py:44
  89.8 4.8 %spatial.1 = bf16[4,4,56,72]{3,2,1,0:T(8,128)(2,1)S(1)} custom-call(bf16[3,896,72]{2,1,0:T(8,128)(2,1)S(1)} %qkv.3.q, bf16[32,64,128]{2,1,0:T(8,128)(2,1)S(1)} %bitcast.37, s32[896,1]{1,0:T(8,128)S(1)} %broadcast_in_dim_reshape.8.rowp, s32[1,1792]{1,0:T(1,128)S(1)} %broadcast_in_dim_reshape.7.colp), custom_call_target="tpu_custom_call" | custom-call | flops 600000000 | bytes 2000000 | tf_op jit(solution)/shard_map/spatial/pallas_call | solution.py:44
  94.6 1.2 collective-permute-done.4.w3
  95.8 8.6 %all_to_all.25 = bf16[4,4,56,72]{3,2,1,0:T(8,128)(2,1)S(1)} all-to-all(bf16[4,4,56,72]{3,2,1,0:T(8,128)(2,1)S(1)} %spatial.1), channel_id=1, replica_groups=mesh['z'=8,'c'=2,'x'=4,'y'=4,'h'=2] {'y'}, dimensions={0} | all-to-all | bytes 258048 | tf_op jit(solution)/shard_map/all_to_all | solution.py:346
  104.5 0.0 all-gather.8.cloned.1.call-update
  104.5 2.0 %heads_out.1 = bf16[4,56,1152]{2,1,0:T(8,128)(2,1)} custom-call(s32[4]{0:T(128)S(1)} %slice_xor_fusion.place, bf16[4,224,72]{2,1,0:T(8,128)(2,1)S(1)} %bitcast.36, bf16[72,1152]{1,0:T(8,128)(2,1)S(1)} %get-tuple-element.21.w0, bf16[72,1152]{1,0:T(8,128)(2,1)S(1)} %collective-permute-done.2.w1, bf16[72,1152]{1,0:T(8,128)(2,1)S(1)} %collective-permute-done.3.w2, ...), custom_call_target="tpu_custom_call" | custom-call | flops 150000000 | bytes 1200000 | tf_op jit(solution)/shard_map/heads_out/pallas_call | solution.py:44
  106.6 4.0 %all-to-all-start.3 = ((bf16[4,56,1152]{2,1,0:T(8,128)(2,1)}), bf16[4,56,1152]{2,1,0:T(8,128)(2,1)S(1)}, u32[]{:S(2)}, u32[]{:S(2)}) async-start(bf16[4,56,1152]{2,1,0:T(8,128)(2,1)} %heads_out.1), calls=%async_computation.3 | async-start | bytes 1032192 | tf_op jit(solution)/shard_map/all_to_all | solution.py:352
  110.5 0.6 slice_bitcast_fusion.2
  111.2 3.4 %collective-permute-start.5 = (bf16[216,1152]{1,0:T(8,128)(2,1)S(1)}, bf16[216,1152]{1,0:T(8,128)(2,1)S(1)}, u32[]{:S(2)}, u32[]{:S(2)}) collective-permute-start(bf16[216,1152]{1,0:T(8,128)(2,1)S(1)} %bitcast.33), channel_id=1, source_target_pairs={{0,32},{32,0},{1,33},{33,1},{2,34},{34,2},{3,35},{35,3},{4,36},{36... | collective-permute-start | bytes 1493000 | tf_op jit(solution)/shard_map/ppermute | solution.py:356
  114.5 3.6 %all-to-all-done.3.part = bf16[4,56,1152]{2,1,0:T(8,128)(2,1)S(1)} async-done(((bf16[4,56,1152]{2,1,0:T(8,128)(2,1)}), bf16[4,56,1152]{2,1,0:T(8,128)(2,1)S(1)}, u32[]{:S(2)}, u32[]{:S(2)}) %all-to-all-start.3) | async-done | bytes 516128 | tf_op jit(solution)/shard_map/all_to_all | solution.py:352
  118.2 0.3 combine.1
  118.5 0.0 copy-start.10
  118.5 26.4 %all-gather.1 = bf16[448,1152]{1,0:T(8,128)(2,1)S(1)} all-gather(bf16[56,1152]{1,0:T(8,128)(2,1)S(1)} %get-tuple-element.25), channel_id=3, replica_groups={{0,128,256,384,448,320,192,64},{1,129,257,385,449,321,193,65},{2,130,25..., dimensions={0}, use_global_device_ids=true | all-gather | bytes 1161216 | tf_op jit(solution)/shard_map/all_gather | solution.py:314
  144.9 1.9 qkv.5
  146.9 10.0 %collective-permute-start.6 = (bf16[3,448,72]{2,1,0:T(8,128)(2,1)S(1)}, bf16[3,448,72]{2,1,0:T(8,128)(2,1)S(1)}, u32[]{:S(2)}, u32[]{:S(2)}) collective-permute-start(bf16[3,448,72]{2,1,0:T(8,128)(2,1)S(1)} %qkv.5), channel_id=1, source_target_pairs={{0,32},{32,0},{1,33},{33,1},{2,34},{34,2},{3,35},{35,3},{4,36},{36... | collective-permute-start | bytes 580616 | tf_op jit(solution)/shard_map/ppermute | solution.py:358
  156.9 1.9 qkv.4
  158.8 3.7 %temporal.1 = bf16[16,32,128]{2,1,0:T(8,128)(2,1)} custom-call(s32[16]{0:T(128)S(1)} %fusion.1.place, bf16[3,8,56,72]{3,2,1,0:T(8,128)(2,1)S(1)} %bitcast.35, bf16[3,8,56,72]{3,2,1,0:T(8,128)(2,1)S(1)} %bitcast.40), custom_call_target="tpu_custom_call" | custom-call | flops 50000000 | bytes 1000000 | tf_op jit(solution)/shard_map/temporal/pallas_call | solution.py:44
  162.5 6.8 %all-to-all-start.4 = ((bf16[16,32,128]{2,1,0:T(8,128)(2,1)}), bf16[16,32,128]{2,1,0:T(8,128)(2,1)S(1)}, u32[]{:S(2)}, u32[]{:S(2)}) async-start(bf16[16,32,128]{2,1,0:T(8,128)(2,1)} %temporal.1), calls=%async_computation.4 | async-start | bytes 262144 | tf_op jit(solution)/shard_map/all_to_all | solution.py:363
  169.3 0.5 and_select_fusion.2.heads
  169.8 11.5 %all-to-all-done.4.attn = bf16[16,32,128]{2,1,0:T(8,128)(2,1)S(1)} async-done(((bf16[16,32,128]{2,1,0:T(8,128)(2,1)}), bf16[16,32,128]{2,1,0:T(8,128)(2,1)S(1)}, u32[]{:S(2)}, u32[]{:S(2)}) %all-to-all-start.4) | async-done | bytes 131104 | tf_op jit(solution)/shard_map/all_to_all | solution.py:363
  181.3 0.6 copy-done.7
  182.0 3.9 %project.1 = bf16[56,1152]{1,0:T(8,128)(2,1)} custom-call(s32[16]{0:T(128)} %and_select_fusion.2.heads, bf16[16,32,128]{2,1,0:T(8,128)(2,1)} %copy-done.7, bf16[1152,1152]{1,0:T(8,128)(2,1)} %all-gather.8.cloned.1.call-done.w, bf16[56,1152]{1,0:T(8,128)(2,1)} %copy-done.5, f32[1,1152]{1,0:T(1,128)} %get-tuple-element.35.gate), custom_call_target="tpu_custom_call" | custom-call | flops 150000000 | bytes 3200000 | tf_op jit(solution)/shard_map/project/pallas_call | solution.py:44
  (37 shorter events, 0.2 us)
Async XLA Ops:
  6.5 76.6 %all-gather.6.cloned.1.call-start = ((), (), s32[]{:S(2)}) async-start(), calls=%async_computation.5 | async-start | bytes 2193408 | tf_op jit(solution)/shard_map/all_gather | solution.py:324
  7.3 0.9 copy-start.1
  8.2 1.9 %copy-start.6 = (bf16[2,3,72,1152]{3,2,1,0:T(8,128)(2,1)S(1)}, bf16[2,3,72,1152]{3,2,1,0:T(8,128)(2,1)}, u32[]{:S(2)}) copy-start(bf16[2,3,72,1152]{3,2,1,0:T(8,128)(2,1)} %param.12) | copy-start | bytes 2985988
  10.2 1.1 copy-start.3
  10.2 1.1 copy-start.4
  10.3 25.1 %copy-start.9 = (f32[2,2,72]{2,1,0:T(2,128)S(1)}, f32[2,2,72]{2,1,0:T(2,128)}, u32[]{:S(2)}) copy-start(f32[2,2,72]{2,1,0:T(2,128)} %param.14) | copy-start | bytes 3460
  10.3 22.5 %collective-permute-start = (bf16[360,1152]{1,0:T(8,128)(2,1)S(1)}, bf16[360,1152]{1,0:T(8,128)(2,1)S(1)}, u32[]{:S(2)}, u32[]{:S(2)}) collective-permute-start(bf16[360,1152]{1,0:T(8,128)(2,1)S(1)} %pad_maximum_fusion), channel_id=1, source_target_pairs={{0,0},{320,64},{128,128},{449,192},{256,256},{65,320},{384,384},{1... | collective-permute-start | bytes 2488328 | tf_op jit(solution)/shard_map/ppermute | solution.py:330
  12.9 47.9 %all-to-all-start = ((bf16[32,64,128]{2,1,0:T(8,128)(2,1)}), bf16[32,64,128]{2,1,0:T(8,128)(2,1)}, u32[]{:S(2)}, u32[]{:S(2)}) async-start(bf16[32,64,128]{2,1,0:T(8,128)(2,1)} %bitcast.7), calls=%async_computation | async-start | bytes 1048576 | tf_op jit(solution)/shard_map/all_to_all | solution.py:327
  32.9 4.4 %collective-permute-start.1 = (bf16[360,1152]{1,0:T(8,128)(2,1)S(1)}, bf16[360,1152]{1,0:T(8,128)(2,1)}, u32[]{:S(2)}, u32[]{:S(2)}) collective-permute-start(bf16[360,1152]{1,0:T(8,128)(2,1)S(1)} %collective-permute-done), channel_id=1, source_target_pairs={{0,32},{32,0},{1,33},{33,1},{2,34},{34,2},{3,35},{35,3},{4,36},{36... | collective-permute-start | bytes 2488328 | tf_op jit(solution)/shard_map/ppermute | solution.py:331
  60.8 29.0 %all-to-all-start.1 = ((bf16[16,2,64,128]{3,2,1,0:T(8,128)(2,1)}), bf16[16,2,64,128]{3,2,1,0:T(8,128)(2,1)S(1)}, u32[]{:S(2)}, u32[]{:S(2)}) async-start(bf16[16,2,64,128]{3,2,1,0:T(8,128)(2,1)} %bitcast.8), calls=%async_computation.1 | async-start | bytes 1048576 | tf_op jit(solution)/shard_map/all_to_all | solution.py:335
  74.8 106.5 %all-gather.8.cloned.1.call-start = ((), (), s32[]{:S(2)}) async-start(), calls=%async_computation.6 | async-start | bytes 2820096 | tf_op jit(solution)/shard_map/all_gather | solution.py:350
  75.6 19.0 %collective-permute-start.2 = (bf16[72,1152]{1,0:T(8,128)(2,1)S(1)}, bf16[72,1152]{1,0:T(8,128)(2,1)S(1)}, u32[]{:S(2)}, u32[]{:S(2)}) collective-permute-start(bf16[72,1152]{1,0:T(8,128)(2,1)S(1)} %get-tuple-element.21.w0), channel_id=1, source_target_pairs={{0,2},{2,0},{4,6},{6,4},{1,3},{3,1},{5,7},{7,5},{8,10},{10,8},{12,... | collective-permute-start | bytes 497672 | tf_op jit(solution)/shard_map/ppermute | solution.py:306
  78.8 15.8 %collective-permute-start.3 = (bf16[72,1152]{1,0:T(8,128)(2,1)S(1)}, bf16[72,1152]{1,0:T(8,128)(2,1)S(1)}, u32[]{:S(2)}, u32[]{:S(2)}) collective-permute-start(bf16[72,1152]{1,0:T(8,128)(2,1)S(1)} %get-tuple-element.21.w0), channel_id=1, source_target_pairs={{0,4},{2,6},{4,0},{6,2},{1,5},{3,7},{5,1},{7,3},{8,12},{10,14},{12... | collective-permute-start | bytes 497672 | tf_op jit(solution)/shard_map/ppermute | solution.py:306
  83.2 12.7 %collective-permute-start.4 = (bf16[72,1152]{1,0:T(8,128)(2,1)S(1)}, bf16[72,1152]{1,0:T(8,128)(2,1)S(1)}, u32[]{:S(2)}, u32[]{:S(2)}) collective-permute-start(bf16[72,1152]{1,0:T(8,128)(2,1)S(1)} %get-tuple-element.21.w0), channel_id=1, source_target_pairs={{0,6},{2,4},{4,2},{6,0},{1,7},{3,5},{5,3},{7,1},{8,14},{10,12},{12... | collective-permute-start | bytes 497672 | tf_op jit(solution)/shard_map/ppermute | solution.py:306
  85.5 1.6 copy-start
  94.6 16.0 %copy-start.8 = (f32[2,3,1152]{2,0,1:T(2,128)S(1)}, f32[2,3,1152]{2,0,1:T(2,128)}, u32[]{:S(2)}) copy-start(f32[2,3,1152]{2,0,1:T(2,128)} %param.11) | copy-start | bytes 82948
  94.6 23.6 %copy-start.2 = (bf16[1,56,1152]{2,1,0:T(8,128)(2,1)S(1)}, bf16[1,56,1152]{2,1,0:T(8,128)(2,1)}, u32[]{:S(2)}) copy-start(bf16[1,56,1152]{2,1,0:T(8,128)(2,1)} %param.8) | copy-start | bytes 387076
  106.6 11.6 %all-to-all-start.3 = ((bf16[4,56,1152]{2,1,0:T(8,128)(2,1)}), bf16[4,56,1152]{2,1,0:T(8,128)(2,1)S(1)}, u32[]{:S(2)}, u32[]{:S(2)}) async-start(bf16[4,56,1152]{2,1,0:T(8,128)(2,1)} %heads_out.1), calls=%async_computation.3 | async-start | bytes 1032192 | tf_op jit(solution)/shard_map/all_to_all | solution.py:352
  111.2 33.8 %collective-permute-start.5 = (bf16[216,1152]{1,0:T(8,128)(2,1)S(1)}, bf16[216,1152]{1,0:T(8,128)(2,1)S(1)}, u32[]{:S(2)}, u32[]{:S(2)}) collective-permute-start(bf16[216,1152]{1,0:T(8,128)(2,1)S(1)} %bitcast.33), channel_id=1, source_target_pairs={{0,32},{32,0},{1,33},{33,1},{2,34},{34,2},{3,35},{35,3},{4,36},{36... | collective-permute-start | bytes 1493000 | tf_op jit(solution)/shard_map/ppermute | solution.py:356
  118.5 40.4 %copy-start.5 = (bf16[56,1152]{1,0:T(8,128)(2,1)}, bf16[56,1152]{1,0:T(8,128)(2,1)S(1)}, u32[]{:S(2)}) copy-start(bf16[56,1152]{1,0:T(8,128)(2,1)S(1)} %get-tuple-element.28.resid) | copy-start | bytes 387076
  118.5 38.4 %copy-start.10 = (s32[16]{0:T(128)S(1)}, s32[16]{0:T(128)}, u32[]{:S(2)}) copy-start(s32[16]{0:T(128)} %constant.91) | copy-start | bytes 196
  146.9 12.0 %collective-permute-start.6 = (bf16[3,448,72]{2,1,0:T(8,128)(2,1)S(1)}, bf16[3,448,72]{2,1,0:T(8,128)(2,1)S(1)}, u32[]{:S(2)}, u32[]{:S(2)}) collective-permute-start(bf16[3,448,72]{2,1,0:T(8,128)(2,1)S(1)} %qkv.5), channel_id=1, source_target_pairs={{0,32},{32,0},{1,33},{33,1},{2,34},{34,2},{3,35},{35,3},{4,36},{36... | collective-permute-start | bytes 580616 | tf_op jit(solution)/shard_map/ppermute | solution.py:358
  162.5 18.8 %all-to-all-start.4 = ((bf16[16,32,128]{2,1,0:T(8,128)(2,1)}), bf16[16,32,128]{2,1,0:T(8,128)(2,1)S(1)}, u32[]{:S(2)}, u32[]{:S(2)}) async-start(bf16[16,32,128]{2,1,0:T(8,128)(2,1)} %temporal.1), calls=%async_computation.4 | async-start | bytes 262144 | tf_op jit(solution)/shard_map/all_to_all | solution.py:363
  181.3 0.6 copy-start.7
Sparse Core Ops, SparseCore 0:
  10.4 64.6 all-gather.5
  104.6 59.0 all-gather.7
